TPU v7x, 128 devices: a whole 4x4x4 slice. The times are simulated.
128 devices in a mesh: lat: 16 (over z, x), chan: 8 (over y, core).
Axes of the slice: x: 4, y: 4, z: 4, core: 2. Of those that a mesh axis runs over, the one named last changes fastest.
Arguments:
- probe_field: bfloat16 [2, 384, 384, 1024], P(None, 'lat', 'chan'), may hold values from -6 to 6
- gate_slope: bfloat16 [384, 768, 1024], P('lat', None, 'chan'), may hold values from -0.099609375 to 1.09375
- spectral_filter: float32 [384, 384], P(None, 'chan'), may hold values from -4 to 4
- weight_in: bfloat16 [384, 768], replicated, may hold values from -0.3125 to 0.3125
- weight_out: bfloat16 [768, 384], replicated, may hold values from -0.21875 to 0.21875
- weight_flux: bfloat16 [384, 4], replicated, may hold values from -0.3125 to 0.3125
- send_cells: int32 [128, 16, 128], P(('lat', 'chan')), may hold values from 0 to 3071
- recv_slots: int32 [128, 4, 2048], P(('lat', 'chan')), may hold values from 0 to 2047
- recv_weights: float32 [128, 4, 2048], P(('lat', 'chan')), may hold values from 0.1 to 0.5
- ocean_probe: bfloat16 [2, 200, 128, 2048], P(None, None, 'lat', 'chan'), may hold values from -6 to 6
- ocean_mask: int32 [128, 2048], P('lat', 'chan'), may hold values 0 or 1
- coupling: bfloat16 [4, 200], replicated, may hold values from -3 to 3
- base_fine: bfloat16 [200, 128, 2048], P(None, 'lat', 'chan'), may hold values from -5 to 5
- sigma_fine: float32 [128, 2048], P('lat', 'chan'), may hold values from 0.5 to 2
- slope_fine: bfloat16 [800, 128, 2048], P(None, 'lat', 'chan'), may hold values from -0.099609375 to 1.09375
- gain_fine: float32 [200], replicated, may hold values from 0.1 to 1.9
- kernel_fine: float32 [200, 49], replicated, may hold values from -0.875 to 0.875
- expand_fine: bfloat16 [200, 800], replicated, may hold values from -0.4375 to 0.4375
- shrink_fine: bfloat16 [800, 200], replicated, may hold values from -0.21875 to 0.21875
- down_proj: bfloat16 [200, 250], replicated, may hold values from -0.4375 to 0.4375
- base_coarse: bfloat16 [250, 64, 1024], P(None, 'lat', 'chan'), may hold values from -5 to 5
- sigma_coarse: float32 [64, 1024], P('lat', 'chan'), may hold values from 0.5 to 2
- slope_coarse: bfloat16 [1000, 64, 1024], P(None, 'lat', 'chan'), may hold values from -0.099609375 to 1.09375
- gain_coarse: float32 [250], replicated, may hold values from 0.1 to 1.9
- kernel_coarse: float32 [250, 49], replicated, may hold values from -0.875 to 0.875
- expand_coarse: bfloat16 [250, 1000], replicated, may hold values from -0.375 to 0.375
- shrink_coarse: bfloat16 [1000, 250], replicated, may hold values from -0.1875 to 0.1875
- up_proj: bfloat16 [250, 200], replicated, may hold values from -0.375 to 0.375
Outputs:
- atmos_out: bfloat16 [2, 384, 384, 1024], P(None, 'lat', 'chan')
- ocean_out: bfloat16 [2, 200, 128, 2048], P(None, None, 'lat', 'chan')
Inputs may be any that keep to these rules, and one draw needn't show every extreme that they name: `send_cells`: local cell numbers of a flux tile of 24 by 128 cells. `recv_slots`: slot numbers into the 16 times 128 received cells.
All inputs are finite; a program needn't handle non-finite values. No bound on the sum of `ocean_mask` on one device may be relied on, other than what follows from the above.
Results may differ from a plain program's by a relative error of at most 0.023.
Values may be sent and summed in bfloat16 or wider, within the bound.
A program may use at most 192 MiB of HBM per device.

v0:
```python
import math

import jax
import jax.numpy as jnp
from jax import lax
from jax.sharding import PartitionSpec as P


def with_halo(block, sides, width):
    for axis, dim in sides:
        count = lax.axis_size(axis)
        forward = [(i, i + 1) for i in range(count - 1)]
        backward = [(target, source) for source, target in forward]
        low = lax.ppermute(
            lax.slice_in_dim(block, block.shape[dim] - width, None, axis=dim), axis, forward
        )
        high = lax.ppermute(lax.slice_in_dim(block, 0, width, axis=dim), axis, backward)
        block = jnp.concatenate([low, block, high], axis=dim)
    return block


def fourier_tables(count):
    column = jnp.arange(count, dtype=jnp.int32)
    half = count // 2
    wave = jnp.where(column <= half, column, column - half)
    points = jnp.arange(count, dtype=jnp.int32)
    phase = points[:, None] * wave[None, :] % count
    angles = phase.astype(jnp.float32) * (2.0 * math.pi / count)
    basis = jnp.where((column <= half)[None, :], jnp.cos(angles), jnp.sin(angles))
    forward = (basis / count).astype(jnp.bfloat16)
    factor = jnp.where((column == 0) | (column == half), 1.0, 2.0).astype(jnp.float32)
    inverse = (basis.T * factor[:, None]).astype(jnp.bfloat16)
    return (forward, inverse)


def cosine_tables(count):
    degree = jnp.arange(count, dtype=jnp.int32)
    points = jnp.arange(count, dtype=jnp.int32)
    phase = degree[None, :] * (2 * points[:, None] + 1) % (4 * count)
    basis = jnp.cos(phase.astype(jnp.float32) * (math.pi / (2 * count)))
    forward = (basis / count).astype(jnp.bfloat16)
    factor = jnp.where(degree == 0, 1.0, 2.0).astype(jnp.float32)
    inverse = (basis.T * factor[:, None]).astype(jnp.bfloat16)
    return (forward, inverse)


def depthwise(padded, kernel, rows, cols):
    total = jnp.zeros((padded.shape[0], padded.shape[1], rows, cols), jnp.float32)
    wide = padded.astype(jnp.float32)
    for offset in range(49):
        row_start = offset // 7
        col_start = offset % 7
        total = (
            total
            + wide[:, :, row_start : row_start + rows, col_start : col_start + cols]
            * kernel[:, offset][None, :, None, None]
        )
    return total


def level_tangent(field, padded, base, sigma, slope, gain, kernel, expand, shrink, mask_values):
    spread = depthwise(padded, kernel, field.shape[2], field.shape[3])
    center = jnp.mean(spread, axis=1, keepdims=True)
    normed = base.astype(jnp.float32)[None]
    along = jnp.mean(normed * spread, axis=1, keepdims=True)
    tangent = (
        gain[None, :, None, None] * sigma[None, None] * (spread - center - normed * along)
    ).astype(jnp.bfloat16)
    hidden = jnp.einsum("pqyx,qh->phyx", tangent, expand, preferred_element_type=jnp.float32)
    gated = (slope[None] * hidden).astype(jnp.bfloat16)
    output = jnp.einsum("phyx,hq->pqyx", gated, shrink, preferred_element_type=jnp.float32)
    return ((field.astype(jnp.float32) + output) * mask_values).astype(jnp.bfloat16)


def to_columns(mixed):
    return lax.all_to_all(mixed, "chan", split_axis=3, concat_axis=2, tiled=True)


def local(
    probe_field,
    gate_slope,
    spectral_filter,
    weight_in,
    weight_out,
    weight_flux,
    send_cells,
    recv_slots,
    recv_weights,
    ocean_probe,
    ocean_mask,
    coupling,
    base_fine,
    sigma_fine,
    slope_fine,
    gain_fine,
    kernel_fine,
    expand_fine,
    shrink_fine,
    down_proj,
    base_coarse,
    sigma_coarse,
    slope_coarse,
    gain_coarse,
    kernel_coarse,
    expand_coarse,
    shrink_coarse,
    up_proj,
):
    probe_count = probe_field.shape[0]
    band_rows = probe_field.shape[1]
    width_local = probe_field.shape[2]
    lon_count = probe_field.shape[3]
    lat_devices = lax.axis_size("lat")
    lat_count = band_rows * lat_devices
    mode_block = lon_count // lat_devices
    fwd_lon, inv_lon = fourier_tables(lon_count)
    fwd_lat, inv_lat = cosine_tables(lat_count)
    flux_rows = lax.dynamic_slice_in_dim(
        weight_flux, lax.axis_index("chan") * width_local, width_local, 0
    )
    fwd_blocks = fwd_lon.reshape(lon_count, lat_devices, mode_block)
    inv_blocks = inv_lon.reshape(lat_devices, mode_block, lon_count)
    fourier = jnp.einsum(
        "pncx,xam->pnacm", probe_field, fwd_blocks, preferred_element_type=jnp.float32
    )
    fourier = fourier.astype(jnp.bfloat16).reshape(
        probe_count, band_rows, lat_devices, width_local * mode_block
    )
    filter_wide = jnp.repeat(spectral_filter, mode_block, axis=1)
    gathered = lax.all_to_all(fourier, "lat", split_axis=2, concat_axis=1, tiled=True)
    spectrum = jnp.einsum("pnaj,nl->plaj", gathered, fwd_lat, preferred_element_type=jnp.float32)
    filtered = (spectrum * filter_wide[None, :, None, :]).astype(jnp.bfloat16)
    returned = lax.all_to_all(
        jnp.einsum("plaj,ln->pnaj", filtered, inv_lat, preferred_element_type=jnp.float32).astype(
            jnp.bfloat16
        ),
        "lat",
        split_axis=1,
        concat_axis=2,
        tiled=True,
    )
    returned = returned.reshape(probe_count, band_rows, lat_devices, width_local, mode_block)
    spatial = jnp.einsum(
        "pnacm,amx->pncx", returned, inv_blocks, preferred_element_type=jnp.float32
    )
    mixed = (probe_field.astype(jnp.float32) + spatial).astype(jnp.bfloat16)
    regrouped = to_columns(mixed)
    hidden = jnp.einsum("pncx,ch->pnhx", regrouped, weight_in, preferred_element_type=jnp.float32)
    gated = (gate_slope[None] * hidden).astype(jnp.bfloat16)
    update = jnp.einsum(
        "pnhx,hc->pncx", gated, weight_out, preferred_element_type=jnp.float32
    ).astype(jnp.bfloat16)
    update_back = lax.all_to_all(update, "chan", split_axis=2, concat_axis=3, tiled=True)
    result_field = probe_field.astype(jnp.float32) + update_back.astype(jnp.float32)
    atmos_out = result_field.astype(jnp.bfloat16)
    partial_flux = jnp.einsum(
        "pncx,cf->pfnx",
        result_field,
        flux_rows.astype(jnp.float32),
        precision=lax.Precision.HIGHEST,
    )
    flux_field = lax.psum_scatter(
        partial_flux.astype(jnp.bfloat16), "chan", scatter_dimension=3, tiled=True
    )
    flux_count = flux_field.shape[1]
    flat_tile = flux_field.reshape(probe_count, flux_count, -1)
    picked = jnp.take(flat_tile, send_cells.reshape(-1), axis=2)
    picked = picked.reshape(probe_count, flux_count, send_cells.shape[1], send_cells.shape[2])
    arrived = lax.all_to_all(picked, "lat", split_axis=2, concat_axis=2, tiled=True)
    pool_slots = arrived.reshape(probe_count, flux_count, -1)
    tile_rows = ocean_probe.shape[2]
    tile_cols = ocean_probe.shape[3]
    source_count = recv_slots.shape[1]
    taken = jnp.take(pool_slots, recv_slots.reshape(-1), axis=2)
    taken = taken.reshape(probe_count, flux_count, source_count, tile_rows * tile_cols)
    ocean_flux = jnp.sum(taken.astype(jnp.float32) * recv_weights[0][None, None], axis=2)
    ocean_flux = ocean_flux.reshape(probe_count, flux_count, tile_rows, tile_cols)
    mask_values = ocean_mask.astype(jnp.float32)
    forcing = jnp.einsum(
        "pfyx,fq->pqyx", ocean_flux, coupling.astype(jnp.float32), precision=lax.Precision.HIGHEST
    )
    start_field = ((ocean_probe.astype(jnp.float32) + forcing) * mask_values).astype(jnp.bfloat16)
    fine_padded = with_halo(start_field, (("lat", 2), ("chan", 3)), 3)
    level_one = level_tangent(
        start_field,
        fine_padded,
        base_fine,
        sigma_fine,
        slope_fine,
        gain_fine,
        kernel_fine,
        expand_fine,
        shrink_fine,
        mask_values,
    )
    fine_channels = level_one.shape[1]
    shaped = level_one.astype(jnp.float32).reshape(
        probe_count, fine_channels, tile_rows // 2, 2, tile_cols // 2, 2
    )
    pooled = jnp.mean(shaped, axis=(3, 5))
    coarse_field = jnp.einsum(
        "pqyx,qr->pryx", pooled, down_proj.astype(jnp.float32), precision=lax.Precision.HIGHEST
    ).astype(jnp.bfloat16)
    coarse_padded = with_halo(coarse_field, (("lat", 2), ("chan", 3)), 3)
    level_two = level_tangent(
        coarse_field,
        coarse_padded,
        base_coarse,
        sigma_coarse,
        slope_coarse,
        gain_coarse,
        kernel_coarse,
        expand_coarse,
        shrink_coarse,
        1.0,
    )
    raised = jnp.einsum("pryx,rq->pqyx", level_two, up_proj, preferred_element_type=jnp.float32)
    upsampled = jnp.repeat(jnp.repeat(raised, 2, axis=2), 2, axis=3)
    ocean_out = ((level_one.astype(jnp.float32) + upsampled) * mask_values).astype(jnp.bfloat16)
    return (atmos_out, ocean_out)


def solution(mesh):
    return jax.shard_map(
        local,
        mesh=mesh,
        in_specs=(
            P(None, "lat", "chan", None),
            P("lat", None, "chan"),
            P(None, "chan"),
            P(),
            P(),
            P(),
            P(("lat", "chan"), None, None),
            P(("lat", "chan"), None, None),
            P(("lat", "chan"), None, None),
            P(None, None, "lat", "chan"),
            P("lat", "chan"),
            P(),
            P(None, "lat", "chan"),
            P("lat", "chan"),
            P(None, "lat", "chan"),
            P(),
            P(),
            P(),
            P(),
            P(),
            P(None, "lat", "chan"),
            P("lat", "chan"),
            P(None, "lat", "chan"),
            P(),
            P(),
            P(),
            P(),
            P(),
        ),
        out_specs=(P(None, "lat", "chan", None), P(None, None, "lat", "chan")),
        check_vma=False,
    )
```

profile of v0, /device:TPU:32, one launch (start us, length us, event | category | flops | bytes accessed | tf_op | source)
XLA Modules:
  0.0 879.7 jit_solution(18021187998859307307)
XLA Ops:
  7.2 27.5 %convert_bitcast_fusion.1 = bf16[2,24,16,48,64]{4,3,1,0,2:T(8,128)(2,1)} fusion(bf16[2,24,48,1024]{3,2,1,0:T(8,128)(2,1)} %param.28, s32[16,64]{1,0:T(8,128)S(1)} %add_select_fusion.4, pred[16,64]{1,0:T(8,128)(4,1)S(1)} %fusion.236), kind=kOutput, calls=%fused_computation.15 | convolution fusion | flops 4852023296 | bytes 9442304 | tf_op jit(solution)/shard_map/pncx,xam->pnacm/dot_general | solution.py:123
  34.7 12.5 %reshape.408 = bf16[2,24,16,3072]{3,1,0,2:T(8,128)(2,1)} reshape(bf16[2,24,16,48,64]{4,3,1,0,2:T(8,128)(2,1)} %convert_bitcast_fusion.1) | data formatting | bytes 9437184 | tf_op jit(solution)/shard_map/reshape | solution.py:126
  64.3 60.3 %all-to-all-done = bf16[2,24,16,3072]{3,1,0,2:T(8,128)(2,1)} async-done(((bf16[2,24,16,3072]{3,1,0,2:T(8,128)(2,1)}), bf16[2,24,16,3072]{3,1,0,2:T(8,128)(2,1)}, u32[]{:S(2)}, u32[]{:S(2)}) %all-to-all-start) | async-done | bytes 4718624 | tf_op jit(solution)/shard_map/all_to_all | solution.py:130
  129.5 15.4 %fusion.20 = bf16[2,384,1,3072]{3,1,0,2:T(8,128)(2,1)} fusion(bf16[2,384,3072]{2,1,0:T(8,128)(2,1)} %bitcast.351, f32[384,3072]{1,0:T(8,128)} %copy.143, s32[384]{0:T(512)S(1)} %multiply_add_fusion.1, f32[384]{0:T(512)S(1)} %fusion.240), kind=kOutput, calls=%fused_computation.36 | convolution fusion | flops 3634200576 | bytes 14158848 | tf_op jit(solution)/shard_map/plaj,ln->pnaj/dot_general | solution.py:134
  144.9 9.5 %copy.144 = bf16[2,384,1,3072]{3,0,2,1:T(2,128)(2,1)} copy(bf16[2,384,1,3072]{3,1,0,2:T(8,128)(2,1)} %fusion.20) | data formatting | bytes 9437184 | tf_op jit(solution)/shard_map/convert_element_type | solution.py:134
  160.9 18.5 %fusion.284 = bf16[16,64,1024,1,1]{2,1,3,4,0:T(8,128)(2,1)S(1)} fusion(f32[16,64]{1,0:T(8,128)S(1)} %fusion.238, s32[16,64]{1,0:T(8,128)S(1)} %add_select_fusion.4, pred[16,64]{1,0:T(8,128)(4,1)S(1)} %fusion.236), kind=kLoop, calls=%fused_computation.162.clone.clone.1 | loop fusion | flops 17825792 | bytes 2106368 | tf_op jit(solution)/shard_map/pnacm,amx->pncx/dot_general | solution.py:143
  179.4 48.3 %all-to-all-done.1 = bf16[2,384,1,3072]{3,0,2,1:T(2,128)(2,1)} async-done(((bf16[2,384,1,3072]{3,0,2,1:T(2,128)(2,1)}), bf16[2,384,1,3072]{3,0,2,1:T(2,128)(2,1)}, u32[]{:S(2)}, u32[]{:S(2)}) %all-to-all-start.1) | async-done | bytes 4718624 | tf_op jit(solution)/shard_map/all_to_all | solution.py:133
  233.6 12.3 %reshape.411 = bf16[2,24,16,48,64]{4,3,1,0,2:T(8,128)(2,1)} reshape(bf16[2,24,16,1,3072]{4,1,0,2,3:T(8,128)(2,1)} %bitcast.343) | data formatting | bytes 9437184 | tf_op jit(solution)/shard_map/reshape | solution.py:142
  245.9 11.4 %fusion.6 = f32[2,24,48,1024,1]{3,2,0,1,4:T(8,128)} fusion(bf16[2,24,16,48,64]{4,3,1,0,2:T(8,128)(2,1)} %reshape.411, bf16[16,64,1024,1,1]{2,1,3,4,0:T(8,128)(2,1)S(1)} %fusion.284), kind=kOutput, calls=%fused_computation.13 | convolution fusion | flops 4831838208 | bytes 16252928 | tf_op jit(solution)/shard_map/pnacm,amx->pncx/dot_general | solution.py:143
  265.0 15.2 %copy.146 = bf16[2,24,48,1024]{2,1,0,3:T(8,128)(2,1)} copy(bf16[2,24,48,1024]{3,2,1,0:T(8,128)(2,1)} %fusion.2) | data formatting | bytes 9437184 | tf_op jit(solution)/shard_map/convert_element_type | solution.py:146
  280.2 20.3 %reshape.458 = bf16[8,2,147456]{2,1,0:T(2,128)(2,1)} reshape(bf16[1024,2,24,48]{3,2,1,0:T(8,128)(2,1)} %bitcast.337) | data formatting | bytes 9437184
  312.8 47.8 %all-to-all-done.2 = bf16[8,2,147456]{2,1,0:T(2,128)(2,1)} async-done(((bf16[8,2,147456]{2,1,0:T(2,128)(2,1)}), bf16[8,2,147456]{2,1,0:T(2,128)(2,1)}, u32[]{:S(2)}, u32[]{:S(2)}) %all-to-all-start.2) | async-done | bytes 4718624 | tf_op jit(solution)/shard_map/all_to_all | solution.py:76
  360.6 14.2 %reshape.459 = bf16[1024,2,24,48]{3,2,1,0:T(8,128)(2,1)} reshape(bf16[8,2,147456]{2,1,0:T(2,128)(2,1)} %all-to-all-done.2) | data formatting | bytes 9437184
  374.8 13.8 %copy.148 = bf16[2,24,8,48,128]{4,3,2,1,0:T(8,128)(2,1)} copy(bf16[2,24,8,48,128]{3,1,0,4,2:T(8,128)(2,1)} %bitcast.338) | data formatting | bytes 9437184 | tf_op jit(solution)/shard_map/all_to_all | solution.py:76
  388.6 14.8 %convert_bitcast_fusion.2 = bf16[2,24,384,128]{2,3,1,0:T(8,128)(2,1)} fusion(f32[24,768,128]{1,2,0:T(8,128)} %copy.141, bf16[2,24,384,128]{3,2,1,0:T(8,128)(2,1)} %bitcast.344, bf16[768,384]{1,0:T(8,128)(2,1)S(1)} %copy-done, bf16[384,768]{1,0:T(8,128)(2,1)S(1)} %copy-done.4), kind=kOutput, calls=%fused_computation.34 | convolution fusion | flops 7259553792 | bytes 20054016 | tf_op jit(solution)/shard_map/pnhx,hc->pncx/dot_general | solution.py:150
  416.3 54.0 %all-to-all-done.3 = bf16[2,24,384,128]{3,1,0,2:T(8,128)(2,1)} async-done(((bf16[2,24,384,128]{3,1,0,2:T(8,128)(2,1)}), bf16[2,24,384,128]{3,1,0,2:T(8,128)(2,1)}, u32[]{:S(2)}, u32[]{:S(2)}) %all-to-all-start.3) | async-done | bytes 4718624 | tf_op jit(solution)/shard_map/all_to_all | solution.py:153
  482.4 13.1 %copy.192 = bf16[2,4,24,1024]{1,2,0,3:T(8,128)(2,1)} copy(bf16[2,4,24,1024]{3,1,2,0:T(4,128)(2,1)S(1)} %fusion.131) | data formatting | bytes 786432
  495.5 15.0 %reshape.456 = bf16[1024,192]{1,0:T(8,128)(2,1)} reshape(bf16[1024,2,24,4]{3,2,1,0:T(8,128)(2,1)} %bitcast.336) | data formatting | bytes 786432
  510.6 28.8 %reduce-scatter.4.cloned.1.call-done = bf16[128,192]{1,0:T(8,128)(2,1)} async-done(((bf16[1024,192]{1,0:T(8,128)(2,1)}), bf16[128,192]{1,0:T(8,128)(2,1)}) %reduce-scatter.4.cloned.1.call-update) | async-done | bytes 49168
  568.1 54.0 %gather_fusion.1 = bf16[8192,2,4]{2,1,0:T(2,128)(2,1)} fusion(bf16[2,4,2048]{1,0,2:T(2,128)(2,1)S(1)} %bitcast.353, s32[8192]{0:T(1024)S(1)} %broadcast_clamp_fusion), kind=kCustom, calls=%fused_computation.1 | custom fusion | bytes 294912 | tf_op jit(solution)/shard_map/jit(_take)/gather | solution.py:174
  622.1 23.6 %multiply_reduce_fusion = f32[2,4,2048]{1,0,2:T(2,128)} fusion(bf16[2,4,4,2048]{1,0,3,2:T(2,128)(2,1)} %bitcast.352, pred[4,2048]{1,0:T(4,128)(4,1)S(1)} %compare_and_fusion, f32[4,2048]{1,0:T(4,128)S(1)} %bitcast.359), kind=kLoop, calls=%fused_computation.17 | loop fusion | flops 245760 | bytes 237568 | tf_op jit(solution)/shard_map/reduce_sum | solution.py:176
  698.7 89.3 %fusion.262 = (f32[2,8,256]{2,1,0:T(8,128)S(1)}, f32[2,8,256]{2,1,0:T(8,128)S(1)}, f32[2,200,8,256]{3,1,2,0:T(8,128)}) fusion(f32[200,8,256]{2,0,1:T(8,128)S(1)} %copy-done.3, f32[200]{0:T(256)} %bitcast.458, f32[2,200,14,262]{3,1,2,0:T(8,128)} %maximum_convert_fusion, f32[200]{0:T(256)} %bitcast.459, f32[200]{0:T(256)S(1)} %bitcast.412, ...), kind=kLoop, calls=%fused_computation.382 | loop fusion | flops 81911808 | bytes 165550368 | tf_op jit(solution)/shard_map/reduce_sum | solution.py:63
  788.0 10.4 %fusion.114 = f32[2,200,8,256]{3,1,2,0:T(8,128)} fusion(f32[800,8,256]{2,0,1:T(8,128)} %copy.158, bf16[2,200,8,256]{3,1,2,0:T(8,128)(2,1)S(1)} %fusion.87, f32[2,200,8,256]{3,1,2,0:T(8,128)} %get-tuple-element.19, f32[2,8,256]{2,1,0:T(8,128)S(1)} %get-tuple-element.126, f32[200,8,256]{2,0,1:T(8,128)} %copy.163, f32[2,8,256]{2,1,0:T(8,128)S(1)} %get-tuple-element.127, ...), kind=kOutput, calls=%fused_computation.179 | convolution fusion | flops 2636185600 | bytes 18703360 | tf_op jit(solution)/shard_map/phyx,hq->pqyx/dot_general | solution.py:71
  842.1 10.1 %fusion.263 = (f32[2,4,128]{2,1,0:T(4,128)S(1)}, f32[2,4,128]{2,1,0:T(4,128)S(1)}, f32[2,250,4,128]{1,3,2,0:T(8,128)}) fusion(f32[250,4,128]{0,2,1:T(8,128)} %copy.167, f32[250]{0:T(256)} %bitcast.409, f32[2,250,10,134]{1,3,2,0:T(8,128)S(1)} %maximum_convert_fusion.1, f32[250]{0:T(256)} %bitcast.410, f32[250]{0:T(256)S(1)} %bitcast.363, ...), kind=kLoop, calls=%fused_computation.383 | loop fusion | flops 25597952 | bytes 51769192 | tf_op jit(solution)/shard_map/reduce_sum | solution.py:63
  (244 shorter events, 223.9 us)
Async XLA Ops:
  7.2 381.5 %copy-start = (bf16[768,384]{1,0:T(8,128)(2,1)S(1)}, bf16[768,384]{1,0:T(8,128)(2,1)}, u32[]{:S(2)}) copy-start(bf16[768,384]{1,0:T(8,128)(2,1)} %param.32) | copy-start | bytes 1769476
  47.2 77.4 %all-to-all-start = ((bf16[2,24,16,3072]{3,1,0,2:T(8,128)(2,1)}), bf16[2,24,16,3072]{3,1,0,2:T(8,128)(2,1)}, u32[]{:S(2)}, u32[]{:S(2)}) async-start(bf16[2,24,16,3072]{3,1,0,2:T(8,128)(2,1)} %reshape.408), calls=%async_computation | async-start | bytes 9437184 | tf_op jit(solution)/shard_map/all_to_all | solution.py:130
  154.4 73.3 %all-to-all-start.1 = ((bf16[2,384,1,3072]{3,0,2,1:T(2,128)(2,1)}), bf16[2,384,1,3072]{3,0,2,1:T(2,128)(2,1)}, u32[]{:S(2)}, u32[]{:S(2)}) async-start(bf16[2,384,1,3072]{3,0,2,1:T(2,128)(2,1)} %copy.144), calls=%async_computation.1 | async-start | bytes 9437184 | tf_op jit(solution)/shard_map/all_to_all | solution.py:133
  233.6 23.7 %slice-start = ((s8[4718592]{0:T(1024)(128)(4,1)}), s8[524288]{0:T(1024)(128)(4,1)S(1)}, s32[]{:S(2)}) async-start(s8[4718592]{0:T(1024)(128)(4,1)} %bitcast.341), calls=%async_computation.7 | async-start | bytes 1048576
  300.5 60.1 %all-to-all-start.2 = ((bf16[8,2,147456]{2,1,0:T(2,128)(2,1)}), bf16[8,2,147456]{2,1,0:T(2,128)(2,1)}, u32[]{:S(2)}, u32[]{:S(2)}) async-start(bf16[8,2,147456]{2,1,0:T(2,128)(2,1)} %reshape.458), calls=%async_computation.2 | async-start | bytes 9437184 | tf_op jit(solution)/shard_map/all_to_all | solution.py:76
  374.8 13.9 %copy-start.4 = (bf16[384,768]{1,0:T(8,128)(2,1)S(1)}, bf16[384,768]{1,0:T(8,128)(2,1)}, u32[]{:S(2)}) copy-start(bf16[384,768]{1,0:T(8,128)(2,1)} %param.31) | copy-start | bytes 1769476
  410.3 60.1 %all-to-all-start.3 = ((bf16[2,24,384,128]{3,1,0,2:T(8,128)(2,1)}), bf16[2,24,384,128]{3,1,0,2:T(8,128)(2,1)}, u32[]{:S(2)}, u32[]{:S(2)}) async-start(bf16[2,24,384,128]{3,1,0,2:T(8,128)(2,1)} %copy.150), calls=%async_computation.3 | async-start | bytes 9437184 | tf_op jit(solution)/shard_map/all_to_all | solution.py:153
  415.1 124.4 %reduce-scatter.4.cloned.1.call-start = ((), (), s32[]{:S(2)}) async-start(), calls=%async_computation.6 | async-start | bytes 589824
  510.5 51.2 %copy-start.17 = (s32[8,256]{1,0:T(8,128)S(1)}, s32[8,256]{1,0:T(8,128)}, u32[]{:S(2)}) copy-start(s32[8,256]{1,0:T(8,128)} %param.38) | copy-start | bytes 24580
  542.1 80.0 %copy-start.14 = (f32[1,4,2048]{2,1,0:T(4,128)S(1)}, f32[1,4,2048]{2,1,0:T(4,128)}, u32[]{:S(2)}) copy-start(f32[1,4,2048]{2,1,0:T(4,128)} %param.36) | copy-start | bytes 98308
  553.5 13.7 %all-to-all-start.4 = ((bf16[2,4,16,128]{3,1,0,2:T(4,128)(2,1)}), bf16[2,4,16,128]{3,1,0,2:T(4,128)(2,1)S(1)}, u32[]{:S(2)}, u32[]{:S(2)}) async-start(bf16[2,4,16,128]{3,1,0,2:T(4,128)(2,1)} %broadcast_select_fusion.1), calls=%async_computation.4 | async-start | bytes 65536 | tf_op jit(solution)/shard_map/all_to_all | solution.py:169
  568.1 77.6 %copy-start.69 = (bf16[4,200]{1,0:T(4,128)(2,1)S(1)}, bf16[4,200]{1,0:T(4,128)(2,1)}, u32[]{:S(2)}) copy-start(bf16[4,200]{1,0:T(4,128)(2,1)} %param.39) | copy-start | bytes 4804
  645.7 13.3 %copy-start.16 = (f32[8,256]{1,0:T(8,128)S(1)}, f32[8,256]{1,0:T(8,128)}, u32[]{:S(2)}) copy-start(f32[8,256]{1,0:T(8,128)} %param.41) | copy-start | bytes 24580
  645.7 13.3 %copy-start.72 = (f32[200]{0:T(256)S(1)}, f32[200]{0:T(256)}, u32[]{:S(2)}) copy-start(f32[200]{0:T(256)} %param.43) | copy-start | bytes 2404
  649.7 15.5 %collective-permute-start = (bf16[2,200,3,256]{3,1,2,0:T(8,128)(2,1)S(1)}, bf16[2,200,3,256]{3,1,2,0:T(8,128)(2,1)S(1)}, u32[]{:S(2)}, u32[]{:S(2)}) collective-permute-start(bf16[2,200,3,256]{3,1,2,0:T(8,128)(2,1)S(1)} %get-tuple-element.22), channel_id=1, source_target_pairs={{0,8},{8,16},{16,24},{24,32},{32,40},{40,48},{48,56},{56,64},{64,7... | collective-permute-start | bytes 1843208 | tf_op jit(solution)/shard_map/ppermute | solution.py:14
  652.2 14.2 %collective-permute-start.1 = (bf16[2,200,3,256]{3,1,2,0:T(8,128)(2,1)S(1)}, bf16[2,200,3,256]{3,1,2,0:T(8,128)(2,1)S(1)}, u32[]{:S(2)}, u32[]{:S(2)}) collective-permute-start(bf16[2,200,3,256]{3,1,2,0:T(8,128)(2,1)S(1)} %get-tuple-element.23), channel_id=1, source_target_pairs={{8,0},{16,8},{24,16},{32,24},{40,32},{48,40},{56,48},{64,56},{72,6... | collective-permute-start | bytes 1843208 | tf_op jit(solution)/shard_map/ppermute | solution.py:17
  670.8 16.5 %collective-permute-start.2 = (bf16[2,200,14,3]{1,0,3,2:T(2,128)(2,1)S(1)}, bf16[2,200,14,3]{1,0,3,2:T(2,128)(2,1)S(1)}, u32[]{:S(2)}, u32[]{:S(2)}) collective-permute-start(bf16[2,200,14,3]{1,0,3,2:T(2,128)(2,1)S(1)} %copy.159), channel_id=1, source_target_pairs={{0,1},{1,2},{2,3},{3,4},{4,5},{5,6},{6,7},{8,9},{9,10},{10,11},{11... | collective-permute-start | bytes 100808 | tf_op jit(solution)/shard_map/ppermute | solution.py:14
  674.0 15.2 %collective-permute-start.3 = (bf16[2,200,14,3]{1,0,3,2:T(2,128)(2,1)S(1)}, bf16[2,200,14,3]{1,0,3,2:T(2,128)(2,1)S(1)}, u32[]{:S(2)}, u32[]{:S(2)}) collective-permute-start(bf16[2,200,14,3]{1,0,3,2:T(2,128)(2,1)S(1)} %copy.160), channel_id=1, source_target_pairs={{1,0},{2,1},{3,2},{4,3},{5,4},{6,5},{7,6},{9,8},{10,9},{11,10},{12... | collective-permute-start | bytes 100808 | tf_op jit(solution)/shard_map/ppermute | solution.py:17
  698.7 89.3 %copy-start.5 = (bf16[200,800]{1,0:T(8,128)(2,1)S(1)}, bf16[200,800]{1,0:T(8,128)(2,1)}, u32[]{:S(2)}) copy-start(bf16[200,800]{1,0:T(8,128)(2,1)} %param.45) | copy-start | bytes 960004
  698.7 89.3 %copy-start.6 = (bf16[800,200]{0,1:T(8,128)(2,1)S(1)}, bf16[800,200]{0,1:T(8,128)(2,1)}, u32[]{:S(2)}) copy-start(bf16[800,200]{0,1:T(8,128)(2,1)} %param.46) | copy-start | bytes 960004
  812.2 15.9 %collective-permute-start.4 = (bf16[2,250,3,128]{1,3,2,0:T(8,128)(2,1)S(1)}, bf16[2,250,3,128]{1,3,2,0:T(8,128)(2,1)S(1)}, u32[]{:S(2)}, u32[]{:S(2)}) collective-permute-start(bf16[2,250,3,128]{1,3,2,0:T(8,128)(2,1)S(1)} %get-tuple-element.26), channel_id=1, source_target_pairs={{0,8},{8,16},{16,24},{24,32},{32,40},{40,48},{48,56},{56,64},{64,7... | collective-permute-start | bytes 1152008 | tf_op jit(solution)/shard_map/ppermute | solution.py:14
  814.2 15.7 %collective-permute-start.5 = (bf16[2,250,3,128]{1,3,2,0:T(8,128)(2,1)S(1)}, bf16[2,250,3,128]{1,3,2,0:T(8,128)(2,1)S(1)}, u32[]{:S(2)}, u32[]{:S(2)}) collective-permute-start(bf16[2,250,3,128]{1,3,2,0:T(8,128)(2,1)S(1)} %get-tuple-element.27), channel_id=1, source_target_pairs={{8,0},{16,8},{24,16},{32,24},{40,32},{48,40},{56,48},{64,56},{72,6... | collective-permute-start | bytes 1152008 | tf_op jit(solution)/shard_map/ppermute | solution.py:17
  829.9 11.6 %collective-permute-start.6 = (bf16[2,250,10,3]{1,3,2,0:T(4,128)(2,1)S(1)}, bf16[2,250,10,3]{1,3,2,0:T(4,128)(2,1)S(1)}, u32[]{:S(2)}, u32[]{:S(2)}) collective-permute-start(bf16[2,250,10,3]{1,3,2,0:T(4,128)(2,1)S(1)} %get-tuple-element.24), channel_id=1, source_target_pairs={{0,1},{1,2},{2,3},{3,4},{4,5},{5,6},{6,7},{8,9},{9,10},{10,11},{11... | collective-permute-start | bytes 90008 | tf_op jit(solution)/shard_map/ppermute | solution.py:14
  832.2 9.2 %collective-permute-start.7 = (bf16[2,250,10,3]{1,3,2,0:T(4,128)(2,1)S(1)}, bf16[2,250,10,3]{1,3,2,0:T(4,128)(2,1)S(1)}, u32[]{:S(2)}, u32[]{:S(2)}) collective-permute-start(bf16[2,250,10,3]{1,3,2,0:T(4,128)(2,1)S(1)} %get-tuple-element.25), channel_id=1, source_target_pairs={{1,0},{2,1},{3,2},{4,3},{5,4},{6,5},{7,6},{9,8},{10,9},{11,10},{12... | collective-permute-start | bytes 90008 | tf_op jit(solution)/shard_map/ppermute | solution.py:17
  (65 other events, 387.9 us)
Sparse Core Ops, SparseCore 0:
  510.6 28.7 reduce-scatter.3
where the time goes:
time: 895 us; the launch traced here: 880 us
  local copies, waits for them, and re-layouts  279 us (31%)
  waiting for transfers between devices  258 us (29%)
  other arithmetic  176 us (20%)
  matrix products  94.9 us (11%)
  starting transfers between devices  54.7 us (6%)
  between operations  15.8 us (2%)
    reduce_sum x2, other arithmetic, level_tangent(): center = jnp.mean(spread, axis=1, keepdims=True)  99.4 us
    unnamed x158, local copies, waits for them, and re-layouts  70.3 us
    all_to_all x1, waiting for transfers between devices, local(): lax.all_to_all(fourier, 'lat', split_axis=2, concat_axis=1, tiled=True)  60.3 us
    gather x1, local copies, waits for them, and re-layouts, local(): taken = jnp.take(pool_slots, recv_slots.reshape(-1), axis=2)  54 us
    all_to_all x1, waiting for transfers between devices, local(): lax.all_to_all(update, 'chan', split_axis=2, concat_axis=3, tiled=True)  54 us
    all_to_all x1, waiting for transfers between devices, local(): lax.all_to_all(jnp.einsum('plaj,ln->pnaj', filtered, inv_lat, preferred_e...  48.3 us
    all_to_all x1, waiting for transfers between devices, to_columns(): lax.all_to_all(mixed, 'chan', split_axis=3, concat_axis=2, tiled=True)  47.8 us
    unnamed x2, waiting for transfers between devices  28.8 us
  transfers between devices with their start and end apart: 14, of which 10 were waited for; matrix products, arithmetic and copies ran while one was open for 7% of the time, Pallas kernels for 0%

commit v1 on v0

v1 whole, which is shorter than its diff:
```python
import functools
import math

import jax
import jax.numpy as jnp
from jax import lax
from jax.experimental import pallas as pl
from jax.experimental.pallas import tpu as pltpu
from jax.sharding import PartitionSpec as P

F32 = jnp.float32
BF16 = jnp.bfloat16
VMEM_LIMIT = 56 * 1024 * 1024


def params(**more):
    return pltpu.CompilerParams(vmem_limit_bytes=VMEM_LIMIT, **more)


def cost(flops, nbytes):
    return pl.CostEstimate(flops=int(flops), bytes_accessed=int(nbytes), transcendentals=0)


def mm(a, b):
    return jnp.dot(a, b, preferred_element_type=F32)


def whole(shape):
    zeros = (0,) * len(shape)
    return pl.BlockSpec(shape, lambda *_: zeros)


def fourier_tables(count):
    column = jnp.arange(count, dtype=jnp.int32)
    half = count // 2
    wave = jnp.where(column <= half, column, column - half)
    points = jnp.arange(count, dtype=jnp.int32)
    phase = points[:, None] * wave[None, :] % count
    angles = phase.astype(F32) * (2.0 * math.pi / count)
    basis = jnp.where((column <= half)[None, :], jnp.cos(angles), jnp.sin(angles))
    forward = (basis / count).astype(BF16)
    factor = jnp.where((column == 0) | (column == half), 1.0, 2.0).astype(F32)
    inverse = (basis.T * factor[:, None]).astype(BF16)
    return (forward, inverse)


def cosine_tables(count):
    degree = jnp.arange(count, dtype=jnp.int32)
    points = jnp.arange(count, dtype=jnp.int32)
    phase = degree[None, :] * (2 * points[:, None] + 1) % (4 * count)
    basis = jnp.cos(phase.astype(F32) * (math.pi / (2 * count)))
    forward = (basis / count).astype(BF16)
    factor = jnp.where(degree == 0, 1.0, 2.0).astype(F32)
    inverse = (basis.T * factor[:, None]).astype(BF16)
    return (forward, inverse)


def turn_kernel(in_ref, out_ref, wide):
    rows, chans, lanes = in_ref.shape
    wide[...] = in_ref[...].astype(F32).reshape(rows * chans, lanes)
    for c in range(chans):
        out_ref[c] = wide[pl.ds(c, rows, stride=chans), :].astype(BF16)


def turn_channels(field):
    rows, chans, lons = field.shape
    return pl.pallas_call(
        turn_kernel,
        grid=(lons // 128,),
        in_specs=[pl.BlockSpec((rows, chans, 128), lambda i: (0, 0, i))],
        out_specs=pl.BlockSpec((chans, rows, 128), lambda i: (0, 0, i)),
        out_shape=jax.ShapeDtypeStruct((chans, rows, lons), BF16),
        scratch_shapes=[pltpu.VMEM((rows * chans, 128), F32)],
        compiler_params=params(),
        cost_estimate=cost(0, 4 * field.size),
        name="turn_channels",
    )(field)


def probe_flux_kernel(probe_ref, weight_ref, out_ref):
    weight = weight_ref[...]
    rows = probe_ref.shape[1]
    for n in range(0, rows, 2):
        pair = [
            mm(weight, jnp.concatenate([probe_ref[0, m], probe_ref[1, m]], axis=0))
            for m in (n, n + 1)
        ]
        both = jnp.concatenate(pair, axis=0).astype(BF16)
        for j in range(out_ref.shape[0]):
            out_ref[j, n * 8 : n * 8 + 16, :] = both[:, j * 128 : (j + 1) * 128]


def probe_flux(probe, weight):
    probes, rows, chans, lons = probe.shape
    blocks = lons // 128
    step = 4
    return pl.pallas_call(
        probe_flux_kernel,
        grid=(rows // step,),
        in_specs=[
            pl.BlockSpec((probes, step, chans, lons), lambda i: (0, i, 0, 0)),
            whole(weight.shape),
        ],
        out_specs=pl.BlockSpec((blocks, step * 8, 128), lambda i: (0, i, 0)),
        out_shape=jax.ShapeDtypeStruct((blocks, rows * 8, 128), BF16),
        compiler_params=params(),
        cost_estimate=cost(2 * 8 * probe.size, 2 * probe.size),
        name="probe_flux",
    )(probe, weight)


def filter_kernel(in_ref, fwd_ref, inv_ref, filt_ref, diff_ref, out_ref, wide, back):
    bands, _, pair, lons = in_ref.shape
    rows = pair // 2
    blocks = out_ref.shape[1]

    def load(b, carry):
        piece = in_ref[b, 0].astype(F32)
        at = pl.ds(pl.multiple_of(b * rows, 8), rows)
        wide[at, 0:lons] = piece[0:rows]
        wide[at, lons : 2 * lons] = piece[rows:pair]
        return carry

    lax.fori_loop(0, bands, load, 0)
    fwd = fwd_ref[...]
    inv = inv_ref[...]
    filt = filt_ref[0]
    chunk = 512

    def lat_filter(t, carry):
        at = pl.ds(pl.multiple_of(t * chunk, chunk), chunk)
        value = wide[:, at]
        filtered = (mm(fwd, value.astype(BF16)) * filt).astype(BF16)
        returned = mm(inv, filtered)
        back[:, at] = returned.astype(BF16)
        wide[:, at] = value + returned
        return carry

    lax.fori_loop(0, 2 * lons // chunk, lat_filter, 0)
    for p in range(2):
        for t in range(lons // 256):
            at = slice(p * lons + t * 256, p * lons + (t + 1) * 256)
            wide[:, at] = wide[:, at] + mm(
                back[:, p * lons : (p + 1) * lons], diff_ref[:, t * 256 : (t + 1) * 256]
            )

    def store(b, carry):
        at = pl.ds(pl.multiple_of(b * rows, 8), rows)
        for j in range(blocks):
            cols = slice(j * 128, (j + 1) * 128)
            more = slice(lons + j * 128, lons + (j + 1) * 128)
            out_ref[b, j, 0] = jnp.concatenate([wide[at, cols], wide[at, more]], axis=0).astype(
                BF16
            )
        return carry

    lax.fori_loop(0, bands, store, 0)


def lat_filter(received, fwd, inv, filt, diff):
    bands, chans, pair, lons = received.shape
    lats = fwd.shape[0]
    blocks = lons // 128
    return pl.pallas_call(
        filter_kernel,
        grid=(chans,),
        in_specs=[
            pl.BlockSpec((bands, 1, pair, lons), lambda i: (0, i, 0, 0)),
            whole(fwd.shape),
            whole(inv.shape),
            pl.BlockSpec((1, lats, 1), lambda i: (i, 0, 0)),
            whole(diff.shape),
        ],
        out_specs=pl.BlockSpec((bands, blocks, 1, pair, 128), lambda i: (0, 0, i, 0, 0)),
        out_shape=jax.ShapeDtypeStruct((bands, blocks, chans, pair, 128), BF16),
        scratch_shapes=[pltpu.VMEM((lats, 2 * lons), F32), pltpu.VMEM((lats, 2 * lons), BF16)],
        compiler_params=params(),
        cost_estimate=cost(8.4e9, 4 * received.size),
        name="lat_filter",
    )(received, fwd, inv, filt, diff)


def point_kernel(
    mixed_ref, slope_ref, win_ref, wout_ref, pflux_ref, cells_ref, out_ref, picked_ref, wide, flux
):
    chans, pair, lanes = mixed_ref.shape
    rows = pair // 2
    step = pl.program_id(0)

    @pl.when(step == 0)
    def _():
        def load(i, carry):
            at = pl.ds(pl.multiple_of(i * 8, 8), 8)
            wide[pl.ds(pl.multiple_of(i * 8 * pair, 8), 8 * pair), :] = (
                mixed_ref[at].astype(F32).reshape(8 * pair, lanes)
            )
            return carry

        lax.fori_loop(0, chans // 8, load, 0)

    value = jnp.concatenate(
        [wide[pl.ds(step + p * rows, chans, stride=pair), :] for p in range(2)], axis=1
    ).astype(BF16)
    slope = slope_ref[0].astype(F32)
    hidden = mm(win_ref[...], value)
    gated = (jnp.concatenate([slope, slope], axis=1) * hidden).astype(BF16)
    update = mm(wout_ref[...], gated)
    width = out_ref.shape[3]
    for j in range(out_ref.shape[0]):
        for p in range(2):
            out_ref[j, p, 0] = update[
                j * width : (j + 1) * width, p * lanes : (p + 1) * lanes
            ].astype(BF16)
    terms = update[chans : chans + 8]
    which = lax.broadcasted_iota(jnp.int32, (8, lanes), 0)
    flux[pl.ds(pl.multiple_of(step * 8, 8), 8), :] = jnp.where(
        which < 4, terms[:, 0:lanes], terms[:, lanes : 2 * lanes]
    )

    @pl.when(step == rows - 1)
    def _():
        total = flux[...]
        for j in range(pflux_ref.shape[0]):
            total = total + pflux_ref[j].astype(F32)
        total = total.astype(BF16)
        place = lax.broadcasted_iota(jnp.int32, (lanes, lanes), 0)
        for r in range(cells_ref.shape[0]):
            cells = cells_ref[r : r + 1, :]
            row = cells // lanes
            hot = jnp.where(place == cells - row * lanes, 1.0, 0.0).astype(BF16)
            found = mm(total, hot)
            picked = jnp.zeros((8, lanes), F32)
            for n in range(rows):
                picked = picked + jnp.where(row == n, found[n * 8 : (n + 1) * 8], 0.0)
            picked_ref[r] = picked


def pointwise(mixed, slope, win, wout, pflux, cells):
    chans, pair, lanes = mixed.shape
    rows, hid, _ = slope.shape
    blocks = pflux.shape[0]
    width = chans // blocks
    return pl.pallas_call(
        point_kernel,
        grid=(rows,),
        in_specs=[
            whole(mixed.shape),
            pl.BlockSpec((1, hid, lanes), lambda i: (i, 0, 0)),
            whole(win.shape),
            whole(wout.shape),
            whole(pflux.shape),
            whole(cells.shape),
        ],
        out_specs=[
            pl.BlockSpec((blocks, 2, 1, width, lanes), lambda i: (0, 0, i, 0, 0)),
            whole((cells.shape[0], 8, lanes)),
        ],
        out_shape=[
            jax.ShapeDtypeStruct((blocks, 2, rows, width, lanes), BF16),
            jax.ShapeDtypeStruct((cells.shape[0], 8, lanes), F32),
        ],
        scratch_shapes=[
            pltpu.VMEM((chans * pair, lanes), F32),
            pltpu.VMEM((rows * 8, lanes), F32),
        ],
        compiler_params=params(),
        cost_estimate=cost(7.3e9, 4 * mixed.size + 2 * slope.size),
        name="pointwise",
    )(mixed, slope, win, wout, pflux, cells)


def add_kernel(probe_ref, update_ref, out_ref):
    for j in range(update_ref.shape[0]):
        cols = slice(j * 128, (j + 1) * 128)
        out_ref[:, :, cols] = (
            probe_ref[:, :, cols].astype(F32) + update_ref[j].astype(F32)
        ).astype(BF16)


def add_update(probe, update):
    rows, chans, lons = probe.shape
    blocks = update.shape[0]
    step = 6
    return pl.pallas_call(
        add_kernel,
        grid=(rows // step,),
        in_specs=[
            pl.BlockSpec((step, chans, lons), lambda i: (i, 0, 0)),
            pl.BlockSpec((blocks, step, chans, 128), lambda i: (0, i, 0, 0)),
        ],
        out_specs=pl.BlockSpec((step, chans, lons), lambda i: (i, 0, 0)),
        out_shape=jax.ShapeDtypeStruct(probe.shape, BF16),
        compiler_params=params(),
        cost_estimate=cost(probe.size, 6 * probe.size),
        name="add_update",
    )(probe, update)


def depth_kernel(in_ref, kernel_ref, out_ref, wide):
    high, _, chans, broad = in_ref.shape
    rows = high - 6
    cols = broad - 6
    tiles = -(-chans // 8)
    for y in range(high):
        wide[y, 0:chans, 0:broad] = in_ref[y, 0].astype(F32)

    def tile(i, carry):
        at = pl.ds(pl.multiple_of(i * 8, 8), 8)
        weights = kernel_ref[at, :]
        total = [jnp.zeros((8, cols), F32) for _ in range(rows)]
        for b in range(7):
            taps = [
                jnp.broadcast_to(weights[:, 7 * a + b : 7 * a + b + 1], (8, cols))
                for a in range(7)
            ]
            for y in range(high):
                moved = wide[y, at, b : b + cols]
                for a in range(7):
                    if 0 <= y - a < rows:
                        total[y - a] = total[y - a] + moved * taps[a]
        for y in range(rows):
            out_ref[y, at, :] = total[y]
        return carry

    lax.fori_loop(0, tiles, tile, 0)


def depthwise(padded, kernel):
    high, probes, chans, broad = padded.shape
    rows, cols = high - 6, broad - 6
    full = -(-chans // 8) * 8
    kernel = jnp.pad(kernel, ((0, full - chans), (0, 0)))
    return pl.pallas_call(
        depth_kernel,
        grid=(probes,),
        in_specs=[
            pl.BlockSpec((high, 1, chans, broad), lambda p: (0, p, 0, 0)),
            whole(kernel.shape),
        ],
        out_specs=pl.BlockSpec((rows, full, cols), lambda p: (0, 0, p)),
        out_shape=jax.ShapeDtypeStruct((rows, full, probes * cols), F32),
        scratch_shapes=[pltpu.VMEM((high, full, -(-broad // 128) * 128), F32)],
        compiler_params=params(),
        cost_estimate=cost(200 * rows * cols * chans * probes, 4 * padded.size),
        name="depthwise",
    )(padded, kernel)


def combine_kernel(pool_ref, slots_ref, weights_ref, mask_ref, out_ref):
    bands, fields, cap = pool_ref.shape
    pool = pool_ref[...].reshape(bands * fields, cap).astype(BF16)
    rows, cols = mask_ref.shape
    place = lax.broadcasted_iota(jnp.int32, (cap, cols), 0)
    for y in range(rows):
        at = slice(y * cols, (y + 1) * cols)
        total = jnp.zeros((fields, cols), F32)
        for k in range(slots_ref.shape[0]):
            slots = slots_ref[k : k + 1, at]
            weights = weights_ref[k : k + 1, at]
            band = slots // cap
            hot = jnp.where(place == slots - band * cap, 1.0, 0.0).astype(BF16)
            found = mm(pool, hot)
            for b in range(bands):
                total = total + found[b * fields : (b + 1) * fields] * jnp.where(
                    band == b, weights, 0.0
                )
        out_ref[y] = total * mask_ref[y : y + 1, :]


def combine(pool, slots, weights, mask):
    fields = pool.shape[1]
    rows, cols = mask.shape
    return pl.pallas_call(
        combine_kernel,
        in_specs=[whole(a.shape) for a in (pool, slots, weights, mask)],
        out_specs=whole((rows, fields, cols)),
        out_shape=jax.ShapeDtypeStruct((rows, fields, cols), F32),
        compiler_params=params(),
        name="combine",
    )(pool, slots, weights, mask)


def normed_step(spread, base, sigma, gain):
    chans = spread.shape[0]
    wide_base = jnp.concatenate([base, base], axis=1)
    center = jnp.sum(spread, axis=0, keepdims=True) * (1.0 / chans)
    along = jnp.sum(wide_base * spread, axis=0, keepdims=True) * (1.0 / chans)
    scale = jnp.concatenate([sigma, sigma], axis=1)
    return (gain * scale * (spread - center - wide_base * along)).astype(BF16)


def fine_kernel(
    spread_ref,
    probe_ref,
    flux_ref,
    left_ref,
    right_ref,
    mask_ref,
    sigma_ref,
    base_ref,
    slope_ref,
    gain_ref,
    mix_ref,
    couple_ref,
    expand_ref,
    shrink_ref,
    pool_ref,
    down_ref,
    one_ref,
    coarse_ref,
    columns,
    held,
):
    step = pl.program_id(0)
    high = flux_ref.shape[0]
    cols = flux_ref.shape[2]

    @pl.when(step == 0)
    def _():
        for y in range(high):
            row = jnp.concatenate([left_ref[y], flux_ref[y], right_ref[y]], axis=1)
            for b in range(7):
                columns[(y * 7 + b) * 8 : (y * 7 + b + 1) * 8, :] = row[:, 125 + b : 125 + b + cols]

    near = columns[pl.ds(pl.multiple_of(step * 56, 8), 392), :].astype(BF16)
    center = columns[pl.ds(pl.multiple_of((step + 3) * 56 + 24, 8), 8), :].astype(BF16)
    spread = spread_ref[0] + jnp.concatenate([mm(mix_ref[p], near) for p in range(2)], axis=1)
    forcing = jnp.concatenate([mm(couple_ref[p], center) for p in range(2)], axis=1)
    start = (probe_ref[0].astype(F32) + forcing).astype(BF16).astype(F32)
    at = pl.ds(step, 1)
    tangent = normed_step(spread, base_ref[0].astype(F32), sigma_ref[at, :], gain_ref[...])
    slope = slope_ref[0].astype(F32)
    hidden = mm(expand_ref[...], tangent)
    gated = (hidden * jnp.concatenate([slope, slope], axis=1)).astype(BF16)
    mask = mask_ref[at, :]
    one = ((start + mm(shrink_ref[...], gated)) * jnp.concatenate([mask, mask], axis=1)).astype(BF16)
    one_ref[0] = one
    pooled = mm(one, pool_ref[...])

    @pl.when(step % 2 == 0)
    def _():
        held[...] = pooled

    @pl.when(step % 2 == 1)
    def _():
        coarse = mm(down_ref[...], (held[...] + pooled).astype(BF16)).astype(BF16)
        half = coarse.shape[1] // 2
        coarse_ref[0, 0] = coarse[:, 0:half]
        coarse_ref[0, 1] = coarse[:, half : 2 * half]


def fine_level(spread, probe, flux, left, right, mask, sigma, base, slope, gain, mix, couple, expand, shrink, pool, down):
    rows, chans, wide = spread.shape
    cols = wide // 2
    coarse = down.shape[0]
    row = lambda i: (i, 0, 0)
    return pl.pallas_call(
        fine_kernel,
        grid=(rows,),
        in_specs=[
            pl.BlockSpec((1, chans, wide), row),
            pl.BlockSpec((1, chans, wide), row),
            whole(flux.shape),
            whole(left.shape),
            whole(right.shape),
            whole(mask.shape),
            whole(sigma.shape),
            pl.BlockSpec((1, chans, cols), row),
            pl.BlockSpec((1, slope.shape[1], cols), row),
            whole(gain.shape),
            whole(mix.shape),
            whole(couple.shape),
            whole(expand.shape),
            whole(shrink.shape),
            whole(pool.shape),
            whole(down.shape),
        ],
        out_specs=[
            pl.BlockSpec((1, chans, wide), row),
            pl.BlockSpec((1, 2, coarse, cols // 2), lambda i: (i // 2, 0, 0, 0)),
        ],
        out_shape=[
            jax.ShapeDtypeStruct((rows, chans, wide), BF16),
            jax.ShapeDtypeStruct((rows // 2, 2, coarse, cols // 2), BF16),
        ],
        scratch_shapes=[
            pltpu.VMEM((flux.shape[0] * 56, cols), F32),
            pltpu.VMEM((chans, cols), F32),
        ],
        compiler_params=params(),
        name="fine_level",
    )(spread, probe, flux, left, right, mask, sigma, base, slope, gain, mix, couple, expand, shrink, pool, down)


def coarse_kernel(
    spread_ref,
    field_ref,
    sigma_ref,
    base_ref,
    slope_ref,
    gain_ref,
    expand_ref,
    shrink_ref,
    spreadout_ref,
    up_ref,
    one_ref,
    mask_ref,
    out_ref,
    wide,
):
    step = pl.program_id(0)
    chans = field_ref.shape[2]
    probes, fine, rows, cols = out_ref.shape
    field = jnp.concatenate([field_ref[0, 0], field_ref[0, 1]], axis=1).astype(F32)
    at = pl.ds(step, 1)
    tangent = normed_step(
        spread_ref[0, 0:chans], base_ref[0].astype(F32), sigma_ref[at, :], gain_ref[...]
    )
    slope = slope_ref[0].astype(F32)
    hidden = mm(expand_ref[...], tangent)
    gated = (hidden * jnp.concatenate([slope, slope], axis=1)).astype(BF16)
    two = (field + mm(shrink_ref[...], gated)).astype(BF16)
    raised = mm(up_ref[...], mm(two, spreadout_ref[...]).astype(BF16))
    for half in range(2):
        y = step * 2 + half
        mask = mask_ref[pl.ds(y, 1), :]
        for p in range(probes):
            for t in range(cols // 128):
                lanes = slice(p * cols + t * 128, p * cols + (t + 1) * 128)
                wide[p, t, pl.ds(y, fine, stride=rows), :] = (
                    one_ref[half, :, lanes].astype(F32) + raised[:, lanes]
                ) * mask[:, t * 128 : (t + 1) * 128]

    @pl.when(step == rows // 2 - 1)
    def _():
        for p in range(probes):
            for t in range(cols // 128):
                out_ref[p, :, :, t * 128 : (t + 1) * 128] = (
                    wide[p, t].reshape(fine, rows, 128).astype(BF16)
                )


def coarse_level(spread, field, sigma, base, slope, gain, expand, shrink, spreadout, up, one, mask):
    lines, probes, chans, half = field.shape
    rows, fine, wide = one.shape
    cols = wide // 2
    row = lambda i: (i, 0, 0)
    return pl.pallas_call(
        coarse_kernel,
        grid=(lines,),
        in_specs=[
            pl.BlockSpec((1,) + spread.shape[1:], row),
            pl.BlockSpec((1, probes, chans, half), lambda i: (i, 0, 0, 0)),
            whole(sigma.shape),
            pl.BlockSpec((1, chans, half), row),
            pl.BlockSpec((1, slope.shape[1], half), row),
            whole(gain.shape),
            whole(expand.shape),
            whole(shrink.shape),
            whole(spreadout.shape),
            whole(up.shape),
            pl.BlockSpec((2, fine, wide), row),
            whole(mask.shape),
        ],
        out_specs=whole((probes, fine, rows, cols)),
        out_shape=jax.ShapeDtypeStruct((probes, fine, rows, cols), BF16),
        scratch_shapes=[pltpu.VMEM((probes, cols // 128, fine * rows, 128), F32)],
        compiler_params=params(),
        name="coarse_level",
    )(spread, field, sigma, base, slope, gain, expand, shrink, spreadout, up, one, mask)


def shifted(block, axis):
    count = lax.axis_size(axis)
    forward = [(i, i + 1) for i in range(count - 1)]
    backward = [(i + 1, i) for i in range(count - 1)]
    return (
        lambda low: lax.ppermute(low, axis, forward),
        lambda high: lax.ppermute(high, axis, backward),
    )


def with_halo(block, sides, width):
    for axis, dim in sides:
        up, down = shifted(block, axis)
        low = up(lax.slice_in_dim(block, block.shape[dim] - width, None, axis=dim))
        high = down(lax.slice_in_dim(block, 0, width, axis=dim))
        block = jnp.concatenate([low, block, high], axis=dim)
    return block


def local(
    probe_field,
    gate_slope,
    spectral_filter,
    weight_in,
    weight_out,
    weight_flux,
    send_cells,
    recv_slots,
    recv_weights,
    ocean_probe,
    ocean_mask,
    coupling,
    base_fine,
    sigma_fine,
    slope_fine,
    gain_fine,
    kernel_fine,
    expand_fine,
    shrink_fine,
    down_proj,
    base_coarse,
    sigma_coarse,
    slope_coarse,
    gain_coarse,
    kernel_coarse,
    expand_coarse,
    shrink_coarse,
    up_proj,
):
    probes, rows, width, lons = probe_field.shape
    bands = lax.axis_size("lat")
    blocks = lax.axis_size("chan")
    part = width // bands
    pair = probes * rows
    lats = rows * bands
    chans = width * blocks
    fields = weight_flux.shape[1]

    flat_probe = probe_field.reshape(pair, width, lons)
    turned = turn_channels(flat_probe).reshape(bands, part, pair, lons)
    gathered = lax.all_to_all(turned, "lat", split_axis=0, concat_axis=0, tiled=True)

    flux_rows = lax.dynamic_slice_in_dim(
        weight_flux, lax.axis_index("chan") * width, width, 0
    ).T
    none = jnp.zeros_like(flux_rows)
    flux_pair = jnp.concatenate(
        [
            jnp.concatenate([flux_rows, none], axis=1),
            jnp.concatenate([none, flux_rows], axis=1),
        ],
        axis=0,
    )
    probe_terms = lax.all_to_all(
        probe_flux(probe_field, flux_pair), "chan", split_axis=0, concat_axis=0, tiled=True
    )

    fwd_lon, inv_lon = fourier_tables(lons)
    fwd_lat, inv_lat = cosine_tables(lats)
    diff = (mm(fwd_lon, inv_lon) - jnp.eye(lons, dtype=F32)).astype(BF16)
    filt = lax.dynamic_slice_in_dim(
        spectral_filter, lax.axis_index("lat") * part, part, 1
    ).T.reshape(part, lats, 1)
    mixed = lat_filter(gathered, fwd_lat.T, inv_lat.T, filt, diff)
    regrouped = lax.all_to_all(
        mixed.reshape(bands * blocks, part, pair, 128),
        ("lat", "chan"),
        split_axis=0,
        concat_axis=0,
        tiled=True,
    ).reshape(chans, pair, 128)

    win = (
        weight_in.reshape(blocks, bands, part, -1).transpose(1, 0, 2, 3).reshape(chans, -1).T
    )
    folded = mm(weight_out, weight_flux).astype(BF16)
    wout = jnp.concatenate([weight_out, folded, folded], axis=1).T
    update, picked = pointwise(
        regrouped, gate_slope, win, wout, probe_terms, send_cells[0]
    )
    update_back = lax.all_to_all(update, "chan", split_axis=0, concat_axis=0, tiled=True)
    atmos_out = add_update(flat_probe, update_back.reshape(blocks, pair, width, 128)).reshape(
        probe_field.shape
    )

    tile_rows, tile_cols = ocean_mask.shape
    fine = ocean_probe.shape[1]
    mask = ocean_mask.astype(F32)
    masked = ocean_probe * ocean_mask.astype(BF16)
    padded = with_halo(masked, (("lat", 2), ("chan", 3)), 3).transpose(2, 0, 1, 3)
    spread = depthwise(padded, kernel_fine)
    start = masked.transpose(2, 1, 0, 3).reshape(tile_rows, fine, probes * tile_cols)
    base_rows = base_fine.transpose(1, 0, 2)
    slope_rows = slope_fine.transpose(1, 0, 2)
    base_lines = base_coarse.transpose(1, 0, 2)
    slope_lines = slope_coarse.transpose(1, 0, 2)
    couple_t = coupling.T
    no_couple = jnp.zeros_like(couple_t)
    couple = jnp.stack(
        [
            jnp.concatenate([couple_t, no_couple], axis=1),
            jnp.concatenate([no_couple, couple_t], axis=1),
        ]
    )
    mix = (kernel_fine[None, :, :, None] * couple.astype(F32)[:, :, None, :]).astype(BF16)
    mix = mix.reshape(probes, fine, 49 * probes * fields)
    lane = jnp.arange(probes * tile_cols, dtype=jnp.int32)
    meets = lane[:, None] // 2 == jnp.arange(probes * tile_cols // 2, dtype=jnp.int32)[None, :]
    pool = jnp.where(meets, 0.25, 0.0).astype(BF16)
    spreadout = jnp.where(meets.T, 1.0, 0.0).astype(BF16)

    arrived = lax.all_to_all(picked, "lat", split_axis=0, concat_axis=0, tiled=True)
    flux = combine(arrived, recv_slots[0], recv_weights[0], mask)
    up, down = shifted(flux, "lat")
    tall = jnp.concatenate([up(flux[tile_rows - 3 :]), flux, down(flux[:3])], axis=0)
    up, down = shifted(flux, "chan")
    left = up(tall[:, :, tile_cols - 128 :])
    right = down(tall[:, :, :128])
    one, coarse = fine_level(
        spread,
        start,
        tall,
        left,
        right,
        mask,
        sigma_fine,
        base_rows,
        slope_rows,
        gain_fine[:, None],
        mix,
        couple,
        expand_fine.T,
        shrink_fine.T,
        pool,
        down_proj.T,
    )
    coarse_padded = with_halo(coarse, (("lat", 0), ("chan", 3)), 3)
    coarse_spread = depthwise(coarse_padded, kernel_coarse)
    ocean_out = coarse_level(
        coarse_spread,
        coarse,
        sigma_coarse,
        base_lines,
        slope_lines,
        gain_coarse[:, None],
        expand_coarse.T,
        shrink_coarse.T,
        spreadout,
        up_proj.T,
        one,
        mask,
    )
    return (atmos_out, ocean_out)


def solution(mesh):
    tile = P(("lat", "chan"), None, None)
    rows_cols = P(None, "lat", "chan")
    return jax.shard_map(
        local,
        mesh=mesh,
        in_specs=(
            P(None, "lat", "chan", None),
            P("lat", None, "chan"),
            P(None, "chan"),
            P(),
            P(),
            P(),
            tile,
            tile,
            tile,
            P(None, None, "lat", "chan"),
            P("lat", "chan"),
            P(),
            rows_cols,
            P("lat", "chan"),
            rows_cols,
            P(),
            P(),
            P(),
            P(),
            P(),
            rows_cols,
            P("lat", "chan"),
            rows_cols,
            P(),
            P(),
            P(),
            P(),
            P(),
        ),
        out_specs=(P(None, "lat", "chan", None), P(None, None, "lat", "chan")),
        check_vma=False,
    )
```

time: 895 us -> 507 us (0.57); the launches traced: 880 us -> 501 us
  Pallas kernels: 0 us -> 231 us
  local copies, waits for them, and re-layouts: 279 us -> 57.6 us
  waiting for transfers between devices: 258 us -> 61.2 us
  other arithmetic: 176 us -> 46.2 us
  matrix products: 94.9 us -> 21.1 us
  starting transfers between devices: 54.7 us -> 83.3 us
  between operations: 15.8 us -> 1 us
    pallas_call x0 -> x10, Pallas kernels: none -> 231 us  [the longest x2 138 us: depthwise(): pl.pallas_call(depth_kernel, grid=(probes,), in_specs=[pl.BlockSpec((high...]
    all_to_all x5, waiting for transfers between devices: 216 us -> 53 us  [the longest x1 32.8 us: local(): lax.all_to_all(mixed.reshape(bands * blocks, part, pair, 128), ('lat', 'c...]
    reduce_sum x4 -> x0, other arithmetic: 128 us -> none  [the longest x2 99.4 us: level_tangent(): center = jnp.mean(spread, axis=1, keepdims=True)]
    dot_general x10 -> x2, matrix products: 94.9 us -> 21.1 us  [mm(): return jnp.dot(a, b, preferred_element_type=F32)]
    gather x3 -> x0, local copies, waits for them, and re-layouts: 61.8 us -> none  [the longest x1 54 us: local(): taken = jnp.take(pool_slots, recv_slots.reshape(-1), axis=2)]
    convert_element_type x9 -> x0, local copies, waits for them, and re-layouts: 57.7 us -> none  [the longest x1 15.2 us: local(): mixed = (probe_field.astype(jnp.float32) + spatial).astype(jnp.bfloat16)]
    unnamed x158 -> x56, local copies, waits for them, and re-layouts: 70.3 us -> 16.9 us
    all_to_all x5 -> x0, local copies, waits for them, and re-layouts: 29 us -> none  [the longest x1 13.8 us: to_columns(): lax.all_to_all(mixed, 'chan', split_axis=3, concat_axis=2, tiled=True)]
  transfers between devices with their start and end apart: 14 -> 17, of which waited for: 10 -> 5; matrix products, arithmetic and copies ran while one was open for 7% -> 25% of each run, Pallas kernels for 0% -> 43%
where the time goes in v1:
time: 507 us; the launch traced here: 501 us
  Pallas kernels  231 us (46%)
  starting transfers between devices  83.3 us (16%)
  waiting for transfers between devices  61.2 us (12%)
  local copies, waits for them, and re-layouts  57.6 us (11%)
  other arithmetic  46.2 us (9%)
  matrix products  21.1 us (4%)
    pallas_call x2, Pallas kernels, depthwise(): pl.pallas_call(depth_kernel, grid=(probes,), in_specs=[pl.BlockSpec((high...  138 us
    ppermute x6, starting transfers between devices, shifted(): lax.ppermute(low, axis, forward)  33 us
    all_to_all x1, waiting for transfers between devices, local(): lax.all_to_all(mixed.reshape(bands * blocks, part, pair, 128), ('lat', 'c...  32.8 us
    pallas_call x1, Pallas kernels, pointwise(): pl.pallas_call(point_kernel, grid=(rows,), in_specs=[whole(mixed.shape),...  27.9 us
    dot_general x2, matrix products, mm(): return jnp.dot(a, b, preferred_element_type=F32)  21.1 us
    pallas_call x1, Pallas kernels, lat_filter(): pl.pallas_call(filter_kernel, grid=(chans,), in_specs=[pl.BlockSpec((band...  18.8 us
    dot_general x1, other arithmetic, mm(): return jnp.dot(a, b, preferred_element_type=F32)  18.5 us
    all_to_all x1, waiting for transfers between devices, local(): lax.all_to_all(turned, 'lat', split_axis=0, concat_axis=0, tiled=True)  18.2 us
  transfers between devices with their start and end apart: 17, of which 5 were waited for; matrix products, arithmetic and copies ran while one was open for 25% of the time, Pallas kernels for 43%

profile of v1, /device:TPU:32, one launch (start us, length us, event | category | flops | bytes accessed | tf_op | source)
XLA Modules:
  0.0 501.0 jit_solution(4243244053462255217)
XLA Ops:
  0.6 8.2 %turn_channels.1 = bf16[48,48,1024]{2,1,0:T(8,128)(2,1)} custom-call(bf16[48,48,1024]{2,1,0:T(8,128)(2,1)} %bitcast.57), custom_call_target="tpu_custom_call" | custom-call | bytes 9437184 | tf_op jit(solution)/shard_map/turn_channels/pallas_call | solution.py:67
  8.8 8.0 %all-to-all-start = ((bf16[16,3,48,1024]{3,2,1,0:T(8,128)(2,1)}), bf16[16,3,48,1024]{3,2,1,0:T(8,128)(2,1)}, u32[]{:S(2)}, u32[]{:S(2)}) async-start(bf16[16,3,48,1024]{3,2,1,0:T(8,128)(2,1)} %bitcast.59), calls=%async_computation | async-start | bytes 9437184 | tf_op jit(solution)/shard_map/all_to_all | solution.py:633
  18.7 5.5 %probe_flux.1 = bf16[8,192,128]{2,1,0:T(8,128)(2,1)} custom-call(bf16[2,24,48,1024]{3,2,1,0:T(8,128)(2,1)} %probe_ref.1, bf16[8,96]{1,0:T(8,128)(2,1)} %fusion.43.weight_ref), custom_call_target="tpu_custom_call" | custom-call | flops 37748736 | bytes 4718592 | tf_op jit(solution)/shard_map/probe_flux/pallas_call | solution.py:97
  24.2 5.5 %fusion.32 = (bf16[384,384]{1,0:T(8,128)(2,1)}, bf16[384,384]{1,0:T(8,128)(2,1)}) fusion(f32[384]{0:T(512)S(1)} %fusion.47, s32[384]{0:T(512)S(1)} %multiply_add_fusion), kind=kLoop, calls=%fused_computation.54 | loop fusion | flops 3244032 | bytes 592896 | tf_op jit(solution)/shard_map/convert_element_type | solution.py:54
  29.7 18.5 %multiply_convert_fusion.15 = bf16[1024,1024]{1,0:T(8,128)(2,1)S(1)} fusion(f32[1024]{0:T(1024)S(1)} %fusion.42, s32[1024]{0:T(1024)S(1)} %add_select_fusion.4, pred[1024]{0:T(1024)(128)(4,1)S(1)} %iota_compare_fusion.7), kind=kLoop, calls=%fused_computation.15.clone.clone.clone.clone.2 | loop fusion | flops 17825792 | bytes 2106368 | tf_op jit(solution)/shard_map/dot_general | solution.py:25
  48.2 19.8 %subtract_convert_fusion.diff_ref = bf16[1024,1024]{1,0:T(8,128)(2,1)} fusion(s32[1024]{0:T(1024)S(1)} %add_select_fusion.4, pred[1024]{0:T(1024)(128)(4,1)S(1)} %iota_compare_fusion.7, bf16[1024,1024]{1,0:T(8,128)(2,1)S(1)} %multiply_convert_fusion.15), kind=kOutput, calls=%fused_computation.13 | convolution fusion | flops 2169503744 | bytes 4199424 | tf_op jit(solution)/shard_map/dot_general | solution.py:25
  68.0 18.2 %all-to-all-done.in_ref = bf16[16,3,48,1024]{3,2,1,0:T(8,128)(2,1)} async-done(((bf16[16,3,48,1024]{3,2,1,0:T(8,128)(2,1)}), bf16[16,3,48,1024]{3,2,1,0:T(8,128)(2,1)}, u32[]{:S(2)}, u32[]{:S(2)}) %all-to-all-start) | async-done | bytes 4718624 | tf_op jit(solution)/shard_map/all_to_all | solution.py:633
  86.2 4.5 all-to-all-start.2
  90.6 18.8 %lat_filter.1 = bf16[16,8,3,48,128]{4,3,2,1,0:T(8,128)(2,1)} custom-call(bf16[16,3,48,1024]{3,2,1,0:T(8,128)(2,1)} %all-to-all-done.in_ref, bf16[384,384]{1,0:T(8,128)(2,1)} %get-tuple-element.29.fwd_ref, bf16[384,384]{1,0:T(8,128)(2,1)} %get-tuple-element.28.inv_ref, f32[3,384,1]{2,1,0:T(8,128)} %copy.66.filt_ref, ...), custom_call_target="tpu_custom_call" | custom-call | flops 8400000000 | bytes 9437184 | tf_op jit(solution)/shard_map/lat_filter/pallas_call | solution.py:164
  110.2 9.5 %all-to-all-start.1 = ((bf16[128,3,48,128]{3,2,1,0:T(8,128)(2,1)}), bf16[128,3,48,128]{3,2,1,0:T(8,128)(2,1)}, u32[]{:S(2)}, u32[]{:S(2)}) async-start(bf16[128,3,48,128]{3,2,1,0:T(8,128)(2,1)} %bitcast.63), calls=%async_computation.1 | async-start | bytes 9437184 | tf_op jit(solution)/shard_map/all_to_all | solution.py:657
  122.0 4.5 collective-permute-start.1
  144.7 32.8 %all-to-all-done.1 = bf16[128,3,48,128]{3,2,1,0:T(8,128)(2,1)} async-done(((bf16[128,3,48,128]{3,2,1,0:T(8,128)(2,1)}), bf16[128,3,48,128]{3,2,1,0:T(8,128)(2,1)}, u32[]{:S(2)}, u32[]{:S(2)}) %all-to-all-start.1) | async-done | bytes 4718624 | tf_op jit(solution)/shard_map/all_to_all | solution.py:657
  177.5 27.9 %pointwise.1 = (bf16[8,2,24,48,128]{4,3,2,1,0:T(8,128)(2,1)}, f32[16,8,128]{2,1,0:T(8,128)}) custom-call(bf16[384,48,128]{2,1,0:T(8,128)(2,1)} %bitcast.5.mixed_ref, bf16[24,768,128]{2,1,0:T(8,128)(2,1)} %slope_ref.1, bf16[768,384]{1,0:T(8,128)(2,1)} %bitcast.70, bf16[392,768]{1,0:T(8,128)(2,1)} %maximum_bitcast_fusion.1.wout_ref, ...), custom_call_target="tpu_custom_call" | custom-call | flops 7299999744 | bytes 14155776 | tf_op jit(solution)/shard_map/pointwise/pallas_call | solution.py:243
  205.4 5.7 %all-to-all-start.4 = ((f32[16,8,128]{2,1,0:T(8,128)}), f32[16,8,128]{2,1,0:T(8,128)S(1)}, u32[]{:S(2)}, u32[]{:S(2)}) async-start(f32[16,8,128]{2,1,0:T(8,128)} %get-tuple-element.7), calls=%async_computation.4 | async-start | bytes 131072 | tf_op jit(solution)/shard_map/all_to_all | solution.py:704
  218.0 4.6 all-to-all-start.3
  263.9 19.1 %collective-permute-start.6 = (f32[14,8,128]{2,1,0:T(8,128)S(1)}, f32[14,8,128]{2,1,0:T(8,128)S(1)}, u32[]{:S(2)}, u32[]{:S(2)}) collective-permute-start(f32[14,8,128]{2,1,0:T(8,128)S(1)} %get-tuple-element.19), channel_id=1, source_target_pairs={{0,1},{1,2},{2,3},{3,4},{4,5},{5,6},{6,7},{8,9},{9,10},{10,11},{11... | collective-permute-start | bytes 172040 | tf_op jit(solution)/shard_map/ppermute | solution.py:578
  284.5 6.3 %maximum_bitcast_fusion.in_ref = bf16[14,2,200,262]{3,2,1,0:T(8,128)(2,1)} fusion(bf16[2,200,14,3]{3,1,0,2:T(8,128)(2,1)S(1)} %copy.74, bf16[2,200,3,256]{3,1,0,2:T(8,128)(2,1)} %collective-permute-done.1, bf16[2,200,8,256]{3,1,0,2:T(8,128)(2,1)S(1)} %copy_multiply_fusion, bf16[2,200,3,256]{3,1,0,2:T(8,128)(2,1)} %collective-permute-done, ...), kind=kLoop, calls=%fused_computation.6 | loop fusion | flops 14672000 | bytes 5868800 | tf_op jit(solution)/shard_map/transpose | solution.py:682
  290.8 81.7 %depthwise.2.spread_ref = f32[8,200,512]{2,1,0:T(8,128)} custom-call(bf16[14,2,200,262]{3,2,1,0:T(8,128)(2,1)} %maximum_bitcast_fusion.in_ref, f32[200,49]{1,0:T(8,128)} %copy.75.kernel_ref), custom_call_target="tpu_custom_call" | custom-call | flops 163840000 | bytes 5868800 | tf_op jit(solution)/shard_map/depthwise/pallas_call | solution.py:333
  373.2 13.5 %fine_level.1 = (bf16[8,200,512]{2,1,0:T(8,128)(2,1)}, bf16[4,2,250,128]{3,2,1,0:T(8,128)(2,1)}) custom-call(f32[8,200,512]{2,1,0:T(8,128)} %depthwise.2.spread_ref, bf16[8,200,512]{2,1,0:T(8,128)(2,1)} %bitcast.61, f32[14,8,256]{2,1,0:T(8,128)} %copy-done.5, f32[14,8,128]{2,1,0:T(8,128)} %copy-done.15, f32[14,8,128]{2,1,0:T(8,128)} %copy-done.16, ...), custom_call_target="tpu_custom_call" | custom-call | tf_op jit(solution)/shard_map/fine_level/pallas_call | solution.py:457
  390.3 5.5 %collective-permute-start.9 = (bf16[3,2,250,128]{3,2,1,0:T(8,128)(2,1)S(1)}, bf16[3,2,250,128]{3,2,1,0:T(8,128)(2,1)S(1)}, u32[]{:S(2)}, u32[]{:S(2)}) collective-permute-start(bf16[3,2,250,128]{3,2,1,0:T(8,128)(2,1)S(1)} %get-tuple-element.16), channel_id=1, source_target_pairs={{8,0},{16,8},{24,16},{32,24},{40,32},{48,40},{56,48},{64,56},{72,6... | collective-permute-start | bytes 1152008 | tf_op jit(solution)/shard_map/ppermute | solution.py:579
  395.8 7.9 %collective-permute-done.8 = bf16[3,2,250,128]{3,2,1,0:T(8,128)(2,1)S(1)} collective-permute-done((bf16[3,2,250,128]{3,2,1,0:T(8,128)(2,1)S(1)}, bf16[3,2,250,128]{3,2,1,0:T(8,128)(2,1)S(1)}, u32[]{:S(2)}, u32[]{:S(2)}) %collective-permute-start.8) | collective-permute-done | bytes 384032 | tf_op jit(solution)/shard_map/ppermute | solution.py:578
  428.5 56.2 %depthwise.3.spread_ref = f32[4,256,256]{2,1,0:T(8,128)} custom-call(bf16[10,2,250,134]{3,2,1,0:T(8,128)(2,1)} %pad_maximum_fusion.1.in_ref, f32[256,49]{1,0:T(8,128)} %pad.8.kernel_ref), custom_call_target="tpu_custom_call" | custom-call | flops 51200000 | bytes 2680000 | tf_op jit(solution)/shard_map/depthwise/pallas_call | solution.py:333
  484.7 7.9 %coarse_level.1 = bf16[2,200,8,256]{3,2,1,0:T(8,128)(2,1)} custom-call(f32[4,256,256]{2,1,0:T(8,128)} %depthwise.3.spread_ref, bf16[4,2,250,128]{3,2,1,0:T(8,128)(2,1)} %get-tuple-element.8.field_ref, f32[4,128]{1,0:T(4,128)} %sigma_ref.3, bf16[4,250,128]{2,1,0:T(8,128)(2,1)} %bitcast.69, bf16[4,1000,128]{2,1,0:T(8,128)(2,1)} %bitcast.64, ...), custom_call_target="tpu_custom_call" | custom-call | tf_op jit(solution)/shard_map/coarse_level/pallas_call | solution.py:548
  492.6 8.4 %add_update.1 = bf16[48,48,1024]{2,1,0:T(8,128)(2,1)} custom-call(bf16[48,48,1024]{2,1,0:T(8,128)(2,1)} %bitcast.58, bf16[8,48,48,128]{3,2,1,0:T(8,128)(2,1)} %bitcast.11.update_ref), custom_call_target="tpu_custom_call" | custom-call | flops 2359296 | bytes 14155776 | tf_op jit(solution)/shard_map/add_update/pallas_call | solution.py:284
  (131 shorter events, 101.7 us)
Async XLA Ops:
  0.6 16.2 %copy-start = (f32[384,48]{0,1:T(8,128)S(1)}, f32[384,48]{0,1:T(8,128)}, u32[]{:S(2)}) copy-start(f32[384,48]{0,1:T(8,128)} %param.30) | copy-start | bytes 221188
  8.8 77.4 %all-to-all-start = ((bf16[16,3,48,1024]{3,2,1,0:T(8,128)(2,1)}), bf16[16,3,48,1024]{3,2,1,0:T(8,128)(2,1)}, u32[]{:S(2)}, u32[]{:S(2)}) async-start(bf16[16,3,48,1024]{3,2,1,0:T(8,128)(2,1)} %bitcast.59), calls=%async_computation | async-start | bytes 9437184 | tf_op jit(solution)/shard_map/all_to_all | solution.py:633
  86.2 23.3 %all-to-all-start.2 = ((bf16[8,192,128]{2,1,0:T(8,128)(2,1)}), bf16[8,192,128]{2,1,0:T(8,128)(2,1)S(1)}, u32[]{:S(2)}, u32[]{:S(2)}) async-start(bf16[8,192,128]{2,1,0:T(8,128)(2,1)} %probe_flux.1), calls=%async_computation.2 | async-start | bytes 786432 | tf_op jit(solution)/shard_map/all_to_all | solution.py:646
  110.2 67.3 %all-to-all-start.1 = ((bf16[128,3,48,128]{3,2,1,0:T(8,128)(2,1)}), bf16[128,3,48,128]{3,2,1,0:T(8,128)(2,1)}, u32[]{:S(2)}, u32[]{:S(2)}) async-start(bf16[128,3,48,128]{3,2,1,0:T(8,128)(2,1)} %bitcast.63), calls=%async_computation.1 | async-start | bytes 9437184 | tf_op jit(solution)/shard_map/all_to_all | solution.py:657
  120.9 18.7 %copy-start.19 = (bf16[4,200]{1,0:T(4,128)(2,1)S(1)}, bf16[4,200]{1,0:T(4,128)(2,1)}, u32[]{:S(2)}) copy-start(bf16[4,200]{1,0:T(4,128)(2,1)} %param.39) | copy-start | bytes 4804
  122.0 104.5 %collective-permute-start.1 = (bf16[2,200,3,256]{3,1,0,2:T(8,128)(2,1)}, bf16[2,200,3,256]{3,1,0,2:T(8,128)(2,1)}, u32[]{:S(2)}, u32[]{:S(2)}) collective-permute-start(bf16[2,200,3,256]{3,1,0,2:T(8,128)(2,1)} %get-tuple-element.13), channel_id=1, source_target_pairs={{8,0},{16,8},{24,16},{32,24},{40,32},{48,40},{56,48},{64,56},{72,6... | collective-permute-start | bytes 1843208 | tf_op jit(solution)/shard_map/ppermute | solution.py:579
  126.5 16.4 %copy-start.12 = (f32[200,49]{0,1:T(8,128)S(1)}, f32[200,49]{0,1:T(8,128)}, u32[]{:S(2)}) copy-start(f32[200,49]{0,1:T(8,128)} %param.44) | copy-start | bytes 117604
  126.5 100.0 %collective-permute-start = (bf16[2,200,3,256]{3,1,0,2:T(8,128)(2,1)}, bf16[2,200,3,256]{3,1,0,2:T(8,128)(2,1)}, u32[]{:S(2)}, u32[]{:S(2)}) collective-permute-start(bf16[2,200,3,256]{3,1,0,2:T(8,128)(2,1)} %get-tuple-element.12), channel_id=1, source_target_pairs={{0,8},{8,16},{16,24},{24,32},{32,40},{40,48},{48,56},{56,64},{64,7... | collective-permute-start | bytes 1843208 | tf_op jit(solution)/shard_map/ppermute | solution.py:578
  205.4 12.0 %all-to-all-start.4 = ((f32[16,8,128]{2,1,0:T(8,128)}), f32[16,8,128]{2,1,0:T(8,128)S(1)}, u32[]{:S(2)}, u32[]{:S(2)}) async-start(f32[16,8,128]{2,1,0:T(8,128)} %get-tuple-element.7), calls=%async_computation.4 | async-start | bytes 131072 | tf_op jit(solution)/shard_map/all_to_all | solution.py:704
  218.0 274.5 %all-to-all-start.3 = ((bf16[8,2,24,48,128]{4,3,2,1,0:T(8,128)(2,1)}), bf16[8,2,24,48,128]{4,3,2,1,0:T(8,128)(2,1)}, u32[]{:S(2)}, u32[]{:S(2)}) async-start(bf16[8,2,24,48,128]{4,3,2,1,0:T(8,128)(2,1)} %get-tuple-element.6), calls=%async_computation.3 | async-start | bytes 9437184 | tf_op jit(solution)/shard_map/all_to_all | solution.py:673
  228.1 22.3 %copy-start.3 = (bf16[8,2,25,8,256]{4,3,2,1,0:T(8,128)(2,1)S(1)}, bf16[8,2,25,8,256]{4,3,2,1,0:T(8,128)(2,1)}, u32[]{:S(2)}) copy-start(bf16[8,2,25,8,256]{4,3,2,1,0:T(8,128)(2,1)} %fusion.63) | copy-start | bytes 4915204
  232.2 27.6 %collective-permute-start.3 = (bf16[2,200,14,3]{1,0,3,2:T(2,128)(2,1)S(1)}, bf16[2,200,14,3]{1,0,3,2:T(2,128)(2,1)S(1)}, u32[]{:S(2)}, u32[]{:S(2)}) collective-permute-start(bf16[2,200,14,3]{1,0,3,2:T(2,128)(2,1)S(1)} %copy.72), channel_id=1, source_target_pairs={{1,0},{2,1},{3,2},{4,3},{5,4},{6,5},{7,6},{9,8},{10,9},{11,10},{12... | collective-permute-start | bytes 100808 | tf_op jit(solution)/shard_map/ppermute | solution.py:579
  235.4 25.4 %collective-permute-start.2 = (bf16[2,200,14,3]{1,0,3,2:T(2,128)(2,1)S(1)}, bf16[2,200,14,3]{1,0,3,2:T(2,128)(2,1)}, u32[]{:S(2)}, u32[]{:S(2)}) collective-permute-start(bf16[2,200,14,3]{1,0,3,2:T(2,128)(2,1)S(1)} %copy.71), channel_id=1, source_target_pairs={{0,1},{1,2},{2,3},{3,4},{4,5},{5,6},{6,7},{8,9},{9,10},{10,11},{11... | collective-permute-start | bytes 100808 | tf_op jit(solution)/shard_map/ppermute | solution.py:578
  242.9 20.2 %collective-permute-start.5 = (f32[3,8,256]{2,1,0:T(8,128)}, f32[3,8,256]{2,1,0:T(8,128)}, u32[]{:S(2)}, u32[]{:S(2)}) collective-permute-start(f32[3,8,256]{2,1,0:T(8,128)} %get-tuple-element.21), channel_id=1, source_target_pairs={{8,0},{16,8},{24,16},{32,24},{40,32},{48,40},{56,48},{64,56},{72,6... | collective-permute-start | bytes 73736 | tf_op jit(solution)/shard_map/ppermute | solution.py:579
  246.9 16.2 %collective-permute-start.4 = (f32[3,8,256]{2,1,0:T(8,128)}, f32[3,8,256]{2,1,0:T(8,128)}, u32[]{:S(2)}, u32[]{:S(2)}) collective-permute-start(f32[3,8,256]{2,1,0:T(8,128)} %get-tuple-element.20), channel_id=1, source_target_pairs={{0,8},{8,16},{16,24},{24,32},{32,40},{40,48},{48,56},{56,64},{64,7... | collective-permute-start | bytes 73736 | tf_op jit(solution)/shard_map/ppermute | solution.py:578
  263.8 27.0 %copy-start.5 = (f32[14,8,256]{2,1,0:T(8,128)}, f32[14,8,256]{2,1,0:T(8,128)S(1)}, u32[]{:S(2)}) copy-start(f32[14,8,256]{2,1,0:T(8,128)S(1)} %pad_maximum_fusion.2.flux_ref) | copy-start | bytes 344068
  263.9 108.7 %collective-permute-start.6 = (f32[14,8,128]{2,1,0:T(8,128)S(1)}, f32[14,8,128]{2,1,0:T(8,128)S(1)}, u32[]{:S(2)}, u32[]{:S(2)}) collective-permute-start(f32[14,8,128]{2,1,0:T(8,128)S(1)} %get-tuple-element.19), channel_id=1, source_target_pairs={{0,1},{1,2},{2,3},{3,4},{4,5},{5,6},{6,7},{8,9},{9,10},{10,11},{11... | collective-permute-start | bytes 172040 | tf_op jit(solution)/shard_map/ppermute | solution.py:578
  282.9 89.6 %collective-permute-start.7 = (f32[14,8,128]{2,1,0:T(8,128)S(1)}, f32[14,8,128]{2,1,0:T(8,128)S(1)}, u32[]{:S(2)}, u32[]{:S(2)}) collective-permute-start(f32[14,8,128]{2,1,0:T(8,128)S(1)} %get-tuple-element.18), channel_id=1, source_target_pairs={{1,0},{2,1},{3,2},{4,3},{5,4},{6,5},{7,6},{9,8},{10,9},{11,10},{12... | collective-permute-start | bytes 172040 | tf_op jit(solution)/shard_map/ppermute | solution.py:579
  387.8 15.8 %collective-permute-start.8 = (bf16[3,2,250,128]{3,2,1,0:T(8,128)(2,1)S(1)}, bf16[3,2,250,128]{3,2,1,0:T(8,128)(2,1)S(1)}, u32[]{:S(2)}, u32[]{:S(2)}) collective-permute-start(bf16[3,2,250,128]{3,2,1,0:T(8,128)(2,1)S(1)} %get-tuple-element.17), channel_id=1, source_target_pairs={{0,8},{8,16},{16,24},{24,32},{32,40},{40,48},{48,56},{56,64},{64,7... | collective-permute-start | bytes 1152008 | tf_op jit(solution)/shard_map/ppermute | solution.py:578
  390.3 14.8 %collective-permute-start.9 = (bf16[3,2,250,128]{3,2,1,0:T(8,128)(2,1)S(1)}, bf16[3,2,250,128]{3,2,1,0:T(8,128)(2,1)S(1)}, u32[]{:S(2)}, u32[]{:S(2)}) collective-permute-start(bf16[3,2,250,128]{3,2,1,0:T(8,128)(2,1)S(1)} %get-tuple-element.16), channel_id=1, source_target_pairs={{8,0},{16,8},{24,16},{32,24},{40,32},{48,40},{56,48},{64,56},{72,6... | collective-permute-start | bytes 1152008 | tf_op jit(solution)/shard_map/ppermute | solution.py:579
  405.2 13.4 %copy-start.21 = (f32[250]{0:T(256)S(1)}, f32[250]{0:T(256)}, u32[]{:S(2)}) copy-start(f32[250]{0:T(256)} %param.51) | copy-start | bytes 3004
  406.9 12.6 %copy-start.6 = (bf16[1000,250]{1,0:T(8,128)(2,1)S(1)}, bf16[1000,250]{1,0:T(8,128)(2,1)}, u32[]{:S(2)}) copy-start(bf16[1000,250]{1,0:T(8,128)(2,1)} %param.54) | copy-start | bytes 1500004
  408.7 12.4 %collective-permute-start.11 = (bf16[10,2,250,3]{2,1,3,0:T(2,128)(2,1)S(1)}, bf16[10,2,250,3]{2,1,3,0:T(2,128)(2,1)S(1)}, u32[]{:S(2)}, u32[]{:S(2)}) collective-permute-start(bf16[10,2,250,3]{2,1,3,0:T(2,128)(2,1)S(1)} %copy.86), channel_id=1, source_target_pairs={{1,0},{2,1},{3,2},{4,3},{5,4},{6,5},{7,6},{9,8},{10,9},{11,10},{12... | collective-permute-start | bytes 90008 | tf_op jit(solution)/shard_map/ppermute | solution.py:579
  411.1 10.8 %collective-permute-start.10 = (bf16[10,2,250,3]{2,1,3,0:T(2,128)(2,1)}, bf16[10,2,250,3]{2,1,3,0:T(2,128)(2,1)}, u32[]{:S(2)}, u32[]{:S(2)}) collective-permute-start(bf16[10,2,250,3]{2,1,3,0:T(2,128)(2,1)} %copy.85), channel_id=1, source_target_pairs={{0,1},{1,2},{2,3},{3,4},{4,5},{5,6},{6,7},{8,9},{9,10},{10,11},{11... | collective-permute-start | bytes 90008 | tf_op jit(solution)/shard_map/ppermute | solution.py:578
  (15 other events, 93.5 us)

commit v2 on v1

--- a/solution.py
+++ b/solution.py
@@ -3,6 +3,8 @@
 
 import jax
 import jax.numpy as jnp
+import ml_dtypes
+import numpy as np
 from jax import lax
 from jax.experimental import pallas as pl
 from jax.experimental.pallas import tpu as pltpu
@@ -10,6 +12,7 @@
 
 F32 = jnp.float32
 BF16 = jnp.bfloat16
+MESH = pl.DeviceIdType.MESH
 VMEM_LIMIT = 56 * 1024 * 1024
 
 
@@ -30,28 +33,26 @@
     return pl.BlockSpec(shape, lambda *_: zeros)
 
 
-def fourier_tables(count):
-    column = jnp.arange(count, dtype=jnp.int32)
+def fourier_product(count):
+    column = np.arange(count)
     half = count // 2
-    wave = jnp.where(column <= half, column, column - half)
-    points = jnp.arange(count, dtype=jnp.int32)
-    phase = points[:, None] * wave[None, :] % count
-    angles = phase.astype(F32) * (2.0 * math.pi / count)
-    basis = jnp.where((column <= half)[None, :], jnp.cos(angles), jnp.sin(angles))
-    forward = (basis / count).astype(BF16)
-    factor = jnp.where((column == 0) | (column == half), 1.0, 2.0).astype(F32)
-    inverse = (basis.T * factor[:, None]).astype(BF16)
-    return (forward, inverse)
+    wave = np.where(column <= half, column, column - half)
+    angles = (column[:, None] * wave[None, :] % count) * (2.0 * math.pi / count)
+    basis = np.where((column <= half)[None, :], np.cos(angles), np.sin(angles))
+    forward = (basis / count).astype(ml_dtypes.bfloat16)
+    factor = np.where((column == 0) | (column == half), 1.0, 2.0)
+    inverse = (basis.T * factor[:, None]).astype(ml_dtypes.bfloat16)
+    product = forward.astype(np.float64) @ inverse.astype(np.float64)
+    return (product - np.eye(count)).astype(ml_dtypes.bfloat16)
 
 
 def cosine_tables(count):
-    degree = jnp.arange(count, dtype=jnp.int32)
-    points = jnp.arange(count, dtype=jnp.int32)
-    phase = degree[None, :] * (2 * points[:, None] + 1) % (4 * count)
-    basis = jnp.cos(phase.astype(F32) * (math.pi / (2 * count)))
-    forward = (basis / count).astype(BF16)
-    factor = jnp.where(degree == 0, 1.0, 2.0).astype(F32)
-    inverse = (basis.T * factor[:, None]).astype(BF16)
+    degree = np.arange(count)
+    phase = degree[None, :] * (2 * degree[:, None] + 1) % (4 * count)
+    basis = np.cos(phase * (math.pi / (2 * count)))
+    forward = (basis / count).astype(ml_dtypes.bfloat16)
+    factor = np.where(degree == 0, 1.0, 2.0)
+    inverse = (basis.T * factor[:, None]).astype(ml_dtypes.bfloat16)
     return (forward, inverse)
 
 
@@ -181,7 +182,17 @@
 
 
 def point_kernel(
-    mixed_ref, slope_ref, win_ref, wout_ref, pflux_ref, cells_ref, out_ref, picked_ref, wide, flux
+    mixed_ref,
+    slope_ref,
+    win_ref,
+    wout_ref,
+    pflux_ref,
+    cells_ref,
+    first_ref,
+    second_ref,
+    picked_ref,
+    wide,
+    flux,
 ):
     chans, pair, lanes = mixed_ref.shape
     rows = pair // 2
@@ -205,12 +216,11 @@
     hidden = mm(win_ref[...], value)
     gated = (jnp.concatenate([slope, slope], axis=1) * hidden).astype(BF16)
     update = mm(wout_ref[...], gated)
-    width = out_ref.shape[3]
-    for j in range(out_ref.shape[0]):
-        for p in range(2):
-            out_ref[j, p, 0] = update[
-                j * width : (j + 1) * width, p * lanes : (p + 1) * lanes
-            ].astype(BF16)
+    width = first_ref.shape[2]
+    for j in range(first_ref.shape[0]):
+        piece = update[j * width : (j + 1) * width].astype(BF16)
+        first_ref[j, 0] = piece[:, 0:lanes]
+        second_ref[j, 0] = piece[:, lanes : 2 * lanes]
     terms = update[chans : chans + 8]
     which = lax.broadcasted_iota(jnp.int32, (8, lanes), 0)
     flux[pl.ds(pl.multiple_of(step * 8, 8), 8), :] = jnp.where(
@@ -235,10 +245,9 @@
             picked_ref[r] = picked
 
 
-def pointwise(mixed, slope, win, wout, pflux, cells):
+def pointwise(mixed, slope, win, wout, pflux, cells, blocks):
     chans, pair, lanes = mixed.shape
     rows, hid, _ = slope.shape
-    blocks = pflux.shape[0]
     width = chans // blocks
     return pl.pallas_call(
         point_kernel,
@@ -252,11 +261,13 @@
             whole(cells.shape),
         ],
         out_specs=[
-            pl.BlockSpec((blocks, 2, 1, width, lanes), lambda i: (0, 0, i, 0, 0)),
+            pl.BlockSpec((blocks, 1, width, lanes), lambda i: (0, i, 0, 0)),
+            pl.BlockSpec((blocks, 1, width, lanes), lambda i: (0, i, 0, 0)),
             whole((cells.shape[0], 8, lanes)),
         ],
         out_shape=[
-            jax.ShapeDtypeStruct((blocks, 2, rows, width, lanes), BF16),
+            jax.ShapeDtypeStruct((blocks, rows, width, lanes), BF16),
+            jax.ShapeDtypeStruct((blocks, rows, width, lanes), BF16),
             jax.ShapeDtypeStruct((cells.shape[0], 8, lanes), F32),
         ],
         scratch_shapes=[
@@ -269,7 +280,8 @@
     )(mixed, slope, win, wout, pflux, cells)
 
 
-def add_kernel(probe_ref, update_ref, out_ref):
+def add_kernel(probe_ref, update_ref, *rest):
+    out_ref = rest[-1]
     for j in range(update_ref.shape[0]):
         cols = slice(j * 128, (j + 1) * 128)
         out_ref[:, :, cols] = (
@@ -277,79 +289,179 @@
         ).astype(BF16)
 
 
-def add_update(probe, update):
+def add_update(probe, update, p, partial=None):
     rows, chans, lons = probe.shape
-    blocks = update.shape[0]
+    blocks, count = update.shape[0], update.shape[1]
     step = 6
+    base = p * (count // step)
+    rest = () if partial is None else (partial,)
     return pl.pallas_call(
         add_kernel,
-        grid=(rows // step,),
+        grid=(count // step,),
         in_specs=[
-            pl.BlockSpec((step, chans, lons), lambda i: (i, 0, 0)),
+            pl.BlockSpec((step, chans, lons), lambda i: (base + i, 0, 0)),
             pl.BlockSpec((blocks, step, chans, 128), lambda i: (0, i, 0, 0)),
-        ],
-        out_specs=pl.BlockSpec((step, chans, lons), lambda i: (i, 0, 0)),
+        ]
+        + [pl.BlockSpec(memory_space=pl.ANY) for _ in rest],
+        out_specs=pl.BlockSpec((step, chans, lons), lambda i: (base + i, 0, 0)),
         out_shape=jax.ShapeDtypeStruct(probe.shape, BF16),
+        input_output_aliases={2: 0} if rest else {},
         compiler_params=params(),
-        cost_estimate=cost(probe.size, 6 * probe.size),
+        cost_estimate=cost(update.size, 6 * update.size),
         name="add_update",
-    )(probe, update)
-
-
-def depth_kernel(in_ref, kernel_ref, out_ref, wide):
-    high, _, chans, broad = in_ref.shape
-    rows = high - 6
-    cols = broad - 6
-    tiles = -(-chans // 8)
+    )(probe, update, *rest)
+
+
+def depth_sum(in_ref, p, first, taps_ref, wide, done):
+    high, _, broad, chans = in_ref.shape
+    rows, cols = done.shape[0], done.shape[1]
+    halves = wide.shape[0]
     for y in range(high):
-        wide[y, 0:chans, 0:broad] = in_ref[y, 0].astype(F32)
+        for h in range(halves):
+            lanes = min(128, chans - h * 128)
+            wide[h, y, 0:broad, 0:lanes] = in_ref[y, p, :, h * 128 : h * 128 + lanes].astype(F32)
 
     def tile(i, carry):
-        at = pl.ds(pl.multiple_of(i * 8, 8), 8)
-        weights = kernel_ref[at, :]
-        total = [jnp.zeros((8, cols), F32) for _ in range(rows)]
-        for b in range(7):
-            taps = [
-                jnp.broadcast_to(weights[:, 7 * a + b : 7 * a + b + 1], (8, cols))
-                for a in range(7)
-            ]
-            for y in range(high):
-                moved = wide[y, at, b : b + cols]
-                for a in range(7):
-                    if 0 <= y - a < rows:
-                        total[y - a] = total[y - a] + moved * taps[a]
-        for y in range(rows):
-            out_ref[y, at, :] = total[y]
+        at = pl.multiple_of(i * 8, 8)
+        for h in range(halves):
+            lanes = slice(h * 128, (h + 1) * 128)
+            total = [jnp.zeros((8, 128), F32) for _ in range(rows)]
+            for b in range(7):
+                taps = [taps_ref[(7 * a + b) * 8 : (7 * a + b + 1) * 8, lanes] for a in range(7)]
+                for y in range(high):
+                    moved = wide[h, y, pl.ds(at + (first + b), 8), :]
+                    for a in range(7):
+                        if 0 <= y - a < rows:
+                            total[y - a] = total[y - a] + moved * taps[a]
+            for y in range(rows):
+                done[y, pl.ds(at, 8), lanes] = total[y]
         return carry
 
-    lax.fori_loop(0, tiles, tile, 0)
+    lax.fori_loop(0, cols // 8, tile, 0)
+
+
+def depth_kernel(in_ref, taps_ref, out_ref, wide, done):
+    depth_sum(in_ref, 0, 0, taps_ref, wide, done)
+    for y in range(done.shape[0]):
+        out_ref[y] = done[y].T[0 : in_ref.shape[3]]
+
+
+def tap_rows(kernel):
+    chans = kernel.shape[0]
+    full = -(-chans // 128) * 128
+    return jnp.repeat(jnp.pad(kernel.T, ((0, 0), (0, full - chans))), 8, axis=0)
 
 
 def depthwise(padded, kernel):
-    high, probes, chans, broad = padded.shape
+    high, probes, broad, chans = padded.shape
     rows, cols = high - 6, broad - 6
-    full = -(-chans // 8) * 8
-    kernel = jnp.pad(kernel, ((0, full - chans), (0, 0)))
+    halves = -(-chans // 128)
+    taps = tap_rows(kernel)
     return pl.pallas_call(
         depth_kernel,
         grid=(probes,),
         in_specs=[
-            pl.BlockSpec((high, 1, chans, broad), lambda p: (0, p, 0, 0)),
-            whole(kernel.shape),
-        ],
-        out_specs=pl.BlockSpec((rows, full, cols), lambda p: (0, 0, p)),
-        out_shape=jax.ShapeDtypeStruct((rows, full, probes * cols), F32),
-        scratch_shapes=[pltpu.VMEM((high, full, -(-broad // 128) * 128), F32)],
+            pl.BlockSpec((high, 1, broad, chans), lambda p: (0, p, 0, 0)),
+            whole(taps.shape),
+        ],
+        out_specs=pl.BlockSpec((rows, chans, cols), lambda p: (0, 0, p)),
+        out_shape=jax.ShapeDtypeStruct((rows, chans, probes * cols), F32),
+        scratch_shapes=[
+            pltpu.VMEM((halves, high, -(-broad // 8) * 8, 128), F32),
+            pltpu.VMEM((rows, cols, halves * 128), F32),
+        ],
         compiler_params=params(),
         cost_estimate=cost(200 * rows * cols * chans * probes, 4 * padded.size),
         name="depthwise",
-    )(padded, kernel)
-
-
-def combine_kernel(pool_ref, slots_ref, weights_ref, mask_ref, out_ref):
-    bands, fields, cap = pool_ref.shape
+    )(padded, taps)
+
+
+def greet(partners, more=()):
+    barrier = pltpu.get_barrier_semaphore()
+    for where in more:
+        pl.semaphore_signal(barrier, inc=1, device_id=where, device_id_type=MESH)
+    count = jnp.int32(len(more))
+    for there, where in partners:
+
+        @pl.when(there)
+        def _(where=where):
+            pl.semaphore_signal(barrier, inc=1, device_id=where, device_id_type=MESH)
+
+        count = count + there.astype(jnp.int32)
+    pl.semaphore_wait(barrier, count)
+
+
+def swap_edges(low, high, sems, before, after, low_to, high_to):
+    is_before, device_before = before
+    is_after, device_after = after
+
+    def to_before():
+        return pltpu.make_async_remote_copy(
+            low, low_to, sems.at[0], sems.at[1], device_id=device_before, device_id_type=MESH
+        )
+
+    def to_after():
+        return pltpu.make_async_remote_copy(
+            high, high_to, sems.at[2], sems.at[3], device_id=device_after, device_id_type=MESH
+        )
+
+    @pl.when(is_before)
+    def _():
+        to_before().start()
+
+    @pl.when(is_after)
+    def _():
+        to_after().start()
+
+    @pl.when(is_before)
+    def _():
+        to_before().wait_send()
+        to_after().wait_recv()
+
+    @pl.when(is_after)
+    def _():
+        to_after().wait_send()
+        to_before().wait_recv()
+
+
+def neighbours(bands, blocks):
+    band, block = lax.axis_index("lat"), lax.axis_index("chan")
+    return (
+        (band > 0, (jnp.maximum(band - 1, 0), block)),
+        (band < bands - 1, (jnp.minimum(band + 1, bands - 1), block)),
+        (block > 0, (band, jnp.maximum(block - 1, 0))),
+        (block < blocks - 1, (band, jnp.minimum(block + 1, blocks - 1))),
+    )
+
+
+def flux_kernel(
+    blocks, picked_ref, slots_ref, weights_ref, mask_ref, out_ref, pool_ref, tall, send, recv, edge
+):
+    bands, fields, cap = picked_ref.shape
+    rows, cols = mask_ref.shape
+    band, block = lax.axis_index("lat"), lax.axis_index("chan")
+    lat_before, lat_after, chan_before, chan_after = neighbours(bands, blocks)
+    tall[...] = jnp.zeros_like(tall)
+    pool_ref[pl.ds(band, 1)] = picked_ref[pl.ds(band, 1)]
+    others = [(lax.rem(band + k, bands), block) for k in range(1, bands)]
+    greet((chan_before, chan_after), others)
+
+    copies = []
+    for k, where in enumerate(others):
+        copy = pltpu.make_async_remote_copy(
+            picked_ref.at[where[0]],
+            pool_ref.at[band],
+            send.at[k],
+            recv.at[k],
+            device_id=where,
+            device_id_type=MESH,
+        )
+        copy.start()
+        copies.append(copy)
+    for copy in copies:
+        copy.wait()
+
     pool = pool_ref[...].reshape(bands * fields, cap).astype(BF16)
-    rows, cols = mask_ref.shape
     place = lax.broadcasted_iota(jnp.int32, (cap, cols), 0)
     for y in range(rows):
         at = slice(y * cols, (y + 1) * cols)
@@ -357,27 +469,104 @@
         for k in range(slots_ref.shape[0]):
             slots = slots_ref[k : k + 1, at]
             weights = weights_ref[k : k + 1, at]
-            band = slots // cap
-            hot = jnp.where(place == slots - band * cap, 1.0, 0.0).astype(BF16)
+            source = slots // cap
+            hot = jnp.where(place == slots - source * cap, 1.0, 0.0).astype(BF16)
             found = mm(pool, hot)
             for b in range(bands):
                 total = total + found[b * fields : (b + 1) * fields] * jnp.where(
-                    band == b, weights, 0.0
+                    source == b, weights, 0.0
                 )
-        out_ref[y] = total * mask_ref[y : y + 1, :]
-
-
-def combine(pool, slots, weights, mask):
-    fields = pool.shape[1]
+        tall[3 + y, :, 128 : 128 + cols] = total * mask_ref[y : y + 1, :]
+
+    inner = pl.ds(128, cols)
+    swap_edges(
+        tall.at[pl.ds(3, 3), :, inner],
+        tall.at[pl.ds(rows, 3), :, inner],
+        edge.at[0],
+        lat_before,
+        lat_after,
+        tall.at[pl.ds(rows + 3, 3), :, inner],
+        tall.at[pl.ds(0, 3), :, inner],
+    )
+    swap_edges(
+        tall.at[:, :, pl.ds(128, 128)],
+        tall.at[:, :, pl.ds(cols, 128)],
+        edge.at[1],
+        chan_before,
+        chan_after,
+        tall.at[:, :, pl.ds(128 + cols, 128)],
+        tall.at[:, :, pl.ds(0, 128)],
+    )
+    out_ref[...] = tall[...]
+
+
+def flux_tile(picked, slots, weights, mask, blocks):
+    bands, fields, _ = picked.shape
     rows, cols = mask.shape
+    shape = (rows + 6, fields, cols + 256)
     return pl.pallas_call(
-        combine_kernel,
-        in_specs=[whole(a.shape) for a in (pool, slots, weights, mask)],
-        out_specs=whole((rows, fields, cols)),
-        out_shape=jax.ShapeDtypeStruct((rows, fields, cols), F32),
-        compiler_params=params(),
-        name="combine",
-    )(pool, slots, weights, mask)
+        functools.partial(flux_kernel, blocks),
+        in_specs=[whole(a.shape) for a in (picked, slots, weights, mask)],
+        out_specs=whole(shape),
+        out_shape=jax.ShapeDtypeStruct(shape, F32),
+        scratch_shapes=[
+            pltpu.VMEM(picked.shape, F32),
+            pltpu.VMEM(shape, F32),
+            pltpu.SemaphoreType.DMA((bands - 1,)),
+            pltpu.SemaphoreType.DMA((bands - 1,)),
+            pltpu.SemaphoreType.DMA((2, 4)),
+        ],
+        compiler_params=params(collective_id=1, has_side_effects=True),
+        name="flux_tile",
+    )(picked, slots, weights, mask)
+
+
+def edge_kernel(bands, blocks, field_ref, out_ref, tall, edge, own):
+    lines, _, cols, _ = field_ref.shape
+    lat_before, lat_after, chan_before, chan_after = neighbours(bands, blocks)
+    tall[...] = jnp.zeros_like(tall)
+    greet((lat_before, lat_after, chan_before, chan_after))
+    inner = pl.ds(16, cols)
+    copy = pltpu.make_async_copy(field_ref, tall.at[pl.ds(3, lines), :, inner, :], own)
+    copy.start()
+    swap_edges(
+        field_ref.at[pl.ds(0, 3)],
+        field_ref.at[pl.ds(lines - 3, 3)],
+        edge.at[0],
+        lat_before,
+        lat_after,
+        tall.at[pl.ds(lines + 3, 3), :, inner, :],
+        tall.at[pl.ds(0, 3), :, inner, :],
+    )
+    copy.wait()
+    swap_edges(
+        tall.at[:, :, pl.ds(16, 16), :],
+        tall.at[:, :, pl.ds(cols, 16), :],
+        edge.at[1],
+        chan_before,
+        chan_after,
+        tall.at[:, :, pl.ds(16 + cols, 16), :],
+        tall.at[:, :, pl.ds(0, 16), :],
+    )
+    out_ref[...] = tall[...]
+
+
+def coarse_edges(field, bands, blocks):
+    lines, probes, cols, chans = field.shape
+    shape = (lines + 6, probes, cols + 32, chans)
+    return pl.pallas_call(
+        functools.partial(edge_kernel, bands, blocks),
+        in_specs=[whole(field.shape)],
+        out_specs=whole(shape),
+        out_shape=jax.ShapeDtypeStruct(shape, BF16),
+        scratch_shapes=[
+            pltpu.VMEM(shape, BF16),
+            pltpu.SemaphoreType.DMA((2, 4)),
+            pltpu.SemaphoreType.DMA,
+        ],
+        compiler_params=params(collective_id=2, has_side_effects=True),
+        name="coarse_edges",
+    )(field)
 
 
 def normed_step(spread, base, sigma, gain):
@@ -393,8 +582,6 @@
     spread_ref,
     probe_ref,
     flux_ref,
-    left_ref,
-    right_ref,
     mask_ref,
     sigma_ref,
     base_ref,
@@ -406,19 +593,21 @@
     shrink_ref,
     pool_ref,
     down_ref,
+    turn_ref,
     one_ref,
     coarse_ref,
+    turned_ref,
     columns,
     held,
 ):
     step = pl.program_id(0)
     high = flux_ref.shape[0]
-    cols = flux_ref.shape[2]
+    cols = flux_ref.shape[2] - 256
 
     @pl.when(step == 0)
     def _():
         for y in range(high):
-            row = jnp.concatenate([left_ref[y], flux_ref[y], right_ref[y]], axis=1)
+            row = flux_ref[y]
             for b in range(7):
                 columns[(y * 7 + b) * 8 : (y * 7 + b + 1) * 8, :] = row[:, 125 + b : 125 + b + cols]
 
@@ -443,13 +632,15 @@
 
     @pl.when(step % 2 == 1)
     def _():
-        coarse = mm(down_ref[...], (held[...] + pooled).astype(BF16)).astype(BF16)
-        half = coarse.shape[1] // 2
-        coarse_ref[0, 0] = coarse[:, 0:half]
-        coarse_ref[0, 1] = coarse[:, half : 2 * half]
-
-
-def fine_level(spread, probe, flux, left, right, mask, sigma, base, slope, gain, mix, couple, expand, shrink, pool, down):
+        both = (held[...] + pooled).astype(BF16)
+        coarse_ref[0] = mm(down_ref[...], both).astype(BF16)
+        turned = mm(both.T, turn_ref[...]).astype(BF16)
+        half = turned.shape[0] // 2
+        turned_ref[0, 0] = turned[0:half]
+        turned_ref[0, 1] = turned[half : 2 * half]
+
+
+def fine_level(spread, probe, flux, mask, sigma, base, slope, gain, mix, couple, expand, shrink, pool, down, turn):
     rows, chans, wide = spread.shape
     cols = wide // 2
     coarse = down.shape[0]
@@ -461,8 +652,6 @@
             pl.BlockSpec((1, chans, wide), row),
             pl.BlockSpec((1, chans, wide), row),
             whole(flux.shape),
-            whole(left.shape),
-            whole(right.shape),
             whole(mask.shape),
             whole(sigma.shape),
             pl.BlockSpec((1, chans, cols), row),
@@ -474,14 +663,17 @@
             whole(shrink.shape),
             whole(pool.shape),
             whole(down.shape),
+            whole(turn.shape),
         ],
         out_specs=[
             pl.BlockSpec((1, chans, wide), row),
-            pl.BlockSpec((1, 2, coarse, cols // 2), lambda i: (i // 2, 0, 0, 0)),
+            pl.BlockSpec((1, coarse, cols), lambda i: (i // 2, 0, 0)),
+            pl.BlockSpec((1, 2, cols // 2, turn.shape[1]), lambda i: (i // 2, 0, 0, 0)),
         ],
         out_shape=[
             jax.ShapeDtypeStruct((rows, chans, wide), BF16),
-            jax.ShapeDtypeStruct((rows // 2, 2, coarse, cols // 2), BF16),
+            jax.ShapeDtypeStruct((rows // 2, coarse, cols), BF16),
+            jax.ShapeDtypeStruct((rows // 2, 2, cols // 2, turn.shape[1]), BF16),
         ],
         scratch_shapes=[
             pltpu.VMEM((flux.shape[0] * 56, cols), F32),
@@ -489,11 +681,12 @@
         ],
         compiler_params=params(),
         name="fine_level",
-    )(spread, probe, flux, left, right, mask, sigma, base, slope, gain, mix, couple, expand, shrink, pool, down)
+    )(spread, probe, flux, mask, sigma, base, slope, gain, mix, couple, expand, shrink, pool, down, turn)
 
 
 def coarse_kernel(
-    spread_ref,
+    around_ref,
+    taps_ref,
     field_ref,
     sigma_ref,
     base_ref,
@@ -507,19 +700,30 @@
     mask_ref,
     out_ref,
     wide,
+    tall,
+    done,
+    spread,
 ):
     step = pl.program_id(0)
-    chans = field_ref.shape[2]
+    chans = field_ref.shape[1]
     probes, fine, rows, cols = out_ref.shape
-    field = jnp.concatenate([field_ref[0, 0], field_ref[0, 1]], axis=1).astype(F32)
+
+    @pl.when(step == 0)
+    def _():
+        half = done.shape[1]
+        for p in range(probes):
+            depth_sum(around_ref, p, 13, taps_ref, tall, done)
+            for y in range(done.shape[0]):
+                spread[y, :, p * half : (p + 1) * half] = done[y].T[0:chans]
+
     at = pl.ds(step, 1)
     tangent = normed_step(
-        spread_ref[0, 0:chans], base_ref[0].astype(F32), sigma_ref[at, :], gain_ref[...]
+        spread[step], base_ref[0].astype(F32), sigma_ref[at, :], gain_ref[...]
     )
     slope = slope_ref[0].astype(F32)
     hidden = mm(expand_ref[...], tangent)
     gated = (hidden * jnp.concatenate([slope, slope], axis=1)).astype(BF16)
-    two = (field + mm(shrink_ref[...], gated)).astype(BF16)
+    two = (field_ref[0].astype(F32) + mm(shrink_ref[...], gated)).astype(BF16)
     raised = mm(up_ref[...], mm(two, spreadout_ref[...]).astype(BF16))
     for half in range(2):
         y = step * 2 + half
@@ -540,17 +744,22 @@
                 )
 
 
-def coarse_level(spread, field, sigma, base, slope, gain, expand, shrink, spreadout, up, one, mask):
-    lines, probes, chans, half = field.shape
+def coarse_level(
+    around, kernel, field, sigma, base, slope, gain, expand, shrink, spreadout, up, one, mask
+):
+    lines, chans, double = field.shape
+    half = double // 2
     rows, fine, wide = one.shape
     cols = wide // 2
+    taps = tap_rows(kernel)
     row = lambda i: (i, 0, 0)
     return pl.pallas_call(
         coarse_kernel,
         grid=(lines,),
         in_specs=[
-            pl.BlockSpec((1,) + spread.shape[1:], row),
-            pl.BlockSpec((1, probes, chans, half), lambda i: (i, 0, 0, 0)),
+            whole(around.shape),
+            whole(taps.shape),
+            pl.BlockSpec((1, chans, double), row),
             whole(sigma.shape),
             pl.BlockSpec((1, chans, half), row),
             pl.BlockSpec((1, slope.shape[1], half), row),
@@ -562,12 +771,18 @@
             pl.BlockSpec((2, fine, wide), row),
             whole(mask.shape),
         ],
-        out_specs=whole((probes, fine, rows, cols)),
-        out_shape=jax.ShapeDtypeStruct((probes, fine, rows, cols), BF16),
-        scratch_shapes=[pltpu.VMEM((probes, cols // 128, fine * rows, 128), F32)],
+        out_specs=whole((2, fine, rows, cols)),
+        out_shape=jax.ShapeDtypeStruct((2, fine, rows, cols), BF16),
+        scratch_shapes=[
+            pltpu.VMEM((2, cols // 128, fine * rows, 128), F32),
+            pltpu.VMEM((taps.shape[1] // 128, around.shape[0], around.shape[2], 128), F32),
+            pltpu.VMEM((lines, half, taps.shape[1]), F32),
+            pltpu.VMEM((lines, chans, double), F32),
+        ],
         compiler_params=params(),
+        cost_estimate=cost(1e9, 4e6),
         name="coarse_level",
-    )(spread, field, sigma, base, slope, gain, expand, shrink, spreadout, up, one, mask)
+    )(around, taps, field, sigma, base, slope, gain, expand, shrink, spreadout, up, one, mask)
 
 
 def shifted(block, axis):
@@ -643,44 +858,15 @@
         ],
         axis=0,
     )
-    probe_terms = lax.all_to_all(
-        probe_flux(probe_field, flux_pair), "chan", split_axis=0, concat_axis=0, tiled=True
-    )
-
-    fwd_lon, inv_lon = fourier_tables(lons)
-    fwd_lat, inv_lat = cosine_tables(lats)
-    diff = (mm(fwd_lon, inv_lon) - jnp.eye(lons, dtype=F32)).astype(BF16)
-    filt = lax.dynamic_slice_in_dim(
-        spectral_filter, lax.axis_index("lat") * part, part, 1
-    ).T.reshape(part, lats, 1)
-    mixed = lat_filter(gathered, fwd_lat.T, inv_lat.T, filt, diff)
-    regrouped = lax.all_to_all(
-        mixed.reshape(bands * blocks, part, pair, 128),
-        ("lat", "chan"),
-        split_axis=0,
-        concat_axis=0,
-        tiled=True,
-    ).reshape(chans, pair, 128)
-
-    win = (
-        weight_in.reshape(blocks, bands, part, -1).transpose(1, 0, 2, 3).reshape(chans, -1).T
-    )
-    folded = mm(weight_out, weight_flux).astype(BF16)
-    wout = jnp.concatenate([weight_out, folded, folded], axis=1).T
-    update, picked = pointwise(
-        regrouped, gate_slope, win, wout, probe_terms, send_cells[0]
-    )
-    update_back = lax.all_to_all(update, "chan", split_axis=0, concat_axis=0, tiled=True)
-    atmos_out = add_update(flat_probe, update_back.reshape(blocks, pair, width, 128)).reshape(
-        probe_field.shape
+    probe_terms = lax.psum_scatter(
+        probe_flux(probe_field, flux_pair), "chan", scatter_dimension=0, tiled=True
     )
 
     tile_rows, tile_cols = ocean_mask.shape
     fine = ocean_probe.shape[1]
     mask = ocean_mask.astype(F32)
     masked = ocean_probe * ocean_mask.astype(BF16)
-    padded = with_halo(masked, (("lat", 2), ("chan", 3)), 3).transpose(2, 0, 1, 3)
-    spread = depthwise(padded, kernel_fine)
+    padded = with_halo(masked, (("lat", 2), ("chan", 3)), 3).transpose(2, 0, 3, 1)
     start = masked.transpose(2, 1, 0, 3).reshape(tile_rows, fine, probes * tile_cols)
     base_rows = base_fine.transpose(1, 0, 2)
     slope_rows = slope_fine.transpose(1, 0, 2)
@@ -701,19 +887,73 @@
     pool = jnp.where(meets, 0.25, 0.0).astype(BF16)
     spreadout = jnp.where(meets.T, 1.0, 0.0).astype(BF16)
 
-    arrived = lax.all_to_all(picked, "lat", split_axis=0, concat_axis=0, tiled=True)
-    flux = combine(arrived, recv_slots[0], recv_weights[0], mask)
-    up, down = shifted(flux, "lat")
-    tall = jnp.concatenate([up(flux[tile_rows - 3 :]), flux, down(flux[:3])], axis=0)
-    up, down = shifted(flux, "chan")
-    left = up(tall[:, :, tile_cols - 128 :])
-    right = down(tall[:, :, :128])
-    one, coarse = fine_level(
+    fwd_lat, inv_lat = cosine_tables(lats)
+    diff = jnp.asarray(fourier_product(lons))
+    filt = lax.dynamic_slice_in_dim(
+        spectral_filter, lax.axis_index("lat") * part, part, 1
+    ).T.reshape(part, lats, 1)
+    gathered, padded, start, filt, probe_terms = lax.optimization_barrier(
+        (gathered, padded, start, filt, probe_terms)
+    )
+    mixed = lat_filter(gathered, jnp.asarray(fwd_lat.T), jnp.asarray(inv_lat.T), filt, diff)
+    regrouped = lax.all_to_all(
+        mixed.reshape(bands * blocks, part, pair, 128),
+        ("lat", "chan"),
+        split_axis=0,
+        concat_axis=0,
+        tiled=True,
+    ).reshape(chans, pair, 128)
+
+    win = (
+        weight_in.reshape(blocks, bands, part, -1).transpose(1, 0, 2, 3).reshape(chans, -1).T
+    )
+    folded = mm(weight_out, weight_flux).astype(BF16)
+    wout = jnp.concatenate([weight_out, folded, folded], axis=1).T
+    spread = depthwise(padded, kernel_fine)
+    (
+        regrouped,
+        spread,
+        win,
+        wout,
+        probe_terms,
+        base_rows,
+        slope_rows,
+        base_lines,
+        slope_lines,
+        mix,
+        couple,
+        pool,
+        spreadout,
+        mask,
+    ) = lax.optimization_barrier(
+        (
+            regrouped,
+            spread,
+            win,
+            wout,
+            probe_terms,
+            base_rows,
+            slope_rows,
+            base_lines,
+            slope_lines,
+            mix,
+            couple,
+            pool,
+            spreadout,
+            mask,
+        )
+    )
+    first, second, picked = pointwise(
+        regrouped, gate_slope, win, wout, probe_terms, send_cells[0], blocks
+    )
+
+    tall = flux_tile(picked, recv_slots[0], recv_weights[0], mask, blocks)
+    first, tall = lax.optimization_barrier((first, tall))
+    first = lax.all_to_all(first, "chan", split_axis=0, concat_axis=0, tiled=True)
+    one, coarse, turned = fine_level(
         spread,
         start,
         tall,
-        left,
-        right,
         mask,
         sigma_fine,
         base_rows,
@@ -725,11 +965,14 @@
         shrink_fine.T,
         pool,
         down_proj.T,
-    )
-    coarse_padded = with_halo(coarse, (("lat", 0), ("chan", 3)), 3)
-    coarse_spread = depthwise(coarse_padded, kernel_coarse)
+        jnp.pad(down_proj, ((0, 0), (0, 256 - down_proj.shape[1]))),
+    )
+    around = coarse_edges(turned, bands, blocks)
+    second, around = lax.optimization_barrier((second, around))
+    second = lax.all_to_all(second, "chan", split_axis=0, concat_axis=0, tiled=True)
     ocean_out = coarse_level(
-        coarse_spread,
+        around,
+        kernel_coarse,
         coarse,
         sigma_coarse,
         base_lines,
@@ -742,6 +985,8 @@
         one,
         mask,
     )
+    partial = add_update(flat_probe, first, 0)
+    atmos_out = add_update(flat_probe, second, 1, partial).reshape(probe_field.shape)
     return (atmos_out, ocean_out)
 
 

time: 507 us -> 346 us (0.68)
  Pallas kernels: 231 us -> 154 us
  starting transfers between devices: 83.3 us -> 46.2 us
  other arithmetic: 46.2 us -> 11.6 us
  matrix products: 21.1 us -> 0.26 us
  local copies, waits for them, and re-layouts: 57.6 us -> 37.7 us
  waiting for transfers between devices: 61.2 us -> 79.1 us
  between operations: 1 us -> 14.4 us
    pallas_call x2 -> x1, Pallas kernels: 138 us -> 23 us  [depthwise(): pl.pallas_call(depth_kernel, grid=(probes,), in_specs=[pl.BlockSpec((high...]
    ppermute x6 -> x2, waiting for transfers between devices: 7.88 us -> 51.6 us  [shifted(): lax.ppermute(low, axis, forward)]
    pallas_call x3 -> x5, Pallas kernels: 18.8 us -> 57.3 us  [the longest x1 17.5 us: coarse_edges(): pl.pallas_call(functools.partial(edge_kernel, bands, blocks), in_specs=[w...]
    ppermute x6 -> x2, starting transfers between devices: 33 us -> 4.65 us  [shifted(): lax.ppermute(low, axis, forward)]
    dot_general x2 -> x1, matrix products: 21.1 us -> 0.26 us  [mm(): return jnp.dot(a, b, preferred_element_type=F32)]
    all_to_all x1, waiting for transfers between devices: 32.8 us -> 13.7 us  [local(): lax.all_to_all(mixed.reshape(bands * blocks, part, pair, 128), ('lat', 'c...]
    dot_general x1 -> x0, other arithmetic: 18.5 us -> none  [mm(): return jnp.dot(a, b, preferred_element_type=F32)]
    all_to_all x1, waiting for transfers between devices: 18.2 us -> 0.01 us  [local(): lax.all_to_all(turned, 'lat', split_axis=0, concat_axis=0, tiled=True)]
  transfers between devices with their start and end apart: 17 -> 9, of which waited for: 5 -> 5; matrix products, arithmetic and copies ran while one was open for 25% -> 14% of each run, Pallas kernels for 43% -> 23%
where the time goes in v2:
time: 346 us; the launch traced here: 344 us
  Pallas kernels  154 us (45%)
  waiting for transfers between devices  79.1 us (23%)
  starting transfers between devices  46.2 us (13%)
  local copies, waits for them, and re-layouts  37.7 us (11%)
  between operations  14.4 us (4%)
  other arithmetic  11.6 us (3%)
    ppermute x2, waiting for transfers between devices, shifted(): lax.ppermute(low, axis, forward)  51.6 us
    pallas_call x1, Pallas kernels, pointwise(): pl.pallas_call(point_kernel, grid=(rows,), in_specs=[whole(mixed.shape),...  27.9 us
    pallas_call x1, Pallas kernels, depthwise(): pl.pallas_call(depth_kernel, grid=(probes,), in_specs=[pl.BlockSpec((high...  23 us
    pallas_call x1, Pallas kernels, lat_filter(): pl.pallas_call(filter_kernel, grid=(chans,), in_specs=[pl.BlockSpec((band...  18.8 us
    pallas_call x1, Pallas kernels, coarse_edges(): pl.pallas_call(functools.partial(edge_kernel, bands, blocks), in_specs=[w...  17.5 us
    all_to_all x1, starting transfers between devices, local(): lax.all_to_all(mixed.reshape(bands * blocks, part, pair, 128), ('lat', 'c...  16.9 us
    pallas_call x1, Pallas kernels, flux_tile(): pl.pallas_call(functools.partial(flux_kernel, blocks), in_specs=[whole(a....  15.8 us
    pallas_call x1, Pallas kernels, coarse_level(): pl.pallas_call(coarse_kernel, grid=(lines,), in_specs=[whole(around.shape...  14.8 us
  transfers between devices with their start and end apart: 9, of which 5 were waited for; matrix products, arithmetic and copies ran while one was open for 14% of the time, Pallas kernels for 23%

profile of v2, /device:TPU:32, one launch (start us, length us, event | category | flops | bytes accessed | tf_op | source)
XLA Modules:
  0.0 343.7 jit_solution(3749509485154705479)
XLA Ops:
  7.2 8.2 %turn_channels.1 = bf16[48,48,1024]{2,1,0:T(8,128)(2,1)} custom-call(bf16[48,48,1024]{2,1,0:T(8,128)(2,1)} %bitcast.60), custom_call_target="tpu_custom_call" | custom-call | bytes 9437184 | tf_op jit(solution)/shard_map/turn_channels/pallas_call | solution.py:68
  15.3 8.0 %all-to-all-start = ((bf16[16,3,48,1024]{3,2,1,0:T(8,128)(2,1)}), bf16[16,3,48,1024]{3,2,1,0:T(8,128)(2,1)}, u32[]{:S(2)}, u32[]{:S(2)}) async-start(bf16[16,3,48,1024]{3,2,1,0:T(8,128)(2,1)} %bitcast.64), calls=%async_computation | async-start | bytes 9437184 | tf_op jit(solution)/shard_map/all_to_all | solution.py:848
  23.4 2.7 copy.66
  31.9 3.4 collective-permute-start
  36.3 4.6 %collective-permute-start.1 = (bf16[2,200,3,256]{3,1,2,0:T(8,128)(2,1)}, bf16[2,200,3,256]{3,1,2,0:T(8,128)(2,1)}, u32[]{:S(2)}, u32[]{:S(2)}) collective-permute-start(bf16[2,200,3,256]{3,1,2,0:T(8,128)(2,1)} %copy.68), channel_id=1, source_target_pairs={{8,0},{16,8},{24,16},{32,24},{40,32},{48,40},{56,48},{64,56},{72,6... | collective-permute-start | bytes 1843208 | tf_op jit(solution)/shard_map/ppermute | solution.py:794
  41.7 5.5 %probe_flux.1 = bf16[8,192,128]{2,1,0:T(8,128)(2,1)} custom-call(bf16[2,24,48,1024]{3,2,1,0:T(8,128)(2,1)} %probe_ref.1, bf16[8,96]{1,0:T(8,128)(2,1)} %fusion.2.weight_ref), custom_call_target="tpu_custom_call" | custom-call | flops 37748736 | bytes 4718592 | tf_op jit(solution)/shard_map/probe_flux/pallas_call | solution.py:98
  47.2 51.6 %collective-permute-done = bf16[2,200,3,256]{3,1,2,0:T(8,128)(2,1)} collective-permute-done((bf16[2,200,3,256]{3,1,2,0:T(8,128)(2,1)}, bf16[2,200,3,256]{3,1,2,0:T(8,128)(2,1)}, u32[]{:S(2)}, u32[]{:S(2)}) %collective-permute-start) | collective-permute-done | bytes 614432 | tf_op jit(solution)/shard_map/ppermute | solution.py:793
  100.1 4.3 %collective-permute-done.1 = bf16[2,200,3,256]{3,1,2,0:T(8,128)(2,1)} collective-permute-done((bf16[2,200,3,256]{3,1,2,0:T(8,128)(2,1)}, bf16[2,200,3,256]{3,1,2,0:T(8,128)(2,1)}, u32[]{:S(2)}, u32[]{:S(2)}) %collective-permute-start.1) | collective-permute-done | bytes 614432 | tf_op jit(solution)/shard_map/ppermute | solution.py:794
  113.7 4.2 %maximum_bitcast_fusion.in_ref = bf16[14,2,262,200]{3,2,1,0:T(8,128)(2,1)} fusion(bf16[2,200,14,3]{1,3,0,2:T(4,128)(2,1)S(1)} %collective-permute-done.3, bf16[2,200,3,256]{1,3,0,2:T(8,128)(2,1)} %copy.70, bf16[2,200,8,256]{1,3,0,2:T(8,128)(2,1)S(1)} %broadcast_multiply_fusion, bf16[2,200,3,256]{1,3,0,2:T(8,128)(2,1)S(1)} %copy.69, ...), kind=kLoop, calls=%fused_computation | loop fusion | flops 14672000 | bytes 5868800 | tf_op jit(solution)/shard_map/transpose | solution.py:869
  119.0 18.8 %lat_filter.1 = bf16[16,8,3,48,128]{4,3,2,1,0:T(8,128)(2,1)} custom-call(bf16[16,3,48,1024]{3,2,1,0:T(8,128)(2,1)} %all-to-all-done.in_ref, bf16[384,384]{1,0:T(8,128)(2,1)} %constant.50.clone.fwd_ref, bf16[384,384]{1,0:T(8,128)(2,1)} %constant.51.clone.inv_ref, f32[3,384,1]{2,1,0:T(8,128)} %copy.72.filt_ref, bf16[1024,1024]{1,0:T(8,128)(2,1)} %constant.49.clone.diff_ref), custom_call_target="tpu_custom_call" | custom-call | flops 8400000000 | bytes 9437184 | tf_op jit(solution)/shard_map/lat_filter/pallas_call | solution.py:165
  137.7 16.9 %all-to-all-start.1 = ((bf16[128,3,48,128]{3,2,1,0:T(8,128)(2,1)}), bf16[128,3,48,128]{3,2,1,0:T(8,128)(2,1)}, u32[]{:S(2)}, u32[]{:S(2)}) async-start(bf16[128,3,48,128]{3,2,1,0:T(8,128)(2,1)} %bitcast.67), calls=%async_computation.2 | async-start | bytes 9437184 | tf_op jit(solution)/shard_map/all_to_all | solution.py:899
  155.6 2.7 copy.81
  175.6 23.0 %depthwise.1.spread_ref = f32[8,200,512]{2,1,0:T(8,128)} custom-call(bf16[14,2,262,200]{3,2,1,0:T(8,128)(2,1)} %maximum_bitcast_fusion.in_ref, f32[392,256]{1,0:T(8,128)} %broadcast_bitcast_fusion.3.taps_ref), custom_call_target="tpu_custom_call" | custom-call | flops 163840000 | bytes 5868800 | tf_op jit(solution)/shard_map/depthwise/pallas_call | solution.py:360
  198.6 13.7 %all-to-all-done.1 = bf16[128,3,48,128]{3,2,1,0:T(8,128)(2,1)} async-done(((bf16[128,3,48,128]{3,2,1,0:T(8,128)(2,1)}), bf16[128,3,48,128]{3,2,1,0:T(8,128)(2,1)}, u32[]{:S(2)}, u32[]{:S(2)}) %all-to-all-start.1) | async-done | bytes 4718624 | tf_op jit(solution)/shard_map/all_to_all | solution.py:899
  212.3 27.9 %pointwise.1 = (bf16[8,24,48,128]{3,2,1,0:T(8,128)(2,1)}, bf16[8,24,48,128]{3,2,1,0:T(8,128)(2,1)}, f32[16,8,128]{2,1,0:T(8,128)}) custom-call(bf16[384,48,128]{2,1,0:T(8,128)(2,1)} %bitcast.9.mixed_ref, bf16[24,768,128]{2,1,0:T(8,128)(2,1)} %slope_ref.1, bf16[768,384]{1,0:T(8,128)(2,1)} %bitcast.74, bf16[392,768]{1,0:T(8,128)(2,1)} %maximum_bitcast_fusion.1.wout_ref, ...), custom_call_target="tpu_custom_call" | custom-call | flops 7299999744 | bytes 14155776 | tf_op jit(solution)/shard_map/pointwise/pallas_call | solution.py:252
  240.2 15.8 %flux_tile.1.flux_ref = f32[14,8,512]{2,1,0:T(8,128)} custom-call(f32[16,8,128]{2,1,0:T(8,128)} %get-tuple-element.43.picked_ref, s32[4,2048]{1,0:T(4,128)} %bitcast.81, f32[4,2048]{1,0:T(4,128)} %bitcast.82, f32[8,256]{1,0:T(8,128)} %get-tuple-element.44.mask_ref), custom_call_target="tpu_custom_call" | custom-call | tf_op jit(solution)/shard_map/flux_tile/pallas_call | solution.py:507
  256.0 3.6 %all-to-all-start.3 = ((bf16[8,24,48,128]{3,2,1,0:T(8,128)(2,1)}), bf16[8,24,48,128]{3,2,1,0:T(8,128)(2,1)S(1)}, u32[]{:S(2)}, u32[]{:S(2)}) async-start(bf16[8,24,48,128]{3,2,1,0:T(8,128)(2,1)} %get-tuple-element.53), calls=%async_computation.4 | async-start | bytes 4718592 | tf_op jit(solution)/shard_map/all_to_all | solution.py:952
  263.6 13.9 %fine_level.1 = (bf16[8,200,512]{2,1,0:T(8,128)(2,1)}, bf16[4,250,256]{2,1,0:T(8,128)(2,1)}, bf16[4,2,128,256]{3,2,1,0:T(8,128)(2,1)}) custom-call(f32[8,200,512]{2,1,0:T(8,128)} %depthwise.1.spread_ref, bf16[8,200,512]{2,1,0:T(8,128)(2,1)} %copy.88.probe_ref, f32[14,8,512]{2,1,0:T(8,128)} %flux_tile.1.flux_ref, f32[8,256]{1,0:T(8,128)} %get-tuple-element.44.mask_ref, ...), custom_call_target="tpu_custom_call" | custom-call | tf_op jit(solution)/shard_map/fine_level/pallas_call | solution.py:648
  277.5 17.5 %coarse_edges.1.around_ref = bf16[10,2,160,256]{3,2,1,0:T(8,128)(2,1)} custom-call(bf16[4,2,128,256]{3,2,1,0:T(8,128)(2,1)} %get-tuple-element.51.field_ref), custom_call_target="tpu_custom_call" | custom-call | tf_op jit(solution)/shard_map/coarse_edges/pallas_call | solution.py:557
  295.1 7.1 %all-to-all-start.2 = ((bf16[8,24,48,128]{3,2,1,0:T(8,128)(2,1)}), bf16[8,24,48,128]{3,2,1,0:T(8,128)(2,1)}, u32[]{:S(2)}, u32[]{:S(2)}) async-start(bf16[8,24,48,128]{3,2,1,0:T(8,128)(2,1)} %get-tuple-element.52), calls=%async_computation.3 | async-start | bytes 4718592 | tf_op jit(solution)/shard_map/all_to_all | solution.py:972
  304.8 14.8 %coarse_level.1 = bf16[2,200,8,256]{3,2,1,0:T(8,128)(2,1)} custom-call(bf16[10,2,160,256]{3,2,1,0:T(8,128)(2,1)} %coarse_edges.1.around_ref, f32[392,256]{1,0:T(8,128)} %broadcast_bitcast_fusion.1.taps_ref, bf16[4,250,256]{2,1,0:T(8,128)(2,1)} %get-tuple-element.55.field_ref, f32[4,128]{1,0:T(4,128)} %sigma_ref.3, bf16[4,250,128]{2,1,0:T(8,128)(2,1)} %bitcast.73, ...), custom_call_target="tpu_custom_call" | custom-call | flops 1000000000 | bytes 4000000 | tf_op jit(solution)/shard_map/coarse_level/pallas_call | solution.py:756
  319.5 4.6 %add_update.2.rest_0_ = bf16[48,48,1024]{2,1,0:T(8,128)(2,1)} custom-call(bf16[48,48,1024]{2,1,0:T(8,128)(2,1)} %bitcast.61, bf16[8,24,48,128]{3,2,1,0:T(8,128)(2,1)} %copy-done.2), custom_call_target="tpu_custom_call" | custom-call | flops 1179648 | bytes 7077888 | tf_op jit(solution)/shard_map/add_update/pallas_call | solution.py:298
  324.1 8.2 %all-to-all-done.2.update_ref = bf16[8,24,48,128]{3,2,1,0:T(8,128)(2,1)} async-done(((bf16[8,24,48,128]{3,2,1,0:T(8,128)(2,1)}), bf16[8,24,48,128]{3,2,1,0:T(8,128)(2,1)}, u32[]{:S(2)}, u32[]{:S(2)}) %all-to-all-start.2) | async-done | bytes 2359328 | tf_op jit(solution)/shard_map/all_to_all | solution.py:972
  332.3 4.6 %add_update.3 = bf16[48,48,1024]{2,1,0:T(8,128)(2,1)} custom-call(bf16[48,48,1024]{2,1,0:T(8,128)(2,1)} %bitcast.62, bf16[8,24,48,128]{3,2,1,0:T(8,128)(2,1)} %all-to-all-done.2.update_ref, bf16[48,48,1024]{2,1,0:T(8,128)(2,1)} %add_update.2.rest_0_), custom_call_target="tpu_custom_call", output_to_operand_aliasing={{}: (2, {})} | custom-call | flops 1179648 | bytes 7077888 | tf_op jit(solution)/shard_map/add_update/pallas_call | solution.py:298
  (93 shorter events, 44.1 us)
Async XLA Ops:
  7.2 102.9 %copy-start = (f32[384,48]{0,1:T(8,128)S(1)}, f32[384,48]{0,1:T(8,128)}, u32[]{:S(2)}) copy-start(f32[384,48]{0,1:T(8,128)} %param.33) | copy-start | bytes 221188
  15.3 8.1 %copy-start.6 = (bf16[2,200,8,256]{3,2,1,0:T(8,128)(2,1)S(1)}, bf16[2,200,8,256]{3,2,1,0:T(8,128)(2,1)}, u32[]{:S(2)}) copy-start(bf16[2,200,8,256]{3,2,1,0:T(8,128)(2,1)} %param.40) | copy-start | bytes 4915204
  15.3 102.5 %all-to-all-start = ((bf16[16,3,48,1024]{3,2,1,0:T(8,128)(2,1)}), bf16[16,3,48,1024]{3,2,1,0:T(8,128)(2,1)}, u32[]{:S(2)}, u32[]{:S(2)}) async-start(bf16[16,3,48,1024]{3,2,1,0:T(8,128)(2,1)} %bitcast.64), calls=%async_computation | async-start | bytes 9437184 | tf_op jit(solution)/shard_map/all_to_all | solution.py:848
  23.4 94.5 %reduce-scatter.2.cloned.1.call-start = ((), (), s32[]{:S(2)}) async-start(), calls=%async_computation.5 | async-start | bytes 442368 | tf_op jit(solution)/shard_map/reduce_scatter | solution.py:861
  28.6 12.3 %copy-start.16 = (bf16[384,4]{0,1:T(4,128)(2,1)S(1)}, bf16[384,4]{0,1:T(4,128)(2,1)}, u32[]{:S(2)}) copy-start(bf16[384,4]{0,1:T(4,128)(2,1)} %param.36) | copy-start | bytes 9220
  31.9 66.9 %collective-permute-start = (bf16[2,200,3,256]{3,1,2,0:T(8,128)(2,1)}, bf16[2,200,3,256]{3,1,2,0:T(8,128)(2,1)}, u32[]{:S(2)}, u32[]{:S(2)}) collective-permute-start(bf16[2,200,3,256]{3,1,2,0:T(8,128)(2,1)} %copy.67), channel_id=1, source_target_pairs={{0,8},{8,16},{16,24},{24,32},{32,40},{40,48},{48,56},{56,64},{64,7... | collective-permute-start | bytes 1843208 | tf_op jit(solution)/shard_map/ppermute | solution.py:793
  36.3 68.0 %collective-permute-start.1 = (bf16[2,200,3,256]{3,1,2,0:T(8,128)(2,1)}, bf16[2,200,3,256]{3,1,2,0:T(8,128)(2,1)}, u32[]{:S(2)}, u32[]{:S(2)}) collective-permute-start(bf16[2,200,3,256]{3,1,2,0:T(8,128)(2,1)} %copy.68), channel_id=1, source_target_pairs={{8,0},{16,8},{24,16},{32,24},{40,32},{48,40},{56,48},{64,56},{72,6... | collective-permute-start | bytes 1843208 | tf_op jit(solution)/shard_map/ppermute | solution.py:794
  107.4 4.9 %collective-permute-start.2 = (bf16[2,200,14,3]{1,3,0,2:T(4,128)(2,1)S(1)}, bf16[2,200,14,3]{1,3,0,2:T(4,128)(2,1)S(1)}, u32[]{:S(2)}, u32[]{:S(2)}) collective-permute-start(bf16[2,200,14,3]{1,3,0,2:T(4,128)(2,1)S(1)} %get-tuple-element.60), channel_id=1, source_target_pairs={{0,1},{1,2},{2,3},{3,4},{4,5},{5,6},{6,7},{8,9},{9,10},{10,11},{11... | collective-permute-start | bytes 100808 | tf_op jit(solution)/shard_map/ppermute | solution.py:793
  108.7 4.9 %collective-permute-start.3 = (bf16[2,200,14,3]{1,3,0,2:T(4,128)(2,1)S(1)}, bf16[2,200,14,3]{1,3,0,2:T(4,128)(2,1)S(1)}, u32[]{:S(2)}, u32[]{:S(2)}) collective-permute-start(bf16[2,200,14,3]{1,3,0,2:T(4,128)(2,1)S(1)} %get-tuple-element.61), channel_id=1, source_target_pairs={{1,0},{2,1},{3,2},{4,3},{5,4},{6,5},{7,6},{9,8},{10,9},{11,10},{12... | collective-permute-start | bytes 100808 | tf_op jit(solution)/shard_map/ppermute | solution.py:794
  137.7 16.9 %copy-start.17 = (bf16[4,200]{1,0:T(4,128)(2,1)S(1)}, bf16[4,200]{1,0:T(4,128)(2,1)}, u32[]{:S(2)}) copy-start(bf16[4,200]{1,0:T(4,128)(2,1)} %param.42) | copy-start | bytes 4804
  137.7 20.6 %copy-start.13 = (f32[200,49]{0,1:T(8,128)S(1)}, f32[200,49]{0,1:T(8,128)}, u32[]{:S(2)}) copy-start(f32[200,49]{0,1:T(8,128)} %param.47) | copy-start | bytes 117604
  137.7 74.5 %all-to-all-start.1 = ((bf16[128,3,48,128]{3,2,1,0:T(8,128)(2,1)}), bf16[128,3,48,128]{3,2,1,0:T(8,128)(2,1)}, u32[]{:S(2)}, u32[]{:S(2)}) async-start(bf16[128,3,48,128]{3,2,1,0:T(8,128)(2,1)} %bitcast.67), calls=%async_computation.2 | async-start | bytes 9437184 | tf_op jit(solution)/shard_map/all_to_all | solution.py:899
  154.6 6.4 %copy-start.3 = (bf16[800,8,256]{2,1,0:T(8,128)(2,1)S(1)}, bf16[800,8,256]{2,1,0:T(8,128)(2,1)}, u32[]{:S(2)}) copy-start(bf16[800,8,256]{2,1,0:T(8,128)(2,1)} %param.45) | copy-start | bytes 9830404
  167.0 7.6 %copy-start.4 = (f32[2,200,392]{2,1,0:T(8,128)S(1)}, f32[2,200,392]{2,1,0:T(8,128)}, u32[]{:S(2)}) copy-start(f32[2,200,392]{2,1,0:T(8,128)} %copy.81) | copy-start | bytes 1881604
  167.0 7.6 %copy-start.7 = (f32[200,392]{1,0:T(8,128)S(1)}, f32[200,392]{1,0:T(8,128)}, u32[]{:S(2)}) copy-start(f32[200,392]{1,0:T(8,128)} %copy.80) | copy-start | bytes 940804
  240.1 19.5 %copy-start.11 = (bf16[200,800]{1,0:T(8,128)(2,1)S(1)}, bf16[200,800]{1,0:T(8,128)(2,1)}, u32[]{:S(2)}) copy-start(bf16[200,800]{1,0:T(8,128)(2,1)} %param.48) | copy-start | bytes 960004
  240.1 20.4 %copy-start.10 = (bf16[200,250]{1,0:T(8,128)(2,1)S(1)}, bf16[200,250]{1,0:T(8,128)(2,1)}, u32[]{:S(2)}) copy-start(bf16[200,250]{1,0:T(8,128)(2,1)} %param.50) | copy-start | bytes 300004
  240.2 21.2 %copy-start.18 = (f32[200]{0:T(256)S(1)}, f32[200]{0:T(256)}, u32[]{:S(2)}) copy-start(f32[200]{0:T(256)} %param.46) | copy-start | bytes 2404
  256.0 39.0 %all-to-all-start.3 = ((bf16[8,24,48,128]{3,2,1,0:T(8,128)(2,1)}), bf16[8,24,48,128]{3,2,1,0:T(8,128)(2,1)S(1)}, u32[]{:S(2)}, u32[]{:S(2)}) async-start(bf16[8,24,48,128]{3,2,1,0:T(8,128)(2,1)} %get-tuple-element.53), calls=%async_computation.4 | async-start | bytes 4718592 | tf_op jit(solution)/shard_map/all_to_all | solution.py:952
  277.5 24.7 %copy-start.9 = (bf16[1000,250]{1,0:T(8,128)(2,1)S(1)}, bf16[1000,250]{1,0:T(8,128)(2,1)}, u32[]{:S(2)}) copy-start(bf16[1000,250]{1,0:T(8,128)(2,1)} %param.57) | copy-start | bytes 1500004
  295.0 8.1 %copy-start.14 = (f32[250,49]{0,1:T(8,128)S(1)}, f32[250,49]{0,1:T(8,128)}, u32[]{:S(2)}) copy-start(f32[250,49]{0,1:T(8,128)} %param.55) | copy-start | bytes 147004
  295.0 8.1 %copy-start.19 = (f32[250]{0:T(256)S(1)}, f32[250]{0:T(256)}, u32[]{:S(2)}) copy-start(f32[250]{0:T(256)} %param.54) | copy-start | bytes 3004
  295.0 24.5 %copy-start.2 = (bf16[8,24,48,128]{3,2,1,0:T(8,128)(2,1)}, bf16[8,24,48,128]{3,2,1,0:T(8,128)(2,1)S(1)}, u32[]{:S(2)}) copy-start(bf16[8,24,48,128]{3,2,1,0:T(8,128)(2,1)S(1)} %all-to-all-done.3.update_ref) | copy-start | bytes 7077892
  295.1 37.2 %all-to-all-start.2 = ((bf16[8,24,48,128]{3,2,1,0:T(8,128)(2,1)}), bf16[8,24,48,128]{3,2,1,0:T(8,128)(2,1)}, u32[]{:S(2)}, u32[]{:S(2)}) async-start(bf16[8,24,48,128]{3,2,1,0:T(8,128)(2,1)} %get-tuple-element.52), calls=%async_computation.3 | async-start | bytes 4718592 | tf_op jit(solution)/shard_map/all_to_all | solution.py:972
  (5 other events, 19.1 us)
Sparse Core Ops, SparseCore 0:
  47.3 31.0 reduce-scatter.1

commit v3 on v2

--- a/solution.py
+++ b/solution.py
@@ -56,26 +56,223 @@
     return (forward, inverse)
 
 
-def turn_kernel(in_ref, out_ref, wide):
-    rows, chans, lanes = in_ref.shape
-    wide[...] = in_ref[...].astype(F32).reshape(rows * chans, lanes)
-    for c in range(chans):
-        out_ref[c] = wide[pl.ds(c, rows, stride=chans), :].astype(BF16)
-
-
-def turn_channels(field):
-    rows, chans, lons = field.shape
+def greet(partners, more=()):
+    barrier = pltpu.get_barrier_semaphore()
+    for where in more:
+        pl.semaphore_signal(barrier, inc=1, device_id=where, device_id_type=MESH)
+    count = jnp.int32(len(more))
+    for there, where in partners:
+
+        @pl.when(there)
+        def _(where=where):
+            pl.semaphore_signal(barrier, inc=1, device_id=where, device_id_type=MESH)
+
+        count = count + there.astype(jnp.int32)
+    pl.semaphore_wait(barrier, count)
+
+
+def start_edges(low, high, sems, before, after, low_to, high_to):
+    is_before, device_before = before
+    is_after, device_after = after
+
+    def to_before():
+        return pltpu.make_async_remote_copy(
+            low, low_to, sems.at[0], sems.at[1], device_id=device_before, device_id_type=MESH
+        )
+
+    def to_after():
+        return pltpu.make_async_remote_copy(
+            high, high_to, sems.at[2], sems.at[3], device_id=device_after, device_id_type=MESH
+        )
+
+    @pl.when(is_before)
+    def _():
+        to_before().start()
+
+    @pl.when(is_after)
+    def _():
+        to_after().start()
+
+    def finish():
+        @pl.when(is_before)
+        def _():
+            to_before().wait_send()
+            to_after().wait_recv()
+
+        @pl.when(is_after)
+        def _():
+            to_after().wait_send()
+            to_before().wait_recv()
+
+    return finish
+
+
+def swap_edges(*args):
+    start_edges(*args)()
+
+
+def neighbours(bands, blocks):
+    band, block = lax.axis_index("lat"), lax.axis_index("chan")
+    return (
+        (band > 0, (jnp.maximum(band - 1, 0), block)),
+        (band < bands - 1, (jnp.minimum(band + 1, bands - 1), block)),
+        (block > 0, (band, jnp.maximum(block - 1, 0))),
+        (block < blocks - 1, (band, jnp.minimum(block + 1, blocks - 1))),
+    )
+
+
+def ocean_rows_kernel(in_ref, mask_ref, out_ref, wide):
+    _, chans, rows, cols = in_ref.shape
+    value = in_ref[0].astype(F32) * mask_ref[...][None]
+    for t in range(cols // 128):
+        wide[t] = value[:, :, t * 128 : (t + 1) * 128].reshape(chans * rows, 128)
+    for y in range(rows):
+        for t in range(cols // 128):
+            out_ref[y, 0, :, t * 128 : (t + 1) * 128] = wide[
+                t, pl.ds(y, chans, stride=rows), :
+            ].astype(BF16)
+
+
+def ocean_rows(field, mask):
+    probes, chans, rows, cols = field.shape
     return pl.pallas_call(
-        turn_kernel,
-        grid=(lons // 128,),
-        in_specs=[pl.BlockSpec((rows, chans, 128), lambda i: (0, 0, i))],
-        out_specs=pl.BlockSpec((chans, rows, 128), lambda i: (0, 0, i)),
-        out_shape=jax.ShapeDtypeStruct((chans, rows, lons), BF16),
-        scratch_shapes=[pltpu.VMEM((rows * chans, 128), F32)],
+        ocean_rows_kernel,
+        grid=(probes,),
+        in_specs=[
+            pl.BlockSpec((1, chans, rows, cols), lambda p: (p, 0, 0, 0)),
+            whole(mask.shape),
+        ],
+        out_specs=pl.BlockSpec((rows, 1, chans, cols), lambda p: (0, p, 0, 0)),
+        out_shape=jax.ShapeDtypeStruct((rows, probes, chans, cols), BF16),
+        scratch_shapes=[pltpu.VMEM((cols // 128, chans * rows, 128), F32)],
         compiler_params=params(),
-        cost_estimate=cost(0, 4 * field.size),
-        name="turn_channels",
-    )(field)
+        cost_estimate=cost(field.size, 4 * field.size),
+        name="ocean_rows",
+    )(field, mask)
+
+
+STEPS = (
+    ((0, 1), (1, 0), (0, 3), (3, 0), (1, 1), (3, 3), (1, 3), (3, 1))
+    + ((0, 2), (2, 0), (2, 2), (1, 2), (2, 1), (3, 2), (2, 3))
+)
+
+
+def lat_partner(band, step, side):
+    dz, dx = step
+    return lax.rem(band // side + dz, side) * side + lax.rem(lax.rem(band, side) + dx, side)
+
+
+def open_kernel(
+    blocks, probe_ref, ocean_ref, out_ref, around_ref, taken, wide, turned, tall, sems, own, edge
+):
+    send, recv, load = sems
+    rows, chans, lons = probe_ref.shape
+    bands, part = out_ref.shape[0], out_ref.shape[1]
+    side = math.isqrt(bands)
+    lines, _, _, cols = ocean_ref.shape
+    pieces, lanes = taken.shape[0], taken.shape[3]
+    band, block = lax.axis_index("lat"), lax.axis_index("chan")
+    lat_before, lat_after, chan_before, chan_after = neighbours(bands, blocks)
+
+    def take(i):
+        return pltpu.make_async_copy(
+            probe_ref.at[:, :, pl.ds(i * lanes, lanes)], taken.at[i], load.at[i]
+        )
+
+    for i in range(pieces):
+        take(i).start()
+    tall[...] = jnp.zeros_like(tall)
+    others = [(lat_partner(band, step, side), block) for step in STEPS]
+    greet((chan_before, chan_after), others)
+    inner = pl.ds(128, cols)
+    center = pltpu.make_async_copy(ocean_ref, tall.at[pl.ds(3, lines), :, :, inner], own.at[0])
+    center.start()
+    finish_rows = start_edges(
+        ocean_ref.at[pl.ds(0, 3)],
+        ocean_ref.at[pl.ds(lines - 3, 3)],
+        edge.at[0],
+        lat_before,
+        lat_after,
+        tall.at[pl.ds(lines + 3, 3), :, :, inner],
+        tall.at[pl.ds(0, 3), :, :, inner],
+    )
+    copies = []
+    for i in range(pieces):
+        take(i).wait()
+        for t in range(lanes // 128):
+            at = slice(t * 128, (t + 1) * 128)
+            wide[t] = taken[i, :, :, at].astype(F32).reshape(rows * chans, 128)
+            for c in range(chans):
+                turned[i, c, :, at] = wide[t, pl.ds(c, rows, stride=chans), :].astype(BF16)
+        columns = pl.ds(i * lanes, lanes)
+        for k, where in enumerate(others):
+            copy = pltpu.make_async_remote_copy(
+                turned.at[i, pl.ds(where[0] * part, part)],
+                out_ref.at[band, :, :, columns],
+                send.at[i, k],
+                recv.at[i, k],
+                device_id=where,
+                device_id_type=MESH,
+            )
+            copy.start()
+            copies.append(copy)
+        copy = pltpu.make_async_copy(
+            turned.at[i, pl.ds(band * part, part)],
+            out_ref.at[band, :, :, columns],
+            own.at[i + 1],
+        )
+        copy.start()
+        copies.append(copy)
+    center.wait()
+    finish_rows()
+    finish_columns = start_edges(
+        tall.at[:, :, :, pl.ds(128, 128)],
+        tall.at[:, :, :, pl.ds(cols, 128)],
+        edge.at[1],
+        chan_before,
+        chan_after,
+        tall.at[:, :, :, pl.ds(128 + cols, 128)],
+        tall.at[:, :, :, pl.ds(0, 128)],
+    )
+    finish_columns()
+    store = pltpu.make_async_copy(tall, around_ref, own.at[0])
+    store.start()
+    for copy in copies:
+        copy.wait()
+    store.wait()
+
+
+def open_exchange(probe, ocean, bands, blocks):
+    rows, chans, lons = probe.shape
+    lines, probes, fine, cols = ocean.shape
+    pieces, lanes = 4, lons // 4
+    any_spec = pl.BlockSpec(memory_space=pl.ANY)
+    tall = (lines + 6, probes, fine, cols + 256)
+    return pl.pallas_call(
+        functools.partial(open_kernel, blocks),
+        in_specs=[any_spec, any_spec],
+        out_specs=[any_spec, any_spec],
+        out_shape=[
+            jax.ShapeDtypeStruct((bands, chans // bands, rows, lons), BF16),
+            jax.ShapeDtypeStruct(tall, BF16),
+        ],
+        scratch_shapes=[
+            pltpu.VMEM((pieces, rows, chans, lanes), BF16),
+            pltpu.VMEM((lanes // 128, rows * chans, 128), F32),
+            pltpu.VMEM((pieces, chans, rows, lanes), BF16),
+            pltpu.VMEM(tall, BF16),
+            [
+                pltpu.SemaphoreType.DMA((pieces, bands - 1)),
+                pltpu.SemaphoreType.DMA((pieces, bands - 1)),
+                pltpu.SemaphoreType.DMA((pieces,)),
+            ],
+            pltpu.SemaphoreType.DMA((pieces + 1,)),
+            pltpu.SemaphoreType.DMA((2, 4)),
+        ],
+        compiler_params=params(collective_id=3, has_side_effects=True),
+        cost_estimate=cost(0, 4 * probe.size),
+        name="open_exchange",
+    )(probe, ocean)
 
 
 def probe_flux_kernel(probe_ref, weight_ref, out_ref):
@@ -312,14 +509,9 @@
     )(probe, update, *rest)
 
 
-def depth_sum(in_ref, p, first, taps_ref, wide, done):
-    high, _, broad, chans = in_ref.shape
+def depth_sum(first, taps_ref, wide, done):
+    halves, high = wide.shape[0], wide.shape[1]
     rows, cols = done.shape[0], done.shape[1]
-    halves = wide.shape[0]
-    for y in range(high):
-        for h in range(halves):
-            lanes = min(128, chans - h * 128)
-            wide[h, y, 0:broad, 0:lanes] = in_ref[y, p, :, h * 128 : h * 128 + lanes].astype(F32)
 
     def tile(i, carry):
         at = pl.multiple_of(i * 8, 8)
@@ -341,9 +533,16 @@
 
 
 def depth_kernel(in_ref, taps_ref, out_ref, wide, done):
-    depth_sum(in_ref, 0, 0, taps_ref, wide, done)
+    high, _, chans, broad = in_ref.shape
+    for y in range(high):
+        value = in_ref[y, 0].astype(F32)
+        for h in range(wide.shape[0]):
+            top = min(128, chans - h * 128)
+            part = value[h * 128 : h * 128 + top]
+            wide[h, y, :, 0:top] = part.T
+    depth_sum(125, taps_ref, wide, done)
     for y in range(done.shape[0]):
-        out_ref[y] = done[y].T[0 : in_ref.shape[3]]
+        out_ref[y] = done[y].T[0:chans]
 
 
 def tap_rows(kernel):
@@ -352,86 +551,28 @@
     return jnp.repeat(jnp.pad(kernel.T, ((0, 0), (0, full - chans))), 8, axis=0)
 
 
-def depthwise(padded, kernel):
-    high, probes, broad, chans = padded.shape
-    rows, cols = high - 6, broad - 6
+def depthwise(around, kernel):
+    high, probes, chans, broad = around.shape
+    rows, cols = high - 6, broad - 256
     halves = -(-chans // 128)
     taps = tap_rows(kernel)
     return pl.pallas_call(
         depth_kernel,
         grid=(probes,),
         in_specs=[
-            pl.BlockSpec((high, 1, broad, chans), lambda p: (0, p, 0, 0)),
+            pl.BlockSpec((high, 1, chans, broad), lambda p: (0, p, 0, 0)),
             whole(taps.shape),
         ],
         out_specs=pl.BlockSpec((rows, chans, cols), lambda p: (0, 0, p)),
         out_shape=jax.ShapeDtypeStruct((rows, chans, probes * cols), F32),
         scratch_shapes=[
-            pltpu.VMEM((halves, high, -(-broad // 8) * 8, 128), F32),
+            pltpu.VMEM((halves, high, broad, 128), F32),
             pltpu.VMEM((rows, cols, halves * 128), F32),
         ],
         compiler_params=params(),
-        cost_estimate=cost(200 * rows * cols * chans * probes, 4 * padded.size),
+        cost_estimate=cost(200 * rows * cols * chans * probes, 4 * around.size),
         name="depthwise",
-    )(padded, taps)
-
-
-def greet(partners, more=()):
-    barrier = pltpu.get_barrier_semaphore()
-    for where in more:
-        pl.semaphore_signal(barrier, inc=1, device_id=where, device_id_type=MESH)
-    count = jnp.int32(len(more))
-    for there, where in partners:
-
-        @pl.when(there)
-        def _(where=where):
-            pl.semaphore_signal(barrier, inc=1, device_id=where, device_id_type=MESH)
-
-        count = count + there.astype(jnp.int32)
-    pl.semaphore_wait(barrier, count)
-
-
-def swap_edges(low, high, sems, before, after, low_to, high_to):
-    is_before, device_before = before
-    is_after, device_after = after
-
-    def to_before():
-        return pltpu.make_async_remote_copy(
-            low, low_to, sems.at[0], sems.at[1], device_id=device_before, device_id_type=MESH
-        )
-
-    def to_after():
-        return pltpu.make_async_remote_copy(
-            high, high_to, sems.at[2], sems.at[3], device_id=device_after, device_id_type=MESH
-        )
-
-    @pl.when(is_before)
-    def _():
-        to_before().start()
-
-    @pl.when(is_after)
-    def _():
-        to_after().start()
-
-    @pl.when(is_before)
-    def _():
-        to_before().wait_send()
-        to_after().wait_recv()
-
-    @pl.when(is_after)
-    def _():
-        to_after().wait_send()
-        to_before().wait_recv()
-
-
-def neighbours(bands, blocks):
-    band, block = lax.axis_index("lat"), lax.axis_index("chan")
-    return (
-        (band > 0, (jnp.maximum(band - 1, 0), block)),
-        (band < bands - 1, (jnp.minimum(band + 1, bands - 1), block)),
-        (block > 0, (band, jnp.maximum(block - 1, 0))),
-        (block < blocks - 1, (band, jnp.minimum(block + 1, blocks - 1))),
-    )
+    )(around, taps)
 
 
 def flux_kernel(
@@ -615,7 +756,8 @@
     center = columns[pl.ds(pl.multiple_of((step + 3) * 56 + 24, 8), 8), :].astype(BF16)
     spread = spread_ref[0] + jnp.concatenate([mm(mix_ref[p], near) for p in range(2)], axis=1)
     forcing = jnp.concatenate([mm(couple_ref[p], center) for p in range(2)], axis=1)
-    start = (probe_ref[0].astype(F32) + forcing).astype(BF16).astype(F32)
+    probe = jnp.concatenate([probe_ref[0, 0], probe_ref[0, 1]], axis=1).astype(F32)
+    start = (probe + forcing).astype(BF16).astype(F32)
     at = pl.ds(step, 1)
     tangent = normed_step(spread, base_ref[0].astype(F32), sigma_ref[at, :], gain_ref[...])
     slope = slope_ref[0].astype(F32)
@@ -650,7 +792,7 @@
         grid=(rows,),
         in_specs=[
             pl.BlockSpec((1, chans, wide), row),
-            pl.BlockSpec((1, chans, wide), row),
+            pl.BlockSpec((1,) + probe.shape[1:], lambda i: (i, 0, 0, 0)),
             whole(flux.shape),
             whole(mask.shape),
             whole(sigma.shape),
@@ -712,7 +854,11 @@
     def _():
         half = done.shape[1]
         for p in range(probes):
-            depth_sum(around_ref, p, 13, taps_ref, tall, done)
+            for y in range(tall.shape[1]):
+                for h in range(tall.shape[0]):
+                    top = min(128, chans - h * 128)
+                    tall[h, y, :, 0:top] = around_ref[y, p, :, h * 128 : h * 128 + top].astype(F32)
+            depth_sum(13, taps_ref, tall, done)
             for y in range(done.shape[0]):
                 spread[y, :, p * half : (p + 1) * half] = done[y].T[0:chans]
 
@@ -783,25 +929,6 @@
         cost_estimate=cost(1e9, 4e6),
         name="coarse_level",
     )(around, taps, field, sigma, base, slope, gain, expand, shrink, spreadout, up, one, mask)
-
-
-def shifted(block, axis):
-    count = lax.axis_size(axis)
-    forward = [(i, i + 1) for i in range(count - 1)]
-    backward = [(i + 1, i) for i in range(count - 1)]
-    return (
-        lambda low: lax.ppermute(low, axis, forward),
-        lambda high: lax.ppermute(high, axis, backward),
-    )
-
-
-def with_halo(block, sides, width):
-    for axis, dim in sides:
-        up, down = shifted(block, axis)
-        low = up(lax.slice_in_dim(block, block.shape[dim] - width, None, axis=dim))
-        high = down(lax.slice_in_dim(block, 0, width, axis=dim))
-        block = jnp.concatenate([low, block, high], axis=dim)
-    return block
 
 
 def local(
@@ -844,8 +971,6 @@
     fields = weight_flux.shape[1]
 
     flat_probe = probe_field.reshape(pair, width, lons)
-    turned = turn_channels(flat_probe).reshape(bands, part, pair, lons)
-    gathered = lax.all_to_all(turned, "lat", split_axis=0, concat_axis=0, tiled=True)
 
     flux_rows = lax.dynamic_slice_in_dim(
         weight_flux, lax.axis_index("chan") * width, width, 0
@@ -858,16 +983,12 @@
         ],
         axis=0,
     )
-    probe_terms = lax.psum_scatter(
-        probe_flux(probe_field, flux_pair), "chan", scatter_dimension=0, tiled=True
-    )
+    terms = probe_flux(probe_field, flux_pair)
 
     tile_rows, tile_cols = ocean_mask.shape
     fine = ocean_probe.shape[1]
     mask = ocean_mask.astype(F32)
-    masked = ocean_probe * ocean_mask.astype(BF16)
-    padded = with_halo(masked, (("lat", 2), ("chan", 3)), 3).transpose(2, 0, 3, 1)
-    start = masked.transpose(2, 1, 0, 3).reshape(tile_rows, fine, probes * tile_cols)
+    start = ocean_rows(ocean_probe, mask)
     base_rows = base_fine.transpose(1, 0, 2)
     slope_rows = slope_fine.transpose(1, 0, 2)
     base_lines = base_coarse.transpose(1, 0, 2)
@@ -887,14 +1008,14 @@
     pool = jnp.where(meets, 0.25, 0.0).astype(BF16)
     spreadout = jnp.where(meets.T, 1.0, 0.0).astype(BF16)
 
+    gathered, around = open_exchange(flat_probe, start, bands, blocks)
+
     fwd_lat, inv_lat = cosine_tables(lats)
     diff = jnp.asarray(fourier_product(lons))
     filt = lax.dynamic_slice_in_dim(
         spectral_filter, lax.axis_index("lat") * part, part, 1
     ).T.reshape(part, lats, 1)
-    gathered, padded, start, filt, probe_terms = lax.optimization_barrier(
-        (gathered, padded, start, filt, probe_terms)
-    )
+    gathered, filt = lax.optimization_barrier((gathered, filt))
     mixed = lat_filter(gathered, jnp.asarray(fwd_lat.T), jnp.asarray(inv_lat.T), filt, diff)
     regrouped = lax.all_to_all(
         mixed.reshape(bands * blocks, part, pair, 128),
@@ -909,7 +1030,8 @@
     )
     folded = mm(weight_out, weight_flux).astype(BF16)
     wout = jnp.concatenate([weight_out, folded, folded], axis=1).T
-    spread = depthwise(padded, kernel_fine)
+    probe_terms = lax.psum_scatter(terms, "chan", scatter_dimension=0, tiled=True)
+    spread = depthwise(around, kernel_fine)
     (
         regrouped,
         spread,

time: 346 us -> 315 us (0.910)
  Pallas kernels: 154 us -> 229 us
  waiting for transfers between devices: 79.1 us -> 16.6 us
  starting transfers between devices: 46.2 us -> 23.1 us
  local copies, waits for them, and re-layouts: 37.7 us -> 24.9 us
  other arithmetic: 11.6 us -> 5.37 us
    pallas_call x1 -> x2, Pallas kernels: 8.15 us -> 77.3 us  [the longest x1 74.3 us: open_exchange(): pl.pallas_call(functools.partial(open_kernel, blocks), in_specs=[any_spec...]
    ppermute x4 -> x0, waiting for transfers between devices: 57.2 us -> none  [the longest x2 51.6 us: shifted(): lax.ppermute(low, axis, forward)]
    all_to_all x1, waiting for transfers between devices: 13.7 us -> 0.01 us  [local(): lax.all_to_all(mixed.reshape(bands * blocks, part, pair, 128), ('lat', 'c...]
    ppermute x4 -> x0, starting transfers between devices: 10.5 us -> none  [the longest x2 5.86 us: shifted(): lax.ppermute(high, axis, backward)]
    reduce_scatter x1, waiting for transfers between devices: 0.01 us -> 8.37 us  [local(): lax.psum_scatter(terms, 'chan', scatter_dimension=0, tiled=True)]
    all_to_all x1, starting transfers between devices: 16.9 us -> 8.69 us  [local(): lax.all_to_all(mixed.reshape(bands * blocks, part, pair, 128), ('lat', 'c...]
    all_to_all x1 -> x0, starting transfers between devices: 8.03 us -> none  [local(): lax.all_to_all(turned, 'lat', split_axis=0, concat_axis=0, tiled=True)]
    slice x3 -> x0, local copies, waits for them, and re-layouts: 4.33 us -> none  [the longest x2 3.24 us: with_halo(): low = up(lax.slice_in_dim(block, block.shape[dim] - width, None, axis=dim))]
  transfers between devices with their start and end apart: 9 -> 4, of which waited for: 5 -> 2; matrix products, arithmetic and copies ran while one was open for 14% -> 8% of each run, Pallas kernels for 23% -> 26%
where the time goes in v3:
time: 315 us; the launch traced here: 314 us
  Pallas kernels  229 us (73%)
  local copies, waits for them, and re-layouts  24.9 us (8%)
  starting transfers between devices  23.1 us (7%)
  waiting for transfers between devices  16.6 us (5%)
  between operations  14.3 us (5%)
  other arithmetic  5.37 us (2%)
    pallas_call x1, Pallas kernels, open_exchange(): pl.pallas_call(functools.partial(open_kernel, blocks), in_specs=[any_spec...  74.3 us
    pallas_call x1, Pallas kernels, pointwise(): pl.pallas_call(point_kernel, grid=(rows,), in_specs=[whole(mixed.shape),...  27.9 us
    pallas_call x1, Pallas kernels, depthwise(): pl.pallas_call(depth_kernel, grid=(probes,), in_specs=[pl.BlockSpec((high...  26.9 us
    pallas_call x1, Pallas kernels, lat_filter(): pl.pallas_call(filter_kernel, grid=(chans,), in_specs=[pl.BlockSpec((band...  18.8 us
    pallas_call x1, Pallas kernels, flux_tile(): pl.pallas_call(functools.partial(flux_kernel, blocks), in_specs=[whole(a....  17.5 us
    pallas_call x1, Pallas kernels, coarse_edges(): pl.pallas_call(functools.partial(edge_kernel, bands, blocks), in_specs=[w...  17.3 us
    pallas_call x1, Pallas kernels, coarse_level(): pl.pallas_call(coarse_kernel, grid=(lines,), in_specs=[whole(around.shape...  14.7 us
    pallas_call x1, Pallas kernels, fine_level(): pl.pallas_call(fine_kernel, grid=(rows,), in_specs=[pl.BlockSpec((1, chan...  14 us
  transfers between devices with their start and end apart: 4, of which 2 were waited for; matrix products, arithmetic and copies ran while one was open for 8% of the time, Pallas kernels for 26%

profile of v3, /device:TPU:32, one launch (start us, length us, event | category | flops | bytes accessed | tf_op | source)
XLA Modules:
  0.0 313.6 jit_solution(4185790401916614742)
XLA Ops:
  7.2 1.3 convert_element_type.29.mask_ref
  8.5 3.1 ocean_rows.1.ocean_ref.probe_ref
  11.6 74.3 %open_exchange.1 = (bf16[16,3,48,1024]{3,2,1,0:T(8,128)(2,1)}, bf16[14,2,200,512]{3,2,1,0:T(8,128)(2,1)}) custom-call(bf16[48,48,1024]{2,1,0:T(8,128)(2,1)} %bitcast.54, bf16[8,2,200,256]{3,2,1,0:T(8,128)(2,1)} %ocean_rows.1.ocean_ref.probe_ref), custom_call_target="tpu_custom_call" | custom-call | bytes 9437184 | tf_op jit(solution)/shard_map/open_exchange/pallas_call | solution.py:251
  87.0 18.8 %lat_filter.1 = bf16[16,8,3,48,128]{4,3,2,1,0:T(8,128)(2,1)} custom-call(bf16[16,3,48,1024]{3,2,1,0:T(8,128)(2,1)} %get-tuple-element.31.in_ref, bf16[384,384]{1,0:T(8,128)(2,1)} %constant.50.clone.fwd_ref, bf16[384,384]{1,0:T(8,128)(2,1)} %constant.51.clone.inv_ref, f32[3,384,1]{2,1,0:T(8,128)} %copy.62.filt_ref, bf16[1024,1024]{1,0:T(8,128)(2,1)} %constant.49.clone.diff_ref), custom_call_target="tpu_custom_call" | custom-call | flops 8400000000 | bytes 9437184 | tf_op jit(solution)/shard_map/lat_filter/pallas_call | solution.py:362
  105.7 8.7 %all-to-all-start = ((bf16[128,3,48,128]{3,2,1,0:T(8,128)(2,1)}), bf16[128,3,48,128]{3,2,1,0:T(8,128)(2,1)}, u32[]{:S(2)}, u32[]{:S(2)}) async-start(bf16[128,3,48,128]{3,2,1,0:T(8,128)(2,1)} %bitcast.59), calls=%async_computation | async-start | bytes 9437184 | tf_op jit(solution)/shard_map/all_to_all | solution.py:1020
  115.4 5.6 %probe_flux.1 = bf16[8,192,128]{2,1,0:T(8,128)(2,1)} custom-call(bf16[2,24,48,1024]{3,2,1,0:T(8,128)(2,1)} %probe_ref.1, bf16[8,96]{1,0:T(8,128)(2,1)} %fusion.2.weight_ref), custom_call_target="tpu_custom_call" | custom-call | flops 37748736 | bytes 4718592 | tf_op jit(solution)/shard_map/probe_flux/pallas_call | solution.py:295
  125.0 2.4 copy.71
  127.4 1.9 copy.70
  129.3 2.5 copy.82
  131.8 1.3 reshape.94
  135.0 1.1 copy.83
  138.0 26.9 %depthwise.1.spread_ref = f32[8,200,512]{2,1,0:T(8,128)} custom-call(bf16[14,2,200,512]{3,2,1,0:T(8,128)(2,1)} %get-tuple-element.33.in_ref, f32[392,256]{1,0:T(8,128)} %broadcast_bitcast_fusion.3.taps_ref), custom_call_target="tpu_custom_call" | custom-call | flops 163840000 | bytes 11468800 | tf_op jit(solution)/shard_map/depthwise/pallas_call | solution.py:559
  167.3 8.4 %reduce-scatter.2.cloned.1.call-done.pflux_ref = bf16[1,192,128]{2,1,0:T(8,128)(2,1)} async-done(((bf16[8,192,128]{2,1,0:T(8,128)(2,1)}), bf16[1,192,128]{2,1,0:T(8,128)(2,1)}) %reduce-scatter.2.cloned.1.call-update) | async-done | bytes 49168 | tf_op jit(solution)/shard_map/reduce_scatter | solution.py:1033
  175.7 27.9 %pointwise.1 = (bf16[8,24,48,128]{3,2,1,0:T(8,128)(2,1)}, bf16[8,24,48,128]{3,2,1,0:T(8,128)(2,1)}, f32[16,8,128]{2,1,0:T(8,128)}) custom-call(bf16[384,48,128]{2,1,0:T(8,128)(2,1)} %bitcast.4.mixed_ref, bf16[24,768,128]{2,1,0:T(8,128)(2,1)} %slope_ref.1, bf16[768,384]{1,0:T(8,128)(2,1)} %bitcast.66, bf16[392,768]{1,0:T(8,128)(2,1)} %maximum_bitcast_fusion.wout_ref, ...), custom_call_target="tpu_custom_call" | custom-call | flops 7299999744 | bytes 14155776 | tf_op jit(solution)/shard_map/pointwise/pallas_call | solution.py:449
  203.6 17.5 %flux_tile.1.flux_ref = f32[14,8,512]{2,1,0:T(8,128)} custom-call(f32[16,8,128]{2,1,0:T(8,128)} %get-tuple-element.41.picked_ref, s32[4,2048]{1,0:T(4,128)} %bitcast.73, f32[4,2048]{1,0:T(4,128)} %bitcast.74, f32[8,256]{1,0:T(8,128)} %convert_element_type.29.mask_ref), custom_call_target="tpu_custom_call" | custom-call | tf_op jit(solution)/shard_map/flux_tile/pallas_call | solution.py:648
  221.1 6.9 %all-to-all-start.2 = ((bf16[8,24,48,128]{3,2,1,0:T(8,128)(2,1)}), bf16[8,24,48,128]{3,2,1,0:T(8,128)(2,1)S(1)}, u32[]{:S(2)}, u32[]{:S(2)}) async-start(bf16[8,24,48,128]{3,2,1,0:T(8,128)(2,1)} %get-tuple-element.51), calls=%async_computation.3 | async-start | bytes 4718592 | tf_op jit(solution)/shard_map/all_to_all | solution.py:1074
  231.9 14.0 %fine_level.1 = (bf16[8,200,512]{2,1,0:T(8,128)(2,1)}, bf16[4,250,256]{2,1,0:T(8,128)(2,1)}, bf16[4,2,128,256]{3,2,1,0:T(8,128)(2,1)}) custom-call(f32[8,200,512]{2,1,0:T(8,128)} %depthwise.1.spread_ref, bf16[8,2,200,256]{3,2,1,0:T(8,128)(2,1)} %ocean_rows.1.ocean_ref.probe_ref, f32[14,8,512]{2,1,0:T(8,128)} %flux_tile.1.flux_ref, ...), custom_call_target="tpu_custom_call" | custom-call | tf_op jit(solution)/shard_map/fine_level/pallas_call | solution.py:790
  245.9 17.3 %coarse_edges.1.around_ref = bf16[10,2,160,256]{3,2,1,0:T(8,128)(2,1)} custom-call(bf16[4,2,128,256]{3,2,1,0:T(8,128)(2,1)} %get-tuple-element.49.field_ref), custom_call_target="tpu_custom_call" | custom-call | tf_op jit(solution)/shard_map/coarse_edges/pallas_call | solution.py:698
  263.3 1.4 copy-done.2
  264.7 7.3 %all-to-all-start.1 = ((bf16[8,24,48,128]{3,2,1,0:T(8,128)(2,1)}), bf16[8,24,48,128]{3,2,1,0:T(8,128)(2,1)}, u32[]{:S(2)}, u32[]{:S(2)}) async-start(bf16[8,24,48,128]{3,2,1,0:T(8,128)(2,1)} %get-tuple-element.50), calls=%async_computation.2 | async-start | bytes 4718592 | tf_op jit(solution)/shard_map/all_to_all | solution.py:1094
  274.6 14.7 %coarse_level.1 = bf16[2,200,8,256]{3,2,1,0:T(8,128)(2,1)} custom-call(bf16[10,2,160,256]{3,2,1,0:T(8,128)(2,1)} %coarse_edges.1.around_ref, f32[392,256]{1,0:T(8,128)} %broadcast_bitcast_fusion.1.taps_ref, bf16[4,250,256]{2,1,0:T(8,128)(2,1)} %get-tuple-element.53.field_ref, f32[4,128]{1,0:T(4,128)} %sigma_ref.3, bf16[4,250,128]{2,1,0:T(8,128)(2,1)} %bitcast.65, ...), custom_call_target="tpu_custom_call" | custom-call | flops 1000000000 | bytes 4000000 | tf_op jit(solution)/shard_map/coarse_level/pallas_call | solution.py:902
  289.4 4.6 %add_update.2.rest_0_ = bf16[48,48,1024]{2,1,0:T(8,128)(2,1)} custom-call(bf16[48,48,1024]{2,1,0:T(8,128)(2,1)} %bitcast.55, bf16[8,24,48,128]{3,2,1,0:T(8,128)(2,1)} %copy-done.2), custom_call_target="tpu_custom_call" | custom-call | flops 1179648 | bytes 7077888 | tf_op jit(solution)/shard_map/add_update/pallas_call | solution.py:495
  293.9 8.2 %all-to-all-done.1.update_ref = bf16[8,24,48,128]{3,2,1,0:T(8,128)(2,1)} async-done(((bf16[8,24,48,128]{3,2,1,0:T(8,128)(2,1)}), bf16[8,24,48,128]{3,2,1,0:T(8,128)(2,1)}, u32[]{:S(2)}, u32[]{:S(2)}) %all-to-all-start.1) | async-done | bytes 2359328 | tf_op jit(solution)/shard_map/all_to_all | solution.py:1094
  302.1 4.6 %add_update.3 = bf16[48,48,1024]{2,1,0:T(8,128)(2,1)} custom-call(bf16[48,48,1024]{2,1,0:T(8,128)(2,1)} %bitcast.56, bf16[8,24,48,128]{3,2,1,0:T(8,128)(2,1)} %all-to-all-done.1.update_ref, bf16[48,48,1024]{2,1,0:T(8,128)(2,1)} %add_update.2.rest_0_), custom_call_target="tpu_custom_call", output_to_operand_aliasing={{}: (2, {})} | custom-call | flops 1179648 | bytes 7077888 | tf_op jit(solution)/shard_map/add_update/pallas_call | solution.py:495
  (72 shorter events, 18.8 us)
Async XLA Ops:
  7.2 1.4 copy-start
  105.7 8.9 %copy-start.15 = (bf16[384,4]{0,1:T(4,128)(2,1)S(1)}, bf16[384,4]{0,1:T(4,128)(2,1)}, u32[]{:S(2)}) copy-start(bf16[384,4]{0,1:T(4,128)(2,1)} %param.36) | copy-start | bytes 9220
  105.7 70.0 %all-to-all-start = ((bf16[128,3,48,128]{3,2,1,0:T(8,128)(2,1)}), bf16[128,3,48,128]{3,2,1,0:T(8,128)(2,1)}, u32[]{:S(2)}, u32[]{:S(2)}) async-start(bf16[128,3,48,128]{3,2,1,0:T(8,128)(2,1)} %bitcast.59), calls=%async_computation | async-start | bytes 9437184 | tf_op jit(solution)/shard_map/all_to_all | solution.py:1020
  114.4 61.3 %reduce-scatter.2.cloned.1.call-start = ((), (), s32[]{:S(2)}) async-start(), calls=%async_computation.4 | async-start | bytes 442368 | tf_op jit(solution)/shard_map/reduce_scatter | solution.py:1033
  115.4 5.6 %copy-start.5 = (bf16[768,384]{1,0:T(8,128)(2,1)S(1)}, bf16[768,384]{1,0:T(8,128)(2,1)}, u32[]{:S(2)}) copy-start(bf16[768,384]{1,0:T(8,128)(2,1)} %param.35) | copy-start | bytes 1769476
  115.4 5.9 %copy-start.13 = (f32[200,49]{0,1:T(8,128)S(1)}, f32[200,49]{0,1:T(8,128)}, u32[]{:S(2)}) copy-start(f32[200,49]{0,1:T(8,128)} %param.47) | copy-start | bytes 117604
  115.4 5.9 %copy-start.16 = (bf16[4,200]{1,0:T(4,128)(2,1)S(1)}, bf16[4,200]{1,0:T(4,128)(2,1)}, u32[]{:S(2)}) copy-start(bf16[4,200]{1,0:T(4,128)(2,1)} %param.42) | copy-start | bytes 4804
  122.5 6.8 %copy-start.3 = (bf16[800,8,256]{2,1,0:T(8,128)(2,1)S(1)}, bf16[800,8,256]{2,1,0:T(8,128)(2,1)}, u32[]{:S(2)}) copy-start(bf16[800,8,256]{2,1,0:T(8,128)(2,1)} %param.45) | copy-start | bytes 9830404
  133.1 2.0 copy-start.7
  133.4 2.7 copy-start.8
  134.0 3.2 %copy-start.12 = (bf16[250,4,128]{2,1,0:T(4,128)(2,1)S(1)}, bf16[250,4,128]{2,1,0:T(4,128)(2,1)}, u32[]{:S(2)}) copy-start(bf16[250,4,128]{2,1,0:T(4,128)(2,1)} %param.51) | copy-start | bytes 768004
  138.0 28.5 %copy-start.4 = (f32[2,200,392]{2,1,0:T(8,128)S(1)}, f32[2,200,392]{2,1,0:T(8,128)}, u32[]{:S(2)}) copy-start(f32[2,200,392]{2,1,0:T(8,128)} %copy.71) | copy-start | bytes 1881604
  138.0 28.5 %copy-start.6 = (f32[200,392]{1,0:T(8,128)S(1)}, f32[200,392]{1,0:T(8,128)}, u32[]{:S(2)}) copy-start(f32[200,392]{1,0:T(8,128)} %copy.70) | copy-start | bytes 940804
  221.1 6.9 %copy-start.11 = (bf16[200,800]{1,0:T(8,128)(2,1)S(1)}, bf16[200,800]{1,0:T(8,128)(2,1)}, u32[]{:S(2)}) copy-start(bf16[200,800]{1,0:T(8,128)(2,1)} %param.48) | copy-start | bytes 960004
  221.1 7.9 %copy-start.10 = (bf16[200,250]{1,0:T(8,128)(2,1)S(1)}, bf16[200,250]{1,0:T(8,128)(2,1)}, u32[]{:S(2)}) copy-start(bf16[200,250]{1,0:T(8,128)(2,1)} %param.50) | copy-start | bytes 300004
  221.1 8.6 %copy-start.17 = (f32[200]{0:T(256)S(1)}, f32[200]{0:T(256)}, u32[]{:S(2)}) copy-start(f32[200]{0:T(256)} %param.46) | copy-start | bytes 2404
  221.1 42.1 %all-to-all-start.2 = ((bf16[8,24,48,128]{3,2,1,0:T(8,128)(2,1)}), bf16[8,24,48,128]{3,2,1,0:T(8,128)(2,1)S(1)}, u32[]{:S(2)}, u32[]{:S(2)}) async-start(bf16[8,24,48,128]{3,2,1,0:T(8,128)(2,1)} %get-tuple-element.51), calls=%async_computation.3 | async-start | bytes 4718592 | tf_op jit(solution)/shard_map/all_to_all | solution.py:1074
  263.2 8.8 %copy-start.9 = (bf16[1000,250]{1,0:T(8,128)(2,1)S(1)}, bf16[1000,250]{1,0:T(8,128)(2,1)}, u32[]{:S(2)}) copy-start(bf16[1000,250]{1,0:T(8,128)(2,1)} %param.57) | copy-start | bytes 1500004
  263.2 9.8 %copy-start.14 = (f32[250,49]{0,1:T(8,128)S(1)}, f32[250,49]{0,1:T(8,128)}, u32[]{:S(2)}) copy-start(f32[250,49]{0,1:T(8,128)} %param.55) | copy-start | bytes 147004
  263.2 9.8 %copy-start.18 = (f32[250]{0:T(256)S(1)}, f32[250]{0:T(256)}, u32[]{:S(2)}) copy-start(f32[250]{0:T(256)} %param.54) | copy-start | bytes 3004
  263.3 1.5 copy-start.2
  264.7 37.4 %all-to-all-start.1 = ((bf16[8,24,48,128]{3,2,1,0:T(8,128)(2,1)}), bf16[8,24,48,128]{3,2,1,0:T(8,128)(2,1)}, u32[]{:S(2)}, u32[]{:S(2)}) async-start(bf16[8,24,48,128]{3,2,1,0:T(8,128)(2,1)} %get-tuple-element.50), calls=%async_computation.2 | async-start | bytes 4718592 | tf_op jit(solution)/shard_map/all_to_all | solution.py:1094
  302.1 4.6 %copy-start.1 = (f32[384,48]{0,1:T(8,128)S(1)}, f32[384,48]{0,1:T(8,128)}, u32[]{:S(2)}) copy-start(f32[384,48]{0,1:T(8,128)} %param.33) | copy-start | bytes 221188
Sparse Core Ops, SparseCore 0:
  121.1 54.5 reduce-scatter.1

commit v4 on v3

--- a/solution.py
+++ b/solution.py
@@ -119,6 +119,50 @@
         (block > 0, (band, jnp.maximum(block - 1, 0))),
         (block < blocks - 1, (band, jnp.minimum(block + 1, blocks - 1))),
     )
+
+
+def chan_peers(blocks):
+    band, block = lax.axis_index("lat"), lax.axis_index("chan")
+    return [(band, lax.rem(block + k, blocks)) for k in range(1, blocks)]
+
+
+def homeward(update_ref, back_ref, first, sems):
+    send, recv, own = sems
+    blocks, _, count = back_ref.shape[:3]
+    block = lax.axis_index("chan")
+    some = pl.ds(first, count)
+    copies = [
+        pltpu.make_async_remote_copy(
+            update_ref.at[where[1], :, some],
+            back_ref.at[block],
+            send.at[k],
+            recv.at[k],
+            device_id=where,
+            device_id_type=MESH,
+        )
+        for k, where in enumerate(chan_peers(blocks))
+    ]
+    return copies + [
+        pltpu.make_async_copy(update_ref.at[block, :, some], back_ref.at[block], own.at[0])
+    ]
+
+
+def homeward_sems(blocks):
+    return [
+        pltpu.SemaphoreType.DMA((blocks - 1,)),
+        pltpu.SemaphoreType.DMA((blocks - 1,)),
+        pltpu.SemaphoreType.DMA((1,)),
+    ]
+
+
+def homeward_shape(update, count):
+    blocks, probes, _, width, lanes = update.shape
+    return jax.ShapeDtypeStruct((blocks, probes, count, width, lanes), BF16)
+
+
+SENT_GROUPS = 2
+SENT = ((8, 4), (12, 4), (16, 8))
+ANYWHERE = pl.BlockSpec(memory_space=pl.ANY)
 
 
 def ocean_rows_kernel(in_ref, mask_ref, out_ref, wide):
@@ -320,21 +364,14 @@
         return carry
 
     lax.fori_loop(0, bands, load, 0)
-    fwd = fwd_ref[...]
-    inv = inv_ref[...]
     filt = filt_ref[0]
-    chunk = 512
-
-    def lat_filter(t, carry):
-        at = pl.ds(pl.multiple_of(t * chunk, chunk), chunk)
+    for t in range(2):
+        at = slice(t * lons, (t + 1) * lons)
         value = wide[:, at]
-        filtered = (mm(fwd, value.astype(BF16)) * filt).astype(BF16)
-        returned = mm(inv, filtered)
+        filtered = (mm(fwd_ref[...], value.astype(BF16)) * filt).astype(BF16)
+        returned = mm(inv_ref[...], filtered)
         back[:, at] = returned.astype(BF16)
         wide[:, at] = value + returned
-        return carry
-
-    lax.fori_loop(0, 2 * lons // chunk, lat_filter, 0)
     for p in range(2):
         for t in range(lons // 256):
             at = slice(p * lons + t * 256, p * lons + (t + 1) * 256)
@@ -378,25 +415,51 @@
     )(received, fwd, inv, filt, diff)
 
 
+GROUP = 4
+
+
 def point_kernel(
+    sent,
     mixed_ref,
     slope_ref,
     win_ref,
     wout_ref,
     pflux_ref,
     cells_ref,
-    first_ref,
-    second_ref,
+    out_ref,
     picked_ref,
-    wide,
-    flux,
+    *rest,
 ):
+    back_refs = rest[:sent]
+    wide, flux, ship, home_sems = rest[sent:]
     chans, pair, lanes = mixed_ref.shape
     rows = pair // 2
     step = pl.program_id(0)
+    send, recv, own = home_sems
+    blocks = out_ref.shape[0]
+    block = lax.axis_index("chan")
+    peers = chan_peers(blocks)
+
+    def homeward_group(i):
+        copies = [
+            pltpu.make_async_remote_copy(
+                ship.at[i, where[1]],
+                back_refs[i].at[block],
+                send.at[i, k],
+                recv.at[i, k],
+                device_id=where,
+                device_id_type=MESH,
+            )
+            for k, where in enumerate(peers)
+        ]
+        return copies + [
+            pltpu.make_async_copy(ship.at[i, block], back_refs[i].at[block], own.at[i])
+        ]
 
     @pl.when(step == 0)
     def _():
+        greet((), peers)
+
         def load(i, carry):
             at = pl.ds(pl.multiple_of(i * 8, 8), 8)
             wide[pl.ds(pl.multiple_of(i * 8 * pair, 8), 8 * pair), :] = (
@@ -406,25 +469,40 @@
 
         lax.fori_loop(0, chans // 8, load, 0)
 
-    value = jnp.concatenate(
-        [wide[pl.ds(step + p * rows, chans, stride=pair), :] for p in range(2)], axis=1
-    ).astype(BF16)
-    slope = slope_ref[0].astype(F32)
-    hidden = mm(win_ref[...], value)
-    gated = (jnp.concatenate([slope, slope], axis=1) * hidden).astype(BF16)
-    update = mm(wout_ref[...], gated)
-    width = first_ref.shape[2]
-    for j in range(first_ref.shape[0]):
-        piece = update[j * width : (j + 1) * width].astype(BF16)
-        first_ref[j, 0] = piece[:, 0:lanes]
-        second_ref[j, 0] = piece[:, lanes : 2 * lanes]
-    terms = update[chans : chans + 8]
     which = lax.broadcasted_iota(jnp.int32, (8, lanes), 0)
-    flux[pl.ds(pl.multiple_of(step * 8, 8), 8), :] = jnp.where(
-        which < 4, terms[:, 0:lanes], terms[:, lanes : 2 * lanes]
-    )
-
-    @pl.when(step == rows - 1)
+    width = out_ref.shape[3]
+    gated = []
+    for g in range(GROUP):
+        value = jnp.concatenate(
+            [
+                wide[pl.ds(step * GROUP + g + p * rows, chans, stride=pair), :]
+                for p in range(2)
+            ],
+            axis=1,
+        ).astype(BF16)
+        slope = slope_ref[g].astype(F32)
+        hidden = mm(win_ref[...], value)
+        gated.append((jnp.concatenate([slope, slope], axis=1) * hidden).astype(BF16))
+    for g in range(GROUP):
+        update = mm(wout_ref[...], gated[g])
+        for j in range(blocks):
+            piece = update[j * width : (j + 1) * width].astype(BF16)
+            out_ref[j, 0, g] = piece[:, 0:lanes]
+            out_ref[j, 1, g] = piece[:, lanes : 2 * lanes]
+        terms = update[chans : chans + 8]
+        flux[pl.ds(pl.multiple_of((step * GROUP + g) * 8, 8), 8), :] = jnp.where(
+            which < 4, terms[:, 0:lanes], terms[:, lanes : 2 * lanes]
+        )
+
+    for i in range(sent):
+
+        @pl.when(step == i)
+        def _(i=i):
+            ship[i] = out_ref[...]
+            for copy in homeward_group(i):
+                copy.start()
+
+    @pl.when(step == rows // GROUP - 1)
     def _():
         total = flux[...]
         for j in range(pflux_ref.shape[0]):
@@ -440,73 +518,90 @@
             for n in range(rows):
                 picked = picked + jnp.where(row == n, found[n * 8 : (n + 1) * 8], 0.0)
             picked_ref[r] = picked
-
-
-def pointwise(mixed, slope, win, wout, pflux, cells, blocks):
+        for i in range(sent):
+            for copy in homeward_group(i):
+                copy.wait()
+
+
+def pointwise(mixed, slope, win, wout, pflux, cells, blocks, sent):
     chans, pair, lanes = mixed.shape
     rows, hid, _ = slope.shape
     width = chans // blocks
+    shipped = (sent, blocks, 2, GROUP, width, lanes)
     return pl.pallas_call(
-        point_kernel,
-        grid=(rows,),
+        functools.partial(point_kernel, sent),
+        grid=(rows // GROUP,),
         in_specs=[
             whole(mixed.shape),
-            pl.BlockSpec((1, hid, lanes), lambda i: (i, 0, 0)),
+            pl.BlockSpec((GROUP, hid, lanes), lambda i: (i, 0, 0)),
             whole(win.shape),
             whole(wout.shape),
             whole(pflux.shape),
             whole(cells.shape),
         ],
         out_specs=[
-            pl.BlockSpec((blocks, 1, width, lanes), lambda i: (0, i, 0, 0)),
-            pl.BlockSpec((blocks, 1, width, lanes), lambda i: (0, i, 0, 0)),
+            pl.BlockSpec((blocks, 2, GROUP, width, lanes), lambda i: (0, 0, i, 0, 0)),
             whole((cells.shape[0], 8, lanes)),
-        ],
+        ]
+        + [ANYWHERE] * sent,
         out_shape=[
-            jax.ShapeDtypeStruct((blocks, rows, width, lanes), BF16),
-            jax.ShapeDtypeStruct((blocks, rows, width, lanes), BF16),
+            jax.ShapeDtypeStruct((blocks, 2, rows, width, lanes), BF16),
             jax.ShapeDtypeStruct((cells.shape[0], 8, lanes), F32),
-        ],
+        ]
+        + [jax.ShapeDtypeStruct(shipped[1:], BF16)] * sent,
         scratch_shapes=[
             pltpu.VMEM((chans * pair, lanes), F32),
             pltpu.VMEM((rows * 8, lanes), F32),
-        ],
-        compiler_params=params(),
+            pltpu.VMEM(shipped, BF16),
+            [
+                pltpu.SemaphoreType.DMA((sent, blocks - 1)),
+                pltpu.SemaphoreType.DMA((sent, blocks - 1)),
+                pltpu.SemaphoreType.DMA((sent,)),
+            ],
+        ],
+        compiler_params=params(collective_id=6, has_side_effects=True),
         cost_estimate=cost(7.3e9, 4 * mixed.size + 2 * slope.size),
         name="pointwise",
     )(mixed, slope, win, wout, pflux, cells)
 
 
-def add_kernel(probe_ref, update_ref, *rest):
-    out_ref = rest[-1]
-    for j in range(update_ref.shape[0]):
-        cols = slice(j * 128, (j + 1) * 128)
-        out_ref[:, :, cols] = (
-            probe_ref[:, :, cols].astype(F32) + update_ref[j].astype(F32)
-        ).astype(BF16)
-
-
-def add_update(probe, update, p, partial=None):
-    rows, chans, lons = probe.shape
-    blocks, count = update.shape[0], update.shape[1]
-    step = 6
-    base = p * (count // step)
-    rest = () if partial is None else (partial,)
+def add_kernel(starts, probe_ref, *refs):
+    out_ref = refs[-1]
+    step = pl.program_id(1)
+    for k, update_ref in enumerate(refs[:-1]):
+
+        @pl.when((step >= starts[k]) & (step < starts[k + 1]))
+        def _(update_ref=update_ref):
+            for j in range(update_ref.shape[0]):
+                cols = slice(j * 128, (j + 1) * 128)
+                out_ref[:, :, cols] = probe_ref[:, :, cols] + update_ref[j, 0]
+
+
+def add_update(probe, parts):
+    lines, chans, lons = probe.shape
+    blocks = parts[0].shape[0]
+    rows = lines // 2
+    step = 4
+    counts = [a.shape[2] // step for a in parts]
+    starts = [sum(counts[:k]) for k in range(len(counts) + 1)]
+
+    def spec(k):
+        return pl.BlockSpec(
+            (blocks, 1, step, chans, 128),
+            lambda p, i: (0, p, jnp.clip(i - starts[k], 0, counts[k] - 1), 0, 0),
+        )
+
+    field = pl.BlockSpec((step, chans, lons), lambda p, i: (p * (rows // step) + i, 0, 0))
     return pl.pallas_call(
-        add_kernel,
-        grid=(count // step,),
-        in_specs=[
-            pl.BlockSpec((step, chans, lons), lambda i: (base + i, 0, 0)),
-            pl.BlockSpec((blocks, step, chans, 128), lambda i: (0, i, 0, 0)),
-        ]
-        + [pl.BlockSpec(memory_space=pl.ANY) for _ in rest],
-        out_specs=pl.BlockSpec((step, chans, lons), lambda i: (base + i, 0, 0)),
+        functools.partial(add_kernel, starts),
+        grid=(2, rows // step),
+        in_specs=[field] + [spec(k) for k in range(len(parts))],
+        out_specs=field,
         out_shape=jax.ShapeDtypeStruct(probe.shape, BF16),
-        input_output_aliases={2: 0} if rest else {},
         compiler_params=params(),
-        cost_estimate=cost(update.size, 6 * update.size),
+        cost_estimate=cost(probe.size, 6 * probe.size),
         name="add_update",
-    )(probe, update, *rest)
+    )(probe, *parts)
 
 
 def depth_sum(first, taps_ref, wide, done):
@@ -576,7 +671,21 @@
 
 
 def flux_kernel(
-    blocks, picked_ref, slots_ref, weights_ref, mask_ref, out_ref, pool_ref, tall, send, recv, edge
+    rows_sent,
+    blocks,
+    picked_ref,
+    slots_ref,
+    weights_ref,
+    mask_ref,
+    update_ref,
+    out_ref,
+    back_ref,
+    pool_ref,
+    tall,
+    send,
+    recv,
+    edge,
+    home_sems,
 ):
     bands, fields, cap = picked_ref.shape
     rows, cols = mask_ref.shape
@@ -585,7 +694,7 @@
     tall[...] = jnp.zeros_like(tall)
     pool_ref[pl.ds(band, 1)] = picked_ref[pl.ds(band, 1)]
     others = [(lax.rem(band + k, bands), block) for k in range(1, bands)]
-    greet((chan_before, chan_after), others)
+    greet((), others + chan_peers(blocks))
 
     copies = []
     for k, where in enumerate(others):
@@ -599,6 +708,9 @@
         )
         copy.start()
         copies.append(copy)
+    home = homeward(update_ref, back_ref, rows_sent[0], home_sems)
+    for copy in home:
+        copy.start()
     for copy in copies:
         copy.wait()
 
@@ -639,75 +751,34 @@
         tall.at[:, :, pl.ds(0, 128)],
     )
     out_ref[...] = tall[...]
-
-
-def flux_tile(picked, slots, weights, mask, blocks):
+    for copy in home:
+        copy.wait()
+
+
+def flux_tile(picked, slots, weights, mask, update, rows_sent):
     bands, fields, _ = picked.shape
+    blocks = update.shape[0]
     rows, cols = mask.shape
     shape = (rows + 6, fields, cols + 256)
     return pl.pallas_call(
-        functools.partial(flux_kernel, blocks),
-        in_specs=[whole(a.shape) for a in (picked, slots, weights, mask)],
-        out_specs=whole(shape),
-        out_shape=jax.ShapeDtypeStruct(shape, F32),
+        functools.partial(flux_kernel, rows_sent, blocks),
+        in_specs=[whole(a.shape) for a in (picked, slots, weights, mask)] + [ANYWHERE],
+        out_specs=[whole(shape), ANYWHERE],
+        out_shape=[
+            jax.ShapeDtypeStruct(shape, F32),
+            homeward_shape(update, rows_sent[1]),
+        ],
         scratch_shapes=[
             pltpu.VMEM(picked.shape, F32),
             pltpu.VMEM(shape, F32),
             pltpu.SemaphoreType.DMA((bands - 1,)),
             pltpu.SemaphoreType.DMA((bands - 1,)),
             pltpu.SemaphoreType.DMA((2, 4)),
+            homeward_sems(blocks),
         ],
         compiler_params=params(collective_id=1, has_side_effects=True),
         name="flux_tile",
-    )(picked, slots, weights, mask)
-
-
-def edge_kernel(bands, blocks, field_ref, out_ref, tall, edge, own):
-    lines, _, cols, _ = field_ref.shape
-    lat_before, lat_after, chan_before, chan_after = neighbours(bands, blocks)
-    tall[...] = jnp.zeros_like(tall)
-    greet((lat_before, lat_after, chan_before, chan_after))
-    inner = pl.ds(16, cols)
-    copy = pltpu.make_async_copy(field_ref, tall.at[pl.ds(3, lines), :, inner, :], own)
-    copy.start()
-    swap_edges(
-        field_ref.at[pl.ds(0, 3)],
-        field_ref.at[pl.ds(lines - 3, 3)],
-        edge.at[0],
-        lat_before,
-        lat_after,
-        tall.at[pl.ds(lines + 3, 3), :, inner, :],
-        tall.at[pl.ds(0, 3), :, inner, :],
-    )
-    copy.wait()
-    swap_edges(
-        tall.at[:, :, pl.ds(16, 16), :],
-        tall.at[:, :, pl.ds(cols, 16), :],
-        edge.at[1],
-        chan_before,
-        chan_after,
-        tall.at[:, :, pl.ds(16 + cols, 16), :],
-        tall.at[:, :, pl.ds(0, 16), :],
-    )
-    out_ref[...] = tall[...]
-
-
-def coarse_edges(field, bands, blocks):
-    lines, probes, cols, chans = field.shape
-    shape = (lines + 6, probes, cols + 32, chans)
-    return pl.pallas_call(
-        functools.partial(edge_kernel, bands, blocks),
-        in_specs=[whole(field.shape)],
-        out_specs=whole(shape),
-        out_shape=jax.ShapeDtypeStruct(shape, BF16),
-        scratch_shapes=[
-            pltpu.VMEM(shape, BF16),
-            pltpu.SemaphoreType.DMA((2, 4)),
-            pltpu.SemaphoreType.DMA,
-        ],
-        compiler_params=params(collective_id=2, has_side_effects=True),
-        name="coarse_edges",
-    )(field)
+    )(picked, slots, weights, mask, update)
 
 
 def normed_step(spread, base, sigma, gain):
@@ -719,7 +790,33 @@
     return (gain * scale * (spread - center - wide_base * along)).astype(BF16)
 
 
+def row_edges(bands, blocks, line, lines, rows_ref, edges_ref, sems):
+    before, after, _, _ = neighbours(bands, blocks)
+    pairs = []
+    if line < 3:
+        pairs.append((before, 3 + line, after))
+    if line >= lines - 3:
+        pairs.append((after, line - (lines - 3), before))
+    return [
+        (
+            there,
+            comes[0],
+            pltpu.make_async_remote_copy(
+                rows_ref.at[line],
+                edges_ref.at[slot],
+                sems.at[0, slot],
+                sems.at[1, slot],
+                device_id=where,
+                device_id_type=MESH,
+            ),
+        )
+        for (there, where), slot, comes in pairs
+    ]
+
+
 def fine_kernel(
+    bands,
+    rows_sent,
     spread_ref,
     probe_ref,
     flux_ref,
@@ -735,69 +832,133 @@
     pool_ref,
     down_ref,
     turn_ref,
+    update_ref,
     one_ref,
     coarse_ref,
     turned_ref,
+    edges_ref,
+    back_ref,
     columns,
     held,
+    edge_sems,
+    home_sems,
 ):
     step = pl.program_id(0)
+    blocks = back_ref.shape[0]
+    lines = held.shape[0]
+    home = homeward(update_ref, back_ref, rows_sent[0], home_sems)
     high = flux_ref.shape[0]
     cols = flux_ref.shape[2] - 256
 
     @pl.when(step == 0)
     def _():
+        before, after, _, _ = neighbours(bands, blocks)
+        greet((before, after), chan_peers(blocks))
+        for copy in home:
+            copy.start()
         for y in range(high):
             row = flux_ref[y]
             for b in range(7):
                 columns[(y * 7 + b) * 8 : (y * 7 + b + 1) * 8, :] = row[:, 125 + b : 125 + b + cols]
 
-    near = columns[pl.ds(pl.multiple_of(step * 56, 8), 392), :].astype(BF16)
-    center = columns[pl.ds(pl.multiple_of((step + 3) * 56 + 24, 8), 8), :].astype(BF16)
-    spread = spread_ref[0] + jnp.concatenate([mm(mix_ref[p], near) for p in range(2)], axis=1)
-    forcing = jnp.concatenate([mm(couple_ref[p], center) for p in range(2)], axis=1)
-    probe = jnp.concatenate([probe_ref[0, 0], probe_ref[0, 1]], axis=1).astype(F32)
-    start = (probe + forcing).astype(BF16).astype(F32)
-    at = pl.ds(step, 1)
-    tangent = normed_step(spread, base_ref[0].astype(F32), sigma_ref[at, :], gain_ref[...])
-    slope = slope_ref[0].astype(F32)
-    hidden = mm(expand_ref[...], tangent)
-    gated = (hidden * jnp.concatenate([slope, slope], axis=1)).astype(BF16)
-    mask = mask_ref[at, :]
-    one = ((start + mm(shrink_ref[...], gated)) * jnp.concatenate([mask, mask], axis=1)).astype(BF16)
-    one_ref[0] = one
-    pooled = mm(one, pool_ref[...])
-
-    @pl.when(step % 2 == 0)
+    pooled = []
+    for h in range(2):
+        y = step * 2 + h
+        near = columns[pl.ds(pl.multiple_of(y * 56, 8), 392), :].astype(BF16)
+        center = columns[pl.ds(pl.multiple_of((y + 3) * 56 + 24, 8), 8), :].astype(BF16)
+        spread = spread_ref[h] + jnp.concatenate(
+            [mm(mix_ref[p], near) for p in range(2)], axis=1
+        )
+        forcing = jnp.concatenate([mm(couple_ref[p], center) for p in range(2)], axis=1)
+        probe = jnp.concatenate([probe_ref[h, 0], probe_ref[h, 1]], axis=1).astype(F32)
+        start = (probe + forcing).astype(BF16).astype(F32)
+        at = pl.ds(y, 1)
+        tangent = normed_step(spread, base_ref[h].astype(F32), sigma_ref[at, :], gain_ref[...])
+        slope = slope_ref[h].astype(F32)
+        hidden = mm(expand_ref[...], tangent)
+        gated = (hidden * jnp.concatenate([slope, slope], axis=1)).astype(BF16)
+        mask = mask_ref[at, :]
+        one = (
+            (start + mm(shrink_ref[...], gated)) * jnp.concatenate([mask, mask], axis=1)
+        ).astype(BF16)
+        one_ref[h] = one
+        pooled.append(mm(one, pool_ref[...]))
+
+    both = (pooled[0] + pooled[1]).astype(BF16)
+    coarse_ref[0] = mm(down_ref[...], both).astype(BF16)
+    turned = mm(both.T, turn_ref[...]).astype(BF16)
+    half = turned.shape[0] // 2
+    turned_ref[0, 0] = turned[0:half]
+    turned_ref[0, 1] = turned[half : 2 * half]
+    for line in range(lines):
+
+        @pl.when(step == line)
+        def _(line=line):
+            held[line] = turned_ref[0]
+            for there, _, copy in row_edges(
+                bands, blocks, line, lines, held, edges_ref, edge_sems
+            ):
+
+                @pl.when(there)
+                def _(copy=copy):
+                    copy.start()
+
+    @pl.when(step == lines - 1)
     def _():
-        held[...] = pooled
-
-    @pl.when(step % 2 == 1)
-    def _():
-        both = (held[...] + pooled).astype(BF16)
-        coarse_ref[0] = mm(down_ref[...], both).astype(BF16)
-        turned = mm(both.T, turn_ref[...]).astype(BF16)
-        half = turned.shape[0] // 2
-        turned_ref[0, 0] = turned[0:half]
-        turned_ref[0, 1] = turned[half : 2 * half]
-
-
-def fine_level(spread, probe, flux, mask, sigma, base, slope, gain, mix, couple, expand, shrink, pool, down, turn):
+        for line in range(lines):
+            for there, comes, copy in row_edges(
+                bands, blocks, line, lines, held, edges_ref, edge_sems
+            ):
+
+                @pl.when(there)
+                def _(copy=copy):
+                    copy.wait_send()
+
+                @pl.when(comes)
+                def _(copy=copy):
+                    copy.wait_recv()
+
+        for copy in home:
+            copy.wait()
+
+
+def fine_level(
+    spread,
+    probe,
+    flux,
+    mask,
+    sigma,
+    base,
+    slope,
+    gain,
+    mix,
+    couple,
+    expand,
+    shrink,
+    pool,
+    down,
+    turn,
+    update,
+    bands,
+    rows_sent,
+):
     rows, chans, wide = spread.shape
     cols = wide // 2
     coarse = down.shape[0]
+    lines = rows // 2
+    turned = (2, cols // 2, turn.shape[1])
     row = lambda i: (i, 0, 0)
     return pl.pallas_call(
-        fine_kernel,
-        grid=(rows,),
+        functools.partial(fine_kernel, bands, rows_sent),
+        grid=(lines,),
         in_specs=[
-            pl.BlockSpec((1, chans, wide), row),
-            pl.BlockSpec((1,) + probe.shape[1:], lambda i: (i, 0, 0, 0)),
+            pl.BlockSpec((2, chans, wide), row),
+            pl.BlockSpec((2,) + probe.shape[1:], lambda i: (i, 0, 0, 0)),
             whole(flux.shape),
             whole(mask.shape),
             whole(sigma.shape),
-            pl.BlockSpec((1, chans, cols), row),
-            pl.BlockSpec((1, slope.shape[1], cols), row),
+            pl.BlockSpec((2, chans, cols), row),
+            pl.BlockSpec((2, slope.shape[1], cols), row),
             whole(gain.shape),
             whole(mix.shape),
             whole(couple.shape),
@@ -806,28 +967,55 @@
             whole(pool.shape),
             whole(down.shape),
             whole(turn.shape),
+            ANYWHERE,
         ],
         out_specs=[
-            pl.BlockSpec((1, chans, wide), row),
-            pl.BlockSpec((1, coarse, cols), lambda i: (i // 2, 0, 0)),
-            pl.BlockSpec((1, 2, cols // 2, turn.shape[1]), lambda i: (i // 2, 0, 0, 0)),
+            pl.BlockSpec((2, chans, wide), row),
+            pl.BlockSpec((1, coarse, cols), row),
+            pl.BlockSpec((1,) + turned, lambda i: (i, 0, 0, 0)),
+            ANYWHERE,
+            ANYWHERE,
         ],
         out_shape=[
             jax.ShapeDtypeStruct((rows, chans, wide), BF16),
-            jax.ShapeDtypeStruct((rows // 2, coarse, cols), BF16),
-            jax.ShapeDtypeStruct((rows // 2, 2, cols // 2, turn.shape[1]), BF16),
+            jax.ShapeDtypeStruct((lines, coarse, cols), BF16),
+            jax.ShapeDtypeStruct((lines,) + turned, BF16),
+            jax.ShapeDtypeStruct((6,) + turned, BF16),
+            homeward_shape(update, rows_sent[1]),
         ],
         scratch_shapes=[
             pltpu.VMEM((flux.shape[0] * 56, cols), F32),
-            pltpu.VMEM((chans, cols), F32),
-        ],
-        compiler_params=params(),
+            pltpu.VMEM((lines,) + turned, BF16),
+            pltpu.SemaphoreType.DMA((2, 6)),
+            homeward_sems(update.shape[0]),
+        ],
+        compiler_params=params(collective_id=4, has_side_effects=True),
         name="fine_level",
-    )(spread, probe, flux, mask, sigma, base, slope, gain, mix, couple, expand, shrink, pool, down, turn)
+    )(
+        spread,
+        probe,
+        flux,
+        mask,
+        sigma,
+        base,
+        slope,
+        gain,
+        mix,
+        couple,
+        expand,
+        shrink,
+        pool,
+        down,
+        turn,
+        update,
+    )
 
 
 def coarse_kernel(
-    around_ref,
+    bands,
+    rows_sent,
+    turned_ref,
+    edges_ref,
     taps_ref,
     field_ref,
     sigma_ref,
@@ -840,95 +1028,135 @@
     up_ref,
     one_ref,
     mask_ref,
+    update_ref,
     out_ref,
+    back_ref,
+    around,
     wide,
     tall,
     done,
     spread,
+    edge,
+    home_sems,
 ):
-    step = pl.program_id(0)
-    chans = field_ref.shape[1]
+    blocks = back_ref.shape[0]
+    home = homeward(update_ref, back_ref, rows_sent[0], home_sems)
+    lines, chans, _ = field_ref.shape
     probes, fine, rows, cols = out_ref.shape
-
-    @pl.when(step == 0)
+    half = cols // 2
+    before, after, chan_before, chan_after = neighbours(bands, blocks)
+    inner = slice(16, 16 + half)
+    around[...] = jnp.zeros_like(around)
+    around[3 : 3 + lines, :, inner, :] = turned_ref[...]
+
+    @pl.when(before[0])
     def _():
-        half = done.shape[1]
-        for p in range(probes):
-            for y in range(tall.shape[1]):
-                for h in range(tall.shape[0]):
-                    top = min(128, chans - h * 128)
-                    tall[h, y, :, 0:top] = around_ref[y, p, :, h * 128 : h * 128 + top].astype(F32)
-            depth_sum(13, taps_ref, tall, done)
-            for y in range(done.shape[0]):
-                spread[y, :, p * half : (p + 1) * half] = done[y].T[0:chans]
-
-    at = pl.ds(step, 1)
-    tangent = normed_step(
-        spread[step], base_ref[0].astype(F32), sigma_ref[at, :], gain_ref[...]
-    )
-    slope = slope_ref[0].astype(F32)
-    hidden = mm(expand_ref[...], tangent)
-    gated = (hidden * jnp.concatenate([slope, slope], axis=1)).astype(BF16)
-    two = (field_ref[0].astype(F32) + mm(shrink_ref[...], gated)).astype(BF16)
-    raised = mm(up_ref[...], mm(two, spreadout_ref[...]).astype(BF16))
-    for half in range(2):
-        y = step * 2 + half
-        mask = mask_ref[pl.ds(y, 1), :]
-        for p in range(probes):
-            for t in range(cols // 128):
-                lanes = slice(p * cols + t * 128, p * cols + (t + 1) * 128)
-                wide[p, t, pl.ds(y, fine, stride=rows), :] = (
-                    one_ref[half, :, lanes].astype(F32) + raised[:, lanes]
-                ) * mask[:, t * 128 : (t + 1) * 128]
-
-    @pl.when(step == rows // 2 - 1)
+        around[0:3, :, inner, :] = edges_ref[0:3]
+
+    @pl.when(after[0])
     def _():
-        for p in range(probes):
-            for t in range(cols // 128):
-                out_ref[p, :, :, t * 128 : (t + 1) * 128] = (
-                    wide[p, t].reshape(fine, rows, 128).astype(BF16)
-                )
+        around[3 + lines : 6 + lines, :, inner, :] = edges_ref[3:6]
+
+    greet((), chan_peers(blocks))
+    finish = start_edges(
+        around.at[:, :, pl.ds(16, 16), :],
+        around.at[:, :, pl.ds(half, 16), :],
+        edge,
+        chan_before,
+        chan_after,
+        around.at[:, :, pl.ds(16 + half, 16), :],
+        around.at[:, :, pl.ds(0, 16), :],
+    )
+    for copy in home:
+        copy.start()
+    finish()
+    for p in range(probes):
+        for y in range(tall.shape[1]):
+            for h in range(tall.shape[0]):
+                lanes = slice(h * 128, (h + 1) * 128)
+                tall[h, y] = around[y, p, :, lanes].astype(F32)
+        depth_sum(13, taps_ref, tall, done)
+        for y in range(lines):
+            spread[y, :, p * half : (p + 1) * half] = done[y].T[0:chans]
+
+    gated = []
+    for y in range(lines):
+        tangent = normed_step(
+            spread[y], base_ref[y].astype(F32), sigma_ref[y : y + 1, :], gain_ref[...]
+        )
+        slope = slope_ref[y].astype(F32)
+        hidden = mm(expand_ref[...], tangent)
+        gated.append((hidden * jnp.concatenate([slope, slope], axis=1)).astype(BF16))
+    for y in range(lines):
+        two = (field_ref[y].astype(F32) + mm(shrink_ref[...], gated[y])).astype(BF16)
+        raised = mm(up_ref[...], mm(two, spreadout_ref[...]).astype(BF16))
+        for h in range(2):
+            line = y * 2 + h
+            mask = mask_ref[line : line + 1, :]
+            for p in range(probes):
+                for t in range(cols // 128):
+                    lanes = slice(p * cols + t * 128, p * cols + (t + 1) * 128)
+                    wide[p, t, pl.ds(line, fine, stride=rows), :] = (
+                        one_ref[line, :, lanes].astype(F32) + raised[:, lanes]
+                    ) * mask[:, t * 128 : (t + 1) * 128]
+    for p in range(probes):
+        for t in range(cols // 128):
+            out_ref[p, :, :, t * 128 : (t + 1) * 128] = (
+                wide[p, t].reshape(fine, rows, 128).astype(BF16)
+            )
+    for copy in home:
+        copy.wait()
 
 
 def coarse_level(
-    around, kernel, field, sigma, base, slope, gain, expand, shrink, spreadout, up, one, mask
+    turned,
+    edges,
+    taps,
+    field,
+    sigma,
+    base,
+    slope,
+    gain,
+    expand,
+    shrink,
+    spreadout,
+    up,
+    one,
+    mask,
+    update,
+    bands,
+    rows_sent,
 ):
     lines, chans, double = field.shape
     half = double // 2
-    rows, fine, wide = one.shape
-    cols = wide // 2
-    taps = tap_rows(kernel)
-    row = lambda i: (i, 0, 0)
+    rows, fine, _ = one.shape
+    cols = double
+    high = lines + 6
+    operands = (
+        (turned, edges, taps, field, sigma, base, slope, gain)
+        + (expand, shrink, spreadout, up, one, mask)
+    )
     return pl.pallas_call(
-        coarse_kernel,
-        grid=(lines,),
-        in_specs=[
-            whole(around.shape),
-            whole(taps.shape),
-            pl.BlockSpec((1, chans, double), row),
-            whole(sigma.shape),
-            pl.BlockSpec((1, chans, half), row),
-            pl.BlockSpec((1, slope.shape[1], half), row),
-            whole(gain.shape),
-            whole(expand.shape),
-            whole(shrink.shape),
-            whole(spreadout.shape),
-            whole(up.shape),
-            pl.BlockSpec((2, fine, wide), row),
-            whole(mask.shape),
-        ],
-        out_specs=whole((2, fine, rows, cols)),
-        out_shape=jax.ShapeDtypeStruct((2, fine, rows, cols), BF16),
+        functools.partial(coarse_kernel, bands, rows_sent),
+        in_specs=[whole(a.shape) for a in operands] + [ANYWHERE],
+        out_specs=[whole((2, fine, rows, cols)), ANYWHERE],
+        out_shape=[
+            jax.ShapeDtypeStruct((2, fine, rows, cols), BF16),
+            homeward_shape(update, rows_sent[1]),
+        ],
         scratch_shapes=[
+            pltpu.VMEM((high, 2, half + 32, taps.shape[1]), BF16),
             pltpu.VMEM((2, cols // 128, fine * rows, 128), F32),
-            pltpu.VMEM((taps.shape[1] // 128, around.shape[0], around.shape[2], 128), F32),
+            pltpu.VMEM((taps.shape[1] // 128, high, half + 32, 128), F32),
             pltpu.VMEM((lines, half, taps.shape[1]), F32),
             pltpu.VMEM((lines, chans, double), F32),
-        ],
-        compiler_params=params(),
+            pltpu.SemaphoreType.DMA((4,)),
+            homeward_sems(update.shape[0]),
+        ],
+        compiler_params=params(collective_id=5, has_side_effects=True),
         cost_estimate=cost(1e9, 4e6),
         name="coarse_level",
-    )(around, taps, field, sigma, base, slope, gain, expand, shrink, spreadout, up, one, mask)
+    )(*operands, update)
 
 
 def local(
@@ -1032,9 +1260,10 @@
     wout = jnp.concatenate([weight_out, folded, folded], axis=1).T
     probe_terms = lax.psum_scatter(terms, "chan", scatter_dimension=0, tiled=True)
     spread = depthwise(around, kernel_fine)
-    (
-        regrouped,
+    early = (
         spread,
+        start,
+        mask,
         win,
         wout,
         probe_terms,
@@ -1042,44 +1271,6 @@
         slope_rows,
         base_lines,
         slope_lines,
-        mix,
-        couple,
-        pool,
-        spreadout,
-        mask,
-    ) = lax.optimization_barrier(
-        (
-            regrouped,
-            spread,
-            win,
-            wout,
-            probe_terms,
-            base_rows,
-            slope_rows,
-            base_lines,
-            slope_lines,
-            mix,
-            couple,
-            pool,
-            spreadout,
-            mask,
-        )
-    )
-    first, second, picked = pointwise(
-        regrouped, gate_slope, win, wout, probe_terms, send_cells[0], blocks
-    )
-
-    tall = flux_tile(picked, recv_slots[0], recv_weights[0], mask, blocks)
-    first, tall = lax.optimization_barrier((first, tall))
-    first = lax.all_to_all(first, "chan", split_axis=0, concat_axis=0, tiled=True)
-    one, coarse, turned = fine_level(
-        spread,
-        start,
-        tall,
-        mask,
-        sigma_fine,
-        base_rows,
-        slope_rows,
         gain_fine[:, None],
         mix,
         couple,
@@ -1088,27 +1279,92 @@
         pool,
         down_proj.T,
         jnp.pad(down_proj, ((0, 0), (0, 256 - down_proj.shape[1]))),
-    )
-    around = coarse_edges(turned, bands, blocks)
-    second, around = lax.optimization_barrier((second, around))
-    second = lax.all_to_all(second, "chan", split_axis=0, concat_axis=0, tiled=True)
-    ocean_out = coarse_level(
-        around,
-        kernel_coarse,
-        coarse,
-        sigma_coarse,
-        base_lines,
-        slope_lines,
+        tap_rows(kernel_coarse),
         gain_coarse[:, None],
         expand_coarse.T,
         shrink_coarse.T,
         spreadout,
         up_proj.T,
+        send_cells[0],
+        recv_slots[0],
+        recv_weights[0],
+    )
+    regrouped, early = lax.optimization_barrier((regrouped, early))
+    (
+        spread,
+        start,
+        mask,
+        win,
+        wout,
+        probe_terms,
+        base_rows,
+        slope_rows,
+        base_lines,
+        slope_lines,
+        gain_one,
+        mix,
+        couple,
+        expand_one,
+        shrink_one,
+        pool,
+        down,
+        turn,
+        taps,
+        gain_two,
+        expand_two,
+        shrink_two,
+        spreadout,
+        raise_two,
+        cells,
+        slots,
+        weights,
+    ) = early
+    update, picked, *shipped = pointwise(
+        regrouped, gate_slope, win, wout, probe_terms, cells, blocks, SENT_GROUPS
+    )
+
+    tall, back0 = flux_tile(picked, slots, weights, mask, update, SENT[0])
+    one, coarse, turned, edges, back1 = fine_level(
+        spread,
+        start,
+        tall,
+        mask,
+        sigma_fine,
+        base_rows,
+        slope_rows,
+        gain_one,
+        mix,
+        couple,
+        expand_one,
+        shrink_one,
+        pool,
+        down,
+        turn,
+        update,
+        bands,
+        SENT[1],
+    )
+    ocean_out, back2 = coarse_level(
+        turned,
+        edges,
+        taps,
+        coarse,
+        sigma_coarse,
+        base_lines,
+        slope_lines,
+        gain_two,
+        expand_two,
+        shrink_two,
+        spreadout,
+        raise_two,
         one,
         mask,
-    )
-    partial = add_update(flat_probe, first, 0)
-    atmos_out = add_update(flat_probe, second, 1, partial).reshape(probe_field.shape)
+        update,
+        bands,
+        SENT[2],
+    )
+    parts = (*shipped, back0, back1, back2)
+    atmos_out = add_update(flat_probe, parts).reshape(probe_field.shape)
     return (atmos_out, ocean_out)
 
 

time: 315 us -> 295 us (0.937); the launches traced: 314 us -> 290 us
  starting transfers between devices: 23.1 us -> 8.91 us
  waiting for transfers between devices: 16.6 us -> 3.23 us
    all_to_all x2 -> x0, starting transfers between devices: 14.2 us -> none  [the longest x1 7.31 us: local(): lax.all_to_all(second, 'chan', split_axis=0, concat_axis=0, tiled=True)]
    all_to_all x2 -> x0, waiting for transfers between devices: 8.19 us -> none  [the longest x1 8.19 us: local(): lax.all_to_all(second, 'chan', split_axis=0, concat_axis=0, tiled=True)]
    pallas_call x7 -> x5, Pallas kernels: 101 us -> 107 us  [the longest x1 29.2 us: pointwise(): pl.pallas_call(functools.partial(point_kernel, sent), grid=(rows // GROUP...]
    reduce_scatter x1, waiting for transfers between devices: 8.37 us -> 3.21 us  [local(): lax.psum_scatter(terms, 'chan', scatter_dimension=0, tiled=True)]
    pallas_call x1, Pallas kernels: 18.8 us -> 15.3 us  [lat_filter(): pl.pallas_call(filter_kernel, grid=(chans,), in_specs=[pl.BlockSpec((band...]
    unnamed x46 -> x49, local copies, waits for them, and re-layouts: 9.92 us -> 10.5 us
  transfers between devices with their start and end apart: 4 -> 2, of which waited for: 2 -> 1; matrix products, arithmetic and copies ran while one was open for 8% -> 9% of each run, Pallas kernels for 26% -> 11%
where the time goes in v4:
time: 295 us; the launch traced here: 290 us
  Pallas kernels  232 us (79%)
  local copies, waits for them, and re-layouts  25.5 us (9%)
  between operations  14.2 us (5%)
  starting transfers between devices  8.91 us (3%)
  other arithmetic  5.39 us (2%)
  waiting for transfers between devices  3.23 us (1%)
    pallas_call x1, Pallas kernels, open_exchange(): pl.pallas_call(functools.partial(open_kernel, blocks), in_specs=[any_spec...  74.3 us
    pallas_call x1, Pallas kernels, pointwise(): pl.pallas_call(functools.partial(point_kernel, sent), grid=(rows // GROUP...  29.2 us
    pallas_call x1, Pallas kernels, depthwise(): pl.pallas_call(depth_kernel, grid=(probes,), in_specs=[pl.BlockSpec((high...  26.9 us
    pallas_call x1, Pallas kernels, coarse_level(): pl.pallas_call(functools.partial(coarse_kernel, bands, rows_sent), in_spe...  25 us
    pallas_call x1, Pallas kernels, fine_level(): pl.pallas_call(functools.partial(fine_kernel, bands, rows_sent), grid=(li...  24 us
    pallas_call x1, Pallas kernels, flux_tile(): pl.pallas_call(functools.partial(flux_kernel, rows_sent, blocks), in_spec...  18.1 us
    pallas_call x1, Pallas kernels, lat_filter(): pl.pallas_call(filter_kernel, grid=(chans,), in_specs=[pl.BlockSpec((band...  15.3 us
    pallas_call x1, Pallas kernels, add_update(): pl.pallas_call(functools.partial(add_kernel, starts), grid=(2, rows // st...  10.7 us
  transfers between devices with their start and end apart: 2, of which 1 were waited for; matrix products, arithmetic and copies ran while one was open for 9% of the time, Pallas kernels for 11%

profile of v4, /device:TPU:32, one launch (start us, length us, event | category | flops | bytes accessed | tf_op | source)
XLA Modules:
  0.0 289.7 jit_solution(3643577760789575633)
XLA Ops:
  7.2 1.3 convert_element_type.29.mask_ref
  8.5 3.1 %ocean_rows.1.ocean_ref.probe_ref = bf16[8,2,200,256]{3,2,1,0:T(8,128)(2,1)} custom-call(bf16[2,200,8,256]{3,2,1,0:T(8,128)(2,1)} %in_ref.1, f32[8,256]{1,0:T(8,128)} %convert_element_type.29.mask_ref), custom_call_target="tpu_custom_call" | custom-call | flops 819200 | bytes 3276800 | tf_op jit(solution)/shard_map/ocean_rows/pallas_call | solution.py:182
  11.6 74.3 %open_exchange.1 = (bf16[16,3,48,1024]{3,2,1,0:T(8,128)(2,1)}, bf16[14,2,200,512]{3,2,1,0:T(8,128)(2,1)}) custom-call(bf16[48,48,1024]{2,1,0:T(8,128)(2,1)} %bitcast.54, bf16[8,2,200,256]{3,2,1,0:T(8,128)(2,1)} %ocean_rows.1.ocean_ref.probe_ref), custom_call_target="tpu_custom_call" | custom-call | bytes 9437184 | tf_op jit(solution)/shard_map/open_exchange/pallas_call | solution.py:295
  85.9 1.1 copy.61.filt_ref
  87.0 15.3 %lat_filter.1 = bf16[16,8,3,48,128]{4,3,2,1,0:T(8,128)(2,1)} custom-call(bf16[16,3,48,1024]{3,2,1,0:T(8,128)(2,1)} %get-tuple-element.48.in_ref, bf16[384,384]{1,0:T(8,128)(2,1)} %constant.50.clone.fwd_ref, bf16[384,384]{1,0:T(8,128)(2,1)} %constant.51.clone.inv_ref, f32[3,384,1]{2,1,0:T(8,128)} %copy.61.filt_ref, bf16[1024,1024]{1,0:T(8,128)(2,1)} %constant.49.clone.diff_ref), custom_call_target="tpu_custom_call" | custom-call | flops 8400000000 | bytes 9437184 | tf_op jit(solution)/shard_map/lat_filter/pallas_call | solution.py:399
  102.3 8.7 %all-to-all-start = ((bf16[128,3,48,128]{3,2,1,0:T(8,128)(2,1)}), bf16[128,3,48,128]{3,2,1,0:T(8,128)(2,1)}, u32[]{:S(2)}, u32[]{:S(2)}) async-start(bf16[128,3,48,128]{3,2,1,0:T(8,128)(2,1)} %bitcast.58), calls=%async_computation | async-start | bytes 9437184 | tf_op jit(solution)/shard_map/all_to_all | solution.py:1248
  112.0 5.5 %probe_flux.1 = bf16[8,192,128]{2,1,0:T(8,128)(2,1)} custom-call(bf16[2,24,48,1024]{3,2,1,0:T(8,128)(2,1)} %probe_ref.1, bf16[8,96]{1,0:T(8,128)(2,1)} %fusion.2.weight_ref), custom_call_target="tpu_custom_call" | custom-call | flops 37748736 | bytes 4718592 | tf_op jit(solution)/shard_map/probe_flux/pallas_call | solution.py:339
  117.5 1.1 copy.64
  123.2 2.4 copy.70
  125.5 1.9 copy.69
  127.5 2.5 copy.81
  129.9 1.3 reshape.94
  132.1 1.1 copy.63
  133.2 1.1 copy.82
  134.3 1.0 copy.83
  135.4 1.0 copy.73
  139.6 26.9 %depthwise.1.spread_ref = f32[8,200,512]{2,1,0:T(8,128)} custom-call(bf16[14,2,200,512]{3,2,1,0:T(8,128)(2,1)} %get-tuple-element.50.in_ref, f32[392,256]{1,0:T(8,128)} %broadcast_bitcast_fusion.3.taps_ref), custom_call_target="tpu_custom_call" | custom-call | flops 163840000 | bytes 11468800 | tf_op jit(solution)/shard_map/depthwise/pallas_call | solution.py:654
  169.0 3.2 %reduce-scatter.2.cloned.1.call-done.pflux_ref = bf16[1,192,128]{2,1,0:T(8,128)(2,1)} async-done(((bf16[8,192,128]{2,1,0:T(8,128)(2,1)}), bf16[1,192,128]{2,1,0:T(8,128)(2,1)}) %reduce-scatter.2.cloned.1.call-update) | async-done | bytes 49168 | tf_op jit(solution)/shard_map/reduce_scatter | solution.py:1261
  174.6 29.2 %pointwise.1 = (bf16[8,2,24,48,128]{4,3,2,1,0:T(8,128)(2,1)}, f32[16,8,128]{2,1,0:T(8,128)}, bf16[8,2,4,48,128]{4,3,2,1,0:T(8,128)(2,1)}, bf16[8,2,4,48,128]{4,3,2,1,0:T(8,128)(2,1)}) custom-call(bf16[384,48,128]{2,1,0:T(8,128)(2,1)} %bitcast.4.mixed_ref, bf16[24,768,128]{2,1,0:T(8,128)(2,1)} %slope_ref.1, bf16[768,384]{1,0:T(8,128)(2,1)} %bitcast.65, ...), custom_call_target="tpu_custom_call" | custom-call | flops 7299999744 | bytes 14155776 | tf_op jit(solution)/shard_map/pointwise/pallas_call | solution.py:531
  203.8 18.1 %flux_tile.1 = (f32[14,8,512]{2,1,0:T(8,128)}, bf16[8,2,4,48,128]{4,3,2,1,0:T(8,128)(2,1)}) custom-call(f32[16,8,128]{2,1,0:T(8,128)} %get-tuple-element.58.picked_ref, s32[4,2048]{1,0:T(4,128)} %bitcast.72, f32[4,2048]{1,0:T(4,128)} %bitcast.73, f32[8,256]{1,0:T(8,128)} %convert_element_type.29.mask_ref, ...), custom_call_target="tpu_custom_call" | custom-call | tf_op jit(solution)/shard_map/flux_tile/pallas_call | solution.py:763
  221.9 24.0 %fine_level.1 = (bf16[8,200,512]{2,1,0:T(8,128)(2,1)}, bf16[4,250,256]{2,1,0:T(8,128)(2,1)}, bf16[4,2,128,256]{3,2,1,0:T(8,128)(2,1)}, bf16[6,2,128,256]{3,2,1,0:T(8,128)(2,1)}, bf16[8,2,4,48,128]{4,3,2,1,0:T(8,128)(2,1)}) custom-call(f32[8,200,512]{2,1,0:T(8,128)} %depthwise.1.spread_ref, bf16[8,2,200,256]{3,2,1,0:T(8,128)(2,1)} %ocean_rows.1.ocean_ref.probe_ref, ...), custom_call_target="tpu_custom_call" | custom-call | tf_op jit(solution)/shard_map/fine_level/pallas_call | solution.py:951
  245.9 25.0 %coarse_level.1 = (bf16[2,200,8,256]{3,2,1,0:T(8,128)(2,1)}, bf16[8,2,8,48,128]{4,3,2,1,0:T(8,128)(2,1)}) custom-call(bf16[4,2,128,256]{3,2,1,0:T(8,128)(2,1)} %get-tuple-element.78.turned_ref, bf16[6,2,128,256]{3,2,1,0:T(8,128)(2,1)} %get-tuple-element.79.edges_ref, f32[392,256]{1,0:T(8,128)} %broadcast_bitcast_fusion.1.taps_ref, ...), custom_call_target="tpu_custom_call" | custom-call | flops 1000000000 | bytes 4000000 | tf_op jit(solution)/shard_map/coarse_level/pallas_call | solution.py:1139
  271.0 10.7 %add_update.1 = bf16[48,48,1024]{2,1,0:T(8,128)(2,1)} custom-call(bf16[48,48,1024]{2,1,0:T(8,128)(2,1)} %bitcast.55, bf16[8,2,4,48,128]{4,3,2,1,0:T(8,128)(2,1)} %get-tuple-element.56.refs_0_, bf16[8,2,4,48,128]{4,3,2,1,0:T(8,128)(2,1)} %get-tuple-element.57.refs_1_, bf16[8,2,4,48,128]{4,3,2,1,0:T(8,128)(2,1)} %get-tuple-element.63.refs_2_, ...), custom_call_target="tpu_custom_call" | custom-call | flops 2359296 | bytes 14155776 | tf_op jit(solution)/shard_map/add_update/pallas_call | solution.py:595
  281.7 1.2 copy.86
  (69 shorter events, 14.5 us)
Async XLA Ops:
  7.2 1.4 copy-start
  102.3 8.9 %copy-start.16 = (bf16[384,4]{0,1:T(4,128)(2,1)S(1)}, bf16[384,4]{0,1:T(4,128)(2,1)}, u32[]{:S(2)}) copy-start(bf16[384,4]{0,1:T(4,128)(2,1)} %param.36) | copy-start | bytes 9220
  102.3 70.0 %all-to-all-start = ((bf16[128,3,48,128]{3,2,1,0:T(8,128)(2,1)}), bf16[128,3,48,128]{3,2,1,0:T(8,128)(2,1)}, u32[]{:S(2)}, u32[]{:S(2)}) async-start(bf16[128,3,48,128]{3,2,1,0:T(8,128)(2,1)} %bitcast.58), calls=%async_computation | async-start | bytes 9437184 | tf_op jit(solution)/shard_map/all_to_all | solution.py:1248
  111.0 61.3 %reduce-scatter.2.cloned.1.call-start = ((), (), s32[]{:S(2)}) async-start(), calls=%async_computation.2 | async-start | bytes 442368 | tf_op jit(solution)/shard_map/reduce_scatter | solution.py:1261
  112.0 5.6 %copy-start.4 = (bf16[768,384]{1,0:T(8,128)(2,1)S(1)}, bf16[768,384]{1,0:T(8,128)(2,1)}, u32[]{:S(2)}) copy-start(bf16[768,384]{1,0:T(8,128)(2,1)} %param.35) | copy-start | bytes 1769476
  112.0 6.7 %copy-start.14 = (f32[200,49]{0,1:T(8,128)S(1)}, f32[200,49]{0,1:T(8,128)}, u32[]{:S(2)}) copy-start(f32[200,49]{0,1:T(8,128)} %param.47) | copy-start | bytes 117604
  112.0 6.7 %copy-start.17 = (bf16[4,200]{1,0:T(4,128)(2,1)S(1)}, bf16[4,200]{1,0:T(4,128)(2,1)}, u32[]{:S(2)}) copy-start(bf16[4,200]{1,0:T(4,128)(2,1)} %param.42) | copy-start | bytes 4804
  118.6 3.7 %copy-start.5 = (bf16[768,384]{0,1:T(8,128)(2,1)S(1)}, bf16[768,384]{0,1:T(8,128)(2,1)}, u32[]{:S(2)}) copy-start(bf16[768,384]{0,1:T(8,128)(2,1)} %copy.64) | copy-start | bytes 1769476
  121.3 6.1 %copy-start.2 = (bf16[800,8,256]{2,1,0:T(8,128)(2,1)S(1)}, bf16[800,8,256]{2,1,0:T(8,128)(2,1)}, u32[]{:S(2)}) copy-start(bf16[800,8,256]{2,1,0:T(8,128)(2,1)} %param.45) | copy-start | bytes 9830404
  131.2 2.0 copy-start.8
  131.6 2.8 copy-start.9
  133.2 2.2 copy-start.10
  133.2 3.2 %copy-start.15 = (f32[250,49]{0,1:T(8,128)S(1)}, f32[250,49]{0,1:T(8,128)}, u32[]{:S(2)}) copy-start(f32[250,49]{0,1:T(8,128)} %param.55) | copy-start | bytes 147004
  133.2 3.2 %copy-start.12 = (bf16[200,800]{1,0:T(8,128)(2,1)S(1)}, bf16[200,800]{1,0:T(8,128)(2,1)}, u32[]{:S(2)}) copy-start(bf16[200,800]{1,0:T(8,128)(2,1)} %param.48) | copy-start | bytes 960004
  134.3 3.1 %copy-start.13 = (bf16[250,4,128]{2,1,0:T(4,128)(2,1)S(1)}, bf16[250,4,128]{2,1,0:T(4,128)(2,1)}, u32[]{:S(2)}) copy-start(bf16[250,4,128]{2,1,0:T(4,128)(2,1)} %param.51) | copy-start | bytes 768004
  134.3 3.8 %copy-start.11 = (bf16[200,250]{1,0:T(8,128)(2,1)S(1)}, bf16[200,250]{1,0:T(8,128)(2,1)}, u32[]{:S(2)}) copy-start(bf16[200,250]{1,0:T(8,128)(2,1)} %param.50) | copy-start | bytes 300004
  139.6 28.6 %copy-start.3 = (f32[2,200,392]{2,1,0:T(8,128)S(1)}, f32[2,200,392]{2,1,0:T(8,128)}, u32[]{:S(2)}) copy-start(f32[2,200,392]{2,1,0:T(8,128)} %copy.70) | copy-start | bytes 1881604
  139.6 28.6 %copy-start.7 = (f32[200,392]{1,0:T(8,128)S(1)}, f32[200,392]{1,0:T(8,128)}, u32[]{:S(2)}) copy-start(f32[200,392]{1,0:T(8,128)} %copy.69) | copy-start | bytes 940804
  166.5 5.8 %copy-start.18 = (f32[200]{0:T(256)S(1)}, f32[200]{0:T(256)}, u32[]{:S(2)}) copy-start(f32[200]{0:T(256)} %param.46) | copy-start | bytes 2404
  166.5 7.3 %copy-start.19 = (f32[250]{0:T(256)S(1)}, f32[250]{0:T(256)}, u32[]{:S(2)}) copy-start(f32[250]{0:T(256)} %param.54) | copy-start | bytes 3004
  270.9 10.7 %copy-start.6 = (bf16[2,200,8,256]{3,2,1,0:T(8,128)(2,1)S(1)}, bf16[2,200,8,256]{3,2,1,0:T(8,128)(2,1)}, u32[]{:S(2)}) copy-start(bf16[2,200,8,256]{3,2,1,0:T(8,128)(2,1)} %get-tuple-element.99) | copy-start | bytes 4915204
  271.0 11.9 %copy-start.1 = (f32[384,48]{0,1:T(8,128)S(1)}, f32[384,48]{0,1:T(8,128)}, u32[]{:S(2)}) copy-start(f32[384,48]{0,1:T(8,128)} %param.33) | copy-start | bytes 221188
Sparse Core Ops, SparseCore 0:
  117.6 54.5 reduce-scatter.1

commit v5 on v4

--- a/solution.py
+++ b/solution.py
@@ -160,14 +160,14 @@
     return jax.ShapeDtypeStruct((blocks, probes, count, width, lanes), BF16)
 
 
-SENT_GROUPS = 2
-SENT = ((8, 4), (12, 4), (16, 8))
+SENT_GROUPS = 1
+SENT = ((4, 4), (8, 8), (16, 8))
 ANYWHERE = pl.BlockSpec(memory_space=pl.ANY)
 
 
 def ocean_rows_kernel(in_ref, mask_ref, out_ref, wide):
     _, chans, rows, cols = in_ref.shape
-    value = in_ref[0].astype(F32) * mask_ref[...][None]
+    value = in_ref[0].astype(F32) * mask_ref[...].astype(F32)[None]
     for t in range(cols // 128):
         wide[t] = value[:, :, t * 128 : (t + 1) * 128].reshape(chans * rows, 128)
     for y in range(rows):
@@ -354,17 +354,14 @@
 def filter_kernel(in_ref, fwd_ref, inv_ref, filt_ref, diff_ref, out_ref, wide, back):
     bands, _, pair, lons = in_ref.shape
     rows = pair // 2
-    blocks = out_ref.shape[1]
-
-    def load(b, carry):
+    which = lax.broadcasted_iota(jnp.int32, filt_ref.shape, 1)
+    filt = jnp.sum(
+        jnp.where(which == pl.program_id(0), filt_ref[...], 0.0), axis=1, keepdims=True
+    )
+    for b in range(bands):
         piece = in_ref[b, 0].astype(F32)
-        at = pl.ds(pl.multiple_of(b * rows, 8), rows)
-        wide[at, 0:lons] = piece[0:rows]
-        wide[at, lons : 2 * lons] = piece[rows:pair]
-        return carry
-
-    lax.fori_loop(0, bands, load, 0)
-    filt = filt_ref[0]
+        wide[b * rows : (b + 1) * rows, 0:lons] = piece[0:rows]
+        wide[b * rows : (b + 1) * rows, lons : 2 * lons] = piece[rows:pair]
     for t in range(2):
         at = slice(t * lons, (t + 1) * lons)
         value = wide[:, at]
@@ -372,24 +369,18 @@
         returned = mm(inv_ref[...], filtered)
         back[:, at] = returned.astype(BF16)
         wide[:, at] = value + returned
-    for p in range(2):
-        for t in range(lons // 256):
-            at = slice(p * lons + t * 256, p * lons + (t + 1) * 256)
-            wide[:, at] = wide[:, at] + mm(
-                back[:, p * lons : (p + 1) * lons], diff_ref[:, t * 256 : (t + 1) * 256]
-            )
-
-    def store(b, carry):
-        at = pl.ds(pl.multiple_of(b * rows, 8), rows)
-        for j in range(blocks):
-            cols = slice(j * 128, (j + 1) * 128)
-            more = slice(lons + j * 128, lons + (j + 1) * 128)
-            out_ref[b, j, 0] = jnp.concatenate([wide[at, cols], wide[at, more]], axis=0).astype(
-                BF16
-            )
-        return carry
-
-    lax.fori_loop(0, bands, store, 0)
+    for t in range(lons // 256):
+        cols = slice(t * 256, (t + 1) * 256)
+        mixed = [
+            wide[:, p * lons + t * 256 : p * lons + (t + 1) * 256]
+            + mm(back[:, p * lons : (p + 1) * lons], diff_ref[:, cols])
+            for p in range(2)
+        ]
+        for b in range(bands):
+            at = slice(b * rows, (b + 1) * rows)
+            both = jnp.concatenate([mixed[0][at], mixed[1][at]], axis=0).astype(BF16)
+            for j in range(2):
+                out_ref[b, 2 * t + j, 0] = both[:, j * 128 : (j + 1) * 128]
 
 
 def lat_filter(received, fwd, inv, filt, diff):
@@ -403,7 +394,7 @@
             pl.BlockSpec((bands, 1, pair, lons), lambda i: (0, i, 0, 0)),
             whole(fwd.shape),
             whole(inv.shape),
-            pl.BlockSpec((1, lats, 1), lambda i: (i, 0, 0)),
+            whole(filt.shape),
             whole(diff.shape),
         ],
         out_specs=pl.BlockSpec((bands, blocks, 1, pair, 128), lambda i: (0, 0, i, 0, 0)),
@@ -567,34 +558,33 @@
 
 def add_kernel(starts, probe_ref, *refs):
     out_ref = refs[-1]
-    step = pl.program_id(1)
+    step = pl.program_id(0)
     for k, update_ref in enumerate(refs[:-1]):
 
         @pl.when((step >= starts[k]) & (step < starts[k + 1]))
         def _(update_ref=update_ref):
             for j in range(update_ref.shape[0]):
                 cols = slice(j * 128, (j + 1) * 128)
-                out_ref[:, :, cols] = probe_ref[:, :, cols] + update_ref[j, 0]
+                out_ref[:, :, :, cols] = probe_ref[:, :, :, cols] + update_ref[j]
 
 
 def add_update(probe, parts):
-    lines, chans, lons = probe.shape
+    probes, rows, chans, lons = probe.shape
     blocks = parts[0].shape[0]
-    rows = lines // 2
     step = 4
     counts = [a.shape[2] // step for a in parts]
     starts = [sum(counts[:k]) for k in range(len(counts) + 1)]
 
     def spec(k):
         return pl.BlockSpec(
-            (blocks, 1, step, chans, 128),
-            lambda p, i: (0, p, jnp.clip(i - starts[k], 0, counts[k] - 1), 0, 0),
+            (blocks, probes, step, chans, 128),
+            lambda i: (0, 0, jnp.clip(i - starts[k], 0, counts[k] - 1), 0, 0),
         )
 
-    field = pl.BlockSpec((step, chans, lons), lambda p, i: (p * (rows // step) + i, 0, 0))
+    field = pl.BlockSpec((probes, step, chans, lons), lambda i: (0, i, 0, 0))
     return pl.pallas_call(
         functools.partial(add_kernel, starts),
-        grid=(2, rows // step),
+        grid=(rows // step,),
         in_specs=[field] + [spec(k) for k in range(len(parts))],
         out_specs=field,
         out_shape=jax.ShapeDtypeStruct(probe.shape, BF16),
@@ -670,117 +660,6 @@
     )(around, taps)
 
 
-def flux_kernel(
-    rows_sent,
-    blocks,
-    picked_ref,
-    slots_ref,
-    weights_ref,
-    mask_ref,
-    update_ref,
-    out_ref,
-    back_ref,
-    pool_ref,
-    tall,
-    send,
-    recv,
-    edge,
-    home_sems,
-):
-    bands, fields, cap = picked_ref.shape
-    rows, cols = mask_ref.shape
-    band, block = lax.axis_index("lat"), lax.axis_index("chan")
-    lat_before, lat_after, chan_before, chan_after = neighbours(bands, blocks)
-    tall[...] = jnp.zeros_like(tall)
-    pool_ref[pl.ds(band, 1)] = picked_ref[pl.ds(band, 1)]
-    others = [(lax.rem(band + k, bands), block) for k in range(1, bands)]
-    greet((), others + chan_peers(blocks))
-
-    copies = []
-    for k, where in enumerate(others):
-        copy = pltpu.make_async_remote_copy(
-            picked_ref.at[where[0]],
-            pool_ref.at[band],
-            send.at[k],
-            recv.at[k],
-            device_id=where,
-            device_id_type=MESH,
-        )
-        copy.start()
-        copies.append(copy)
-    home = homeward(update_ref, back_ref, rows_sent[0], home_sems)
-    for copy in home:
-        copy.start()
-    for copy in copies:
-        copy.wait()
-
-    pool = pool_ref[...].reshape(bands * fields, cap).astype(BF16)
-    place = lax.broadcasted_iota(jnp.int32, (cap, cols), 0)
-    for y in range(rows):
-        at = slice(y * cols, (y + 1) * cols)
-        total = jnp.zeros((fields, cols), F32)
-        for k in range(slots_ref.shape[0]):
-            slots = slots_ref[k : k + 1, at]
-            weights = weights_ref[k : k + 1, at]
-            source = slots // cap
-            hot = jnp.where(place == slots - source * cap, 1.0, 0.0).astype(BF16)
-            found = mm(pool, hot)
-            for b in range(bands):
-                total = total + found[b * fields : (b + 1) * fields] * jnp.where(
-                    source == b, weights, 0.0
-                )
-        tall[3 + y, :, 128 : 128 + cols] = total * mask_ref[y : y + 1, :]
-
-    inner = pl.ds(128, cols)
-    swap_edges(
-        tall.at[pl.ds(3, 3), :, inner],
-        tall.at[pl.ds(rows, 3), :, inner],
-        edge.at[0],
-        lat_before,
-        lat_after,
-        tall.at[pl.ds(rows + 3, 3), :, inner],
-        tall.at[pl.ds(0, 3), :, inner],
-    )
-    swap_edges(
-        tall.at[:, :, pl.ds(128, 128)],
-        tall.at[:, :, pl.ds(cols, 128)],
-        edge.at[1],
-        chan_before,
-        chan_after,
-        tall.at[:, :, pl.ds(128 + cols, 128)],
-        tall.at[:, :, pl.ds(0, 128)],
-    )
-    out_ref[...] = tall[...]
-    for copy in home:
-        copy.wait()
-
-
-def flux_tile(picked, slots, weights, mask, update, rows_sent):
-    bands, fields, _ = picked.shape
-    blocks = update.shape[0]
-    rows, cols = mask.shape
-    shape = (rows + 6, fields, cols + 256)
-    return pl.pallas_call(
-        functools.partial(flux_kernel, rows_sent, blocks),
-        in_specs=[whole(a.shape) for a in (picked, slots, weights, mask)] + [ANYWHERE],
-        out_specs=[whole(shape), ANYWHERE],
-        out_shape=[
-            jax.ShapeDtypeStruct(shape, F32),
-            homeward_shape(update, rows_sent[1]),
-        ],
-        scratch_shapes=[
-            pltpu.VMEM(picked.shape, F32),
-            pltpu.VMEM(shape, F32),
-            pltpu.SemaphoreType.DMA((bands - 1,)),
-            pltpu.SemaphoreType.DMA((bands - 1,)),
-            pltpu.SemaphoreType.DMA((2, 4)),
-            homeward_sems(blocks),
-        ],
-        compiler_params=params(collective_id=1, has_side_effects=True),
-        name="flux_tile",
-    )(picked, slots, weights, mask, update)
-
-
 def normed_step(spread, base, sigma, gain):
     chans = spread.shape[0]
     wide_base = jnp.concatenate([base, base], axis=1)
@@ -790,37 +669,39 @@
     return (gain * scale * (spread - center - wide_base * along)).astype(BF16)
 
 
-def row_edges(bands, blocks, line, lines, rows_ref, edges_ref, sems):
+def row_edges(bands, blocks, line, lines, around, inner, sems):
     before, after, _, _ = neighbours(bands, blocks)
     pairs = []
     if line < 3:
-        pairs.append((before, 3 + line, after))
+        pairs.append((before, lines + 3 + line, 3 + line, after))
     if line >= lines - 3:
-        pairs.append((after, line - (lines - 3), before))
+        pairs.append((after, line - (lines - 3), line - (lines - 3), before))
     return [
         (
             there,
             comes[0],
             pltpu.make_async_remote_copy(
-                rows_ref.at[line],
-                edges_ref.at[slot],
+                around.at[3 + line, :, inner, :],
+                around.at[to, :, inner, :],
                 sems.at[0, slot],
                 sems.at[1, slot],
                 device_id=where,
                 device_id_type=MESH,
             ),
         )
-        for (there, where), slot, comes in pairs
+        for (there, where), to, slot, comes in pairs
     ]
 
 
-def fine_kernel(
+def ocean_kernel(
     bands,
     rows_sent,
+    picked_ref,
+    slots_ref,
+    weights_ref,
+    mask_ref,
     spread_ref,
     probe_ref,
-    flux_ref,
-    mask_ref,
     sigma_ref,
     base_ref,
     slope_ref,
@@ -832,32 +713,106 @@
     pool_ref,
     down_ref,
     turn_ref,
+    taps_ref,
+    sigma_two_ref,
+    base_two_ref,
+    slope_two_ref,
+    gain_two_ref,
+    expand_two_ref,
+    shrink_two_ref,
+    spreadout_ref,
+    up_ref,
     update_ref,
-    one_ref,
-    coarse_ref,
-    turned_ref,
-    edges_ref,
-    back_ref,
-    columns,
-    held,
-    edge_sems,
-    home_sems,
+    out_ref,
+    *rest,
 ):
+    stages = len(rows_sent)
+    back_refs = rest[:stages]
+    (pool, flux, columns, one, coarse, around, wide, tall, done, spread_two) = rest[
+        stages : stages + 10
+    ]
+    send, recv, flux_sems, row_sems, column_sems = rest[stages + 10 : stages + 15]
+    home_sems = rest[stages + 15]
     step = pl.program_id(0)
-    blocks = back_ref.shape[0]
-    lines = held.shape[0]
-    home = homeward(update_ref, back_ref, rows_sent[0], home_sems)
-    high = flux_ref.shape[0]
-    cols = flux_ref.shape[2] - 256
+    blocks = update_ref.shape[0]
+    probes, fine, rows, cols = out_ref.shape
+    lines = rows // 2
+    half = cols // 2
+    fields = picked_ref.shape[1]
+    cap = picked_ref.shape[2]
+    band, block = lax.axis_index("lat"), lax.axis_index("chan")
+    before, after, chan_before, chan_after = neighbours(bands, blocks)
+    inner = pl.ds(16, half)
+    homes = [
+        homeward(update_ref, back_refs[k], rows_sent[k][0], home_sems[k]) for k in range(stages)
+    ]
+
+    def start_home(k):
+        for copy in homes[k]:
+            copy.start()
 
     @pl.when(step == 0)
     def _():
-        before, after, _, _ = neighbours(bands, blocks)
-        greet((before, after), chan_peers(blocks))
-        for copy in home:
+        flux[...] = jnp.zeros_like(flux)
+        around[...] = jnp.zeros_like(around)
+        pool[pl.ds(band, 1)] = picked_ref[pl.ds(band, 1)]
+        others = [(lax.rem(band + k, bands), block) for k in range(1, bands)]
+        greet((), others + chan_peers(blocks))
+        copies = []
+        for k, where in enumerate(others):
+            copy = pltpu.make_async_remote_copy(
+                picked_ref.at[where[0]],
+                pool.at[band],
+                send.at[k],
+                recv.at[k],
+                device_id=where,
+                device_id_type=MESH,
+            )
             copy.start()
-        for y in range(high):
-            row = flux_ref[y]
+            copies.append(copy)
+        start_home(0)
+        for copy in copies:
+            copy.wait()
+
+        values = pool[...].reshape(bands * fields, cap).astype(BF16)
+        place = lax.broadcasted_iota(jnp.int32, (cap, cols), 0)
+        for y in range(rows):
+            at = slice(y * cols, (y + 1) * cols)
+            total = jnp.zeros((fields, cols), F32)
+            for k in range(slots_ref.shape[0]):
+                slots = slots_ref[k : k + 1, at]
+                weights = weights_ref[k : k + 1, at]
+                source = slots // cap
+                hot = jnp.where(place == slots - source * cap, 1.0, 0.0).astype(BF16)
+                found = mm(values, hot)
+                for b in range(bands):
+                    total = total + found[b * fields : (b + 1) * fields] * jnp.where(
+                        source == b, weights, 0.0
+                    )
+            flux[3 + y, :, 128 : 128 + cols] = total * mask_ref[y : y + 1, :]
+
+        center = pl.ds(128, cols)
+        swap_edges(
+            flux.at[pl.ds(3, 3), :, center],
+            flux.at[pl.ds(rows, 3), :, center],
+            flux_sems.at[0],
+            before,
+            after,
+            flux.at[pl.ds(rows + 3, 3), :, center],
+            flux.at[pl.ds(0, 3), :, center],
+        )
+        swap_edges(
+            flux.at[:, :, pl.ds(128, 128)],
+            flux.at[:, :, pl.ds(cols, 128)],
+            flux_sems.at[1],
+            chan_before,
+            chan_after,
+            flux.at[:, :, pl.ds(128 + cols, 128)],
+            flux.at[:, :, pl.ds(0, 128)],
+        )
+        start_home(1)
+        for y in range(rows + 6):
+            row = flux[y]
             for b in range(7):
                 columns[(y * 7 + b) * 8 : (y * 7 + b + 1) * 8, :] = row[:, 125 + b : 125 + b + cols]
 
@@ -878,26 +833,22 @@
         hidden = mm(expand_ref[...], tangent)
         gated = (hidden * jnp.concatenate([slope, slope], axis=1)).astype(BF16)
         mask = mask_ref[at, :]
-        one = (
+        level = (
             (start + mm(shrink_ref[...], gated)) * jnp.concatenate([mask, mask], axis=1)
         ).astype(BF16)
-        one_ref[h] = one
-        pooled.append(mm(one, pool_ref[...]))
+        one[y] = level
+        pooled.append(mm(level, pool_ref[...]))
 
     both = (pooled[0] + pooled[1]).astype(BF16)
-    coarse_ref[0] = mm(down_ref[...], both).astype(BF16)
+    coarse[step] = mm(down_ref[...], both).astype(BF16)
     turned = mm(both.T, turn_ref[...]).astype(BF16)
-    half = turned.shape[0] // 2
-    turned_ref[0, 0] = turned[0:half]
-    turned_ref[0, 1] = turned[half : 2 * half]
     for line in range(lines):
 
         @pl.when(step == line)
         def _(line=line):
-            held[line] = turned_ref[0]
-            for there, _, copy in row_edges(
-                bands, blocks, line, lines, held, edges_ref, edge_sems
-            ):
+            around[3 + line, 0, 16 : 16 + half, :] = turned[0:half]
+            around[3 + line, 1, 16 : 16 + half, :] = turned[half : 2 * half]
+            for there, _, copy in row_edges(bands, blocks, line, lines, around, inner, row_sems):
 
                 @pl.when(there)
                 def _(copy=copy):
@@ -907,7 +858,7 @@
     def _():
         for line in range(lines):
             for there, comes, copy in row_edges(
-                bands, blocks, line, lines, held, edges_ref, edge_sems
+                bands, blocks, line, lines, around, inner, row_sems
             ):
 
                 @pl.when(there)
@@ -918,245 +869,110 @@
                 def _(copy=copy):
                     copy.wait_recv()
 
-        for copy in home:
-            copy.wait()
-
-
-def fine_level(
-    spread,
-    probe,
-    flux,
-    mask,
-    sigma,
-    base,
-    slope,
-    gain,
-    mix,
-    couple,
-    expand,
-    shrink,
-    pool,
-    down,
-    turn,
-    update,
-    bands,
-    rows_sent,
-):
-    rows, chans, wide = spread.shape
-    cols = wide // 2
-    coarse = down.shape[0]
-    lines = rows // 2
-    turned = (2, cols // 2, turn.shape[1])
+        finish = start_edges(
+            around.at[:, :, pl.ds(16, 16), :],
+            around.at[:, :, pl.ds(half, 16), :],
+            column_sems,
+            chan_before,
+            chan_after,
+            around.at[:, :, pl.ds(16 + half, 16), :],
+            around.at[:, :, pl.ds(0, 16), :],
+        )
+        start_home(2)
+        finish()
+        chans = coarse.shape[1]
+        for p in range(probes):
+            for y in range(tall.shape[1]):
+                for h in range(tall.shape[0]):
+                    tall[h, y] = around[y, p, :, h * 128 : (h + 1) * 128].astype(F32)
+            depth_sum(13, taps_ref, tall, done)
+            for y in range(lines):
+                spread_two[y, :, p * half : (p + 1) * half] = done[y].T[0:chans]
+
+        acts = []
+        for y in range(lines):
+            tangent = normed_step(
+                spread_two[y],
+                base_two_ref[y].astype(F32),
+                sigma_two_ref[y : y + 1, :],
+                gain_two_ref[...],
+            )
+            slope = slope_two_ref[y].astype(F32)
+            hidden = mm(expand_two_ref[...], tangent)
+            acts.append((hidden * jnp.concatenate([slope, slope], axis=1)).astype(BF16))
+        for y in range(lines):
+            two = (coarse[y].astype(F32) + mm(shrink_two_ref[...], acts[y])).astype(BF16)
+            raised = mm(up_ref[...], mm(two, spreadout_ref[...]).astype(BF16))
+            for h in range(2):
+                line = y * 2 + h
+                mask = mask_ref[line : line + 1, :]
+                for p in range(probes):
+                    for t in range(cols // 128):
+                        lanes = slice(p * cols + t * 128, p * cols + (t + 1) * 128)
+                        wide[p, t, pl.ds(line, fine, stride=rows), :] = (
+                            one[line, :, lanes].astype(F32) + raised[:, lanes]
+                        ) * mask[:, t * 128 : (t + 1) * 128]
+        for p in range(probes):
+            for t in range(cols // 128):
+                out_ref[p, :, :, t * 128 : (t + 1) * 128] = (
+                    wide[p, t].reshape(fine, rows, 128).astype(BF16)
+                )
+        for home in homes:
+            for copy in home:
+                copy.wait()
+
+
+def ocean_levels(routed, fine_args, coarse_args, update, bands, rows_sent):
+    picked, slots, weights, mask = routed
+    spread, probe, sigma, base, slope = fine_args[:5]
+    taps = coarse_args[0]
+    down = fine_args[11]
+    rows, chans, double = spread.shape
+    cols = double // 2
+    lines, half = rows // 2, cols // 2
+    high = lines + 6
+    fields = picked.shape[1]
+    blocks = update.shape[0]
     row = lambda i: (i, 0, 0)
+    streamed = [
+        pl.BlockSpec((2, chans, double), row),
+        pl.BlockSpec((2,) + probe.shape[1:], lambda i: (i, 0, 0, 0)),
+        whole(sigma.shape),
+        pl.BlockSpec((2, chans, cols), row),
+        pl.BlockSpec((2, slope.shape[1], cols), row),
+    ]
     return pl.pallas_call(
-        functools.partial(fine_kernel, bands, rows_sent),
+        functools.partial(ocean_kernel, bands, rows_sent),
         grid=(lines,),
-        in_specs=[
-            pl.BlockSpec((2, chans, wide), row),
-            pl.BlockSpec((2,) + probe.shape[1:], lambda i: (i, 0, 0, 0)),
-            whole(flux.shape),
-            whole(mask.shape),
-            whole(sigma.shape),
-            pl.BlockSpec((2, chans, cols), row),
-            pl.BlockSpec((2, slope.shape[1], cols), row),
-            whole(gain.shape),
-            whole(mix.shape),
-            whole(couple.shape),
-            whole(expand.shape),
-            whole(shrink.shape),
-            whole(pool.shape),
-            whole(down.shape),
-            whole(turn.shape),
-            ANYWHERE,
-        ],
-        out_specs=[
-            pl.BlockSpec((2, chans, wide), row),
-            pl.BlockSpec((1, coarse, cols), row),
-            pl.BlockSpec((1,) + turned, lambda i: (i, 0, 0, 0)),
-            ANYWHERE,
-            ANYWHERE,
-        ],
-        out_shape=[
-            jax.ShapeDtypeStruct((rows, chans, wide), BF16),
-            jax.ShapeDtypeStruct((lines, coarse, cols), BF16),
-            jax.ShapeDtypeStruct((lines,) + turned, BF16),
-            jax.ShapeDtypeStruct((6,) + turned, BF16),
-            homeward_shape(update, rows_sent[1]),
-        ],
+        in_specs=[whole(a.shape) for a in routed]
+        + streamed
+        + [whole(a.shape) for a in fine_args[5:] + coarse_args]
+        + [ANYWHERE],
+        out_specs=[whole((2, chans, rows, cols))] + [ANYWHERE] * len(rows_sent),
+        out_shape=[jax.ShapeDtypeStruct((2, chans, rows, cols), BF16)]
+        + [homeward_shape(update, count) for _, count in rows_sent],
         scratch_shapes=[
-            pltpu.VMEM((flux.shape[0] * 56, cols), F32),
-            pltpu.VMEM((lines,) + turned, BF16),
-            pltpu.SemaphoreType.DMA((2, 6)),
-            homeward_sems(update.shape[0]),
-        ],
-        compiler_params=params(collective_id=4, has_side_effects=True),
-        name="fine_level",
-    )(
-        spread,
-        probe,
-        flux,
-        mask,
-        sigma,
-        base,
-        slope,
-        gain,
-        mix,
-        couple,
-        expand,
-        shrink,
-        pool,
-        down,
-        turn,
-        update,
-    )
-
-
-def coarse_kernel(
-    bands,
-    rows_sent,
-    turned_ref,
-    edges_ref,
-    taps_ref,
-    field_ref,
-    sigma_ref,
-    base_ref,
-    slope_ref,
-    gain_ref,
-    expand_ref,
-    shrink_ref,
-    spreadout_ref,
-    up_ref,
-    one_ref,
-    mask_ref,
-    update_ref,
-    out_ref,
-    back_ref,
-    around,
-    wide,
-    tall,
-    done,
-    spread,
-    edge,
-    home_sems,
-):
-    blocks = back_ref.shape[0]
-    home = homeward(update_ref, back_ref, rows_sent[0], home_sems)
-    lines, chans, _ = field_ref.shape
-    probes, fine, rows, cols = out_ref.shape
-    half = cols // 2
-    before, after, chan_before, chan_after = neighbours(bands, blocks)
-    inner = slice(16, 16 + half)
-    around[...] = jnp.zeros_like(around)
-    around[3 : 3 + lines, :, inner, :] = turned_ref[...]
-
-    @pl.when(before[0])
-    def _():
-        around[0:3, :, inner, :] = edges_ref[0:3]
-
-    @pl.when(after[0])
-    def _():
-        around[3 + lines : 6 + lines, :, inner, :] = edges_ref[3:6]
-
-    greet((), chan_peers(blocks))
-    finish = start_edges(
-        around.at[:, :, pl.ds(16, 16), :],
-        around.at[:, :, pl.ds(half, 16), :],
-        edge,
-        chan_before,
-        chan_after,
-        around.at[:, :, pl.ds(16 + half, 16), :],
-        around.at[:, :, pl.ds(0, 16), :],
-    )
-    for copy in home:
-        copy.start()
-    finish()
-    for p in range(probes):
-        for y in range(tall.shape[1]):
-            for h in range(tall.shape[0]):
-                lanes = slice(h * 128, (h + 1) * 128)
-                tall[h, y] = around[y, p, :, lanes].astype(F32)
-        depth_sum(13, taps_ref, tall, done)
-        for y in range(lines):
-            spread[y, :, p * half : (p + 1) * half] = done[y].T[0:chans]
-
-    gated = []
-    for y in range(lines):
-        tangent = normed_step(
-            spread[y], base_ref[y].astype(F32), sigma_ref[y : y + 1, :], gain_ref[...]
-        )
-        slope = slope_ref[y].astype(F32)
-        hidden = mm(expand_ref[...], tangent)
-        gated.append((hidden * jnp.concatenate([slope, slope], axis=1)).astype(BF16))
-    for y in range(lines):
-        two = (field_ref[y].astype(F32) + mm(shrink_ref[...], gated[y])).astype(BF16)
-        raised = mm(up_ref[...], mm(two, spreadout_ref[...]).astype(BF16))
-        for h in range(2):
-            line = y * 2 + h
-            mask = mask_ref[line : line + 1, :]
-            for p in range(probes):
-                for t in range(cols // 128):
-                    lanes = slice(p * cols + t * 128, p * cols + (t + 1) * 128)
-                    wide[p, t, pl.ds(line, fine, stride=rows), :] = (
-                        one_ref[line, :, lanes].astype(F32) + raised[:, lanes]
-                    ) * mask[:, t * 128 : (t + 1) * 128]
-    for p in range(probes):
-        for t in range(cols // 128):
-            out_ref[p, :, :, t * 128 : (t + 1) * 128] = (
-                wide[p, t].reshape(fine, rows, 128).astype(BF16)
-            )
-    for copy in home:
-        copy.wait()
-
-
-def coarse_level(
-    turned,
-    edges,
-    taps,
-    field,
-    sigma,
-    base,
-    slope,
-    gain,
-    expand,
-    shrink,
-    spreadout,
-    up,
-    one,
-    mask,
-    update,
-    bands,
-    rows_sent,
-):
-    lines, chans, double = field.shape
-    half = double // 2
-    rows, fine, _ = one.shape
-    cols = double
-    high = lines + 6
-    operands = (
-        (turned, edges, taps, field, sigma, base, slope, gain)
-        + (expand, shrink, spreadout, up, one, mask)
-    )
-    return pl.pallas_call(
-        functools.partial(coarse_kernel, bands, rows_sent),
-        in_specs=[whole(a.shape) for a in operands] + [ANYWHERE],
-        out_specs=[whole((2, fine, rows, cols)), ANYWHERE],
-        out_shape=[
-            jax.ShapeDtypeStruct((2, fine, rows, cols), BF16),
-            homeward_shape(update, rows_sent[1]),
-        ],
-        scratch_shapes=[
+            pltpu.VMEM(picked.shape, F32),
+            pltpu.VMEM((rows + 6, fields, cols + 256), F32),
+            pltpu.VMEM(((rows + 6) * 56, cols), F32),
+            pltpu.VMEM((rows, chans, double), BF16),
+            pltpu.VMEM((lines, down.shape[0], cols), BF16),
             pltpu.VMEM((high, 2, half + 32, taps.shape[1]), BF16),
-            pltpu.VMEM((2, cols // 128, fine * rows, 128), F32),
+            pltpu.VMEM((2, cols // 128, chans * rows, 128), F32),
             pltpu.VMEM((taps.shape[1] // 128, high, half + 32, 128), F32),
             pltpu.VMEM((lines, half, taps.shape[1]), F32),
-            pltpu.VMEM((lines, chans, double), F32),
+            pltpu.VMEM((lines, down.shape[0], cols), F32),
+            pltpu.SemaphoreType.DMA((bands - 1,)),
+            pltpu.SemaphoreType.DMA((bands - 1,)),
+            pltpu.SemaphoreType.DMA((2, 4)),
+            pltpu.SemaphoreType.DMA((2, 6)),
             pltpu.SemaphoreType.DMA((4,)),
-            homeward_sems(update.shape[0]),
+            [homeward_sems(blocks) for _ in rows_sent],
         ],
-        compiler_params=params(collective_id=5, has_side_effects=True),
-        cost_estimate=cost(1e9, 4e6),
-        name="coarse_level",
-    )(*operands, update)
+        compiler_params=params(collective_id=1, has_side_effects=True),
+        cost_estimate=cost(5e9, 2e7),
+        name="ocean_levels",
+    )(*routed, *fine_args, *coarse_args, update)
 
 
 def local(
@@ -1216,7 +1032,7 @@
     tile_rows, tile_cols = ocean_mask.shape
     fine = ocean_probe.shape[1]
     mask = ocean_mask.astype(F32)
-    start = ocean_rows(ocean_probe, mask)
+    start = ocean_rows(ocean_probe, ocean_mask)
     base_rows = base_fine.transpose(1, 0, 2)
     slope_rows = slope_fine.transpose(1, 0, 2)
     base_lines = base_coarse.transpose(1, 0, 2)
@@ -1240,9 +1056,7 @@
 
     fwd_lat, inv_lat = cosine_tables(lats)
     diff = jnp.asarray(fourier_product(lons))
-    filt = lax.dynamic_slice_in_dim(
-        spectral_filter, lax.axis_index("lat") * part, part, 1
-    ).T.reshape(part, lats, 1)
+    filt = lax.dynamic_slice_in_dim(spectral_filter, lax.axis_index("lat") * part, part, 1)
     gathered, filt = lax.optimization_barrier((gathered, filt))
     mixed = lat_filter(gathered, jnp.asarray(fwd_lat.T), jnp.asarray(inv_lat.T), filt, diff)
     regrouped = lax.all_to_all(
@@ -1323,48 +1137,18 @@
         regrouped, gate_slope, win, wout, probe_terms, cells, blocks, SENT_GROUPS
     )
 
-    tall, back0 = flux_tile(picked, slots, weights, mask, update, SENT[0])
-    one, coarse, turned, edges, back1 = fine_level(
-        spread,
-        start,
-        tall,
-        mask,
-        sigma_fine,
-        base_rows,
-        slope_rows,
-        gain_one,
-        mix,
-        couple,
-        expand_one,
-        shrink_one,
-        pool,
-        down,
-        turn,
+    ocean_out, *backs = ocean_levels(
+        (picked, slots, weights, mask),
+        (spread, start, sigma_fine, base_rows, slope_rows, gain_one, mix, couple)
+        + (expand_one, shrink_one, pool, down, turn),
+        (taps, sigma_coarse, base_lines, slope_lines, gain_two, expand_two, shrink_two)
+        + (spreadout, raise_two),
         update,
         bands,
-        SENT[1],
+        SENT,
     )
-    ocean_out, back2 = coarse_level(
-        turned,
-        edges,
-        taps,
-        coarse,
-        sigma_coarse,
-        base_lines,
-        slope_lines,
-        gain_two,
-        expand_two,
-        shrink_two,
-        spreadout,
-        raise_two,
-        one,
-        mask,
-        update,
-        bands,
-        SENT[2],
-    )
-    parts = (*shipped, back0, back1, back2)
-    atmos_out = add_update(flat_probe, parts).reshape(probe_field.shape)
+    parts = (*shipped, *backs)
+    atmos_out = add_update(probe_field, parts)
     return (atmos_out, ocean_out)
 
 

time: 295 us -> 273 us (0.925)
  Pallas kernels: 232 us -> 213 us
    pallas_call x4 -> x2, Pallas kernels: 77.8 us -> 68 us  [the longest x1 60.2 us: ocean_levels(): pl.pallas_call(functools.partial(ocean_kernel, bands, rows_sent), grid=(l...]
    pallas_call x1, Pallas kernels: 29.2 us -> 21 us  [pointwise(): pl.pallas_call(functools.partial(point_kernel, sent), grid=(rows // GROUP...]
    unnamed x49 -> x51, local copies, waits for them, and re-layouts: 10.5 us -> 11.3 us
  transfers between devices with their start and end apart: 2 -> 2, of which waited for: 1 -> 1; matrix products, arithmetic and copies ran while one was open for 9% -> 10% of each run, Pallas kernels for 11% -> 12%
where the time goes in v5:
time: 273 us; the launch traced here: 270 us
  Pallas kernels  213 us (78%)
  local copies, waits for them, and re-layouts  26.1 us (10%)
  between operations  14.2 us (5%)
  starting transfers between devices  8.92 us (3%)
  other arithmetic  4.65 us (2%)
    pallas_call x1, Pallas kernels, open_exchange(): pl.pallas_call(functools.partial(open_kernel, blocks), in_specs=[any_spec...  74.3 us
    pallas_call x1, Pallas kernels, ocean_levels(): pl.pallas_call(functools.partial(ocean_kernel, bands, rows_sent), grid=(l...  60.2 us
    pallas_call x1, Pallas kernels, depthwise(): pl.pallas_call(depth_kernel, grid=(probes,), in_specs=[pl.BlockSpec((high...  26.9 us
    pallas_call x1, Pallas kernels, pointwise(): pl.pallas_call(functools.partial(point_kernel, sent), grid=(rows // GROUP...  21 us
    pallas_call x1, Pallas kernels, lat_filter(): pl.pallas_call(filter_kernel, grid=(chans,), in_specs=[pl.BlockSpec((band...  13.8 us
    unnamed x51, local copies, waits for them, and re-layouts  11.3 us
    all_to_all x1, starting transfers between devices, local(): lax.all_to_all(mixed.reshape(bands * blocks, part, pair, 128), ('lat', 'c...  8.69 us
    pallas_call x1, Pallas kernels, add_update(): pl.pallas_call(functools.partial(add_kernel, starts), grid=(rows // step,...  7.8 us
  transfers between devices with their start and end apart: 2, of which 1 were waited for; matrix products, arithmetic and copies ran while one was open for 10% of the time, Pallas kernels for 12%

profile of v5, /device:TPU:32, one launch (start us, length us, event | category | flops | bytes accessed | tf_op | source)
XLA Modules:
  0.0 269.5 jit_solution(7576899930919340050)
XLA Ops:
  7.2 0.9 copy-done
  8.9 3.1 %ocean_rows.1.ocean_ref.probe_ref = bf16[8,2,200,256]{3,2,1,0:T(8,128)(2,1)} custom-call(bf16[2,200,8,256]{3,2,1,0:T(8,128)(2,1)} %in_ref.1, s32[8,256]{1,0:T(8,128)} %mask_ref.1), custom_call_target="tpu_custom_call" | custom-call | flops 819200 | bytes 3276800 | tf_op jit(solution)/shard_map/ocean_rows/pallas_call | solution.py:182
  12.0 74.3 %open_exchange.1 = (bf16[16,3,48,1024]{3,2,1,0:T(8,128)(2,1)}, bf16[14,2,200,512]{3,2,1,0:T(8,128)(2,1)}) custom-call(bf16[48,48,1024]{2,1,0:T(8,128)(2,1)} %bitcast.49, bf16[8,2,200,256]{3,2,1,0:T(8,128)(2,1)} %ocean_rows.1.ocean_ref.probe_ref), custom_call_target="tpu_custom_call" | custom-call | bytes 9437184 | tf_op jit(solution)/shard_map/open_exchange/pallas_call | solution.py:295
  86.2 13.8 %lat_filter.1 = bf16[16,8,3,48,128]{4,3,2,1,0:T(8,128)(2,1)} custom-call(bf16[16,3,48,1024]{3,2,1,0:T(8,128)(2,1)} %get-tuple-element.42.in_ref, bf16[384,384]{1,0:T(8,128)(2,1)} %constant.50.clone.fwd_ref, bf16[384,384]{1,0:T(8,128)(2,1)} %constant.51.clone.inv_ref, f32[384,3]{1,0:T(8,128)} %copy.78.filt_ref, bf16[1024,1024]{1,0:T(8,128)(2,1)} %constant.49.clone.diff_ref), custom_call_target="tpu_custom_call" | custom-call | flops 8400000000 | bytes 9437184 | tf_op jit(solution)/shard_map/lat_filter/pallas_call | solution.py:390
  100.1 8.7 %all-to-all-start = ((bf16[128,3,48,128]{3,2,1,0:T(8,128)(2,1)}), bf16[128,3,48,128]{3,2,1,0:T(8,128)(2,1)}, u32[]{:S(2)}, u32[]{:S(2)}) async-start(bf16[128,3,48,128]{3,2,1,0:T(8,128)(2,1)} %bitcast.51), calls=%async_computation | async-start | bytes 9437184 | tf_op jit(solution)/shard_map/all_to_all | solution.py:1062
  109.8 5.6 %probe_flux.1 = bf16[8,192,128]{2,1,0:T(8,128)(2,1)} custom-call(bf16[2,24,48,1024]{3,2,1,0:T(8,128)(2,1)} %probe_ref.3, bf16[8,96]{1,0:T(8,128)(2,1)} %fusion.2.weight_ref), custom_call_target="tpu_custom_call" | custom-call | flops 37748736 | bytes 4718592 | tf_op jit(solution)/shard_map/probe_flux/pallas_call | solution.py:339
  115.4 1.1 copy.65
  119.1 1.0 broadcast_bitcast_fusion
  121.6 2.4 copy.71
  123.9 1.9 copy.70
  125.9 2.4 copy.83
  128.2 1.3 reshape.87
  130.4 1.1 copy.64
  131.5 1.1 copy.84
  132.7 1.1 copy.85
  133.8 1.0 copy.74
  134.8 0.9 copy.72
  137.9 26.9 %depthwise.1.spread_ref = f32[8,200,512]{2,1,0:T(8,128)} custom-call(bf16[14,2,200,512]{3,2,1,0:T(8,128)(2,1)} %get-tuple-element.44.in_ref, f32[392,256]{1,0:T(8,128)} %broadcast_bitcast_fusion.3.taps_ref), custom_call_target="tpu_custom_call" | custom-call | flops 163840000 | bytes 11468800 | tf_op jit(solution)/shard_map/depthwise/pallas_call | solution.py:644
  166.5 0.9 multiply_convert_fusion.mix_ref
  167.4 2.7 reduce-scatter.2.cloned.1.call-done.pflux_ref
  172.4 21.0 %pointwise.1 = (bf16[8,2,24,48,128]{4,3,2,1,0:T(8,128)(2,1)}, f32[16,8,128]{2,1,0:T(8,128)}, bf16[8,2,4,48,128]{4,3,2,1,0:T(8,128)(2,1)}) custom-call(bf16[384,48,128]{2,1,0:T(8,128)(2,1)} %bitcast.2.mixed_ref, bf16[24,768,128]{2,1,0:T(8,128)(2,1)} %slope_ref.1, bf16[768,384]{1,0:T(8,128)(2,1)} %bitcast.58, bf16[392,768]{1,0:T(8,128)(2,1)} %maximum_bitcast_fusion.wout_ref, ...), custom_call_target="tpu_custom_call" | custom-call | flops 7299999744 | bytes 14155776 | tf_op jit(solution)/shard_map/pointwise/pallas_call | solution.py:522
  193.4 60.2 %ocean_levels.1 = (bf16[2,200,8,256]{3,2,1,0:T(8,128)(2,1)}, bf16[8,2,4,48,128]{4,3,2,1,0:T(8,128)(2,1)}, bf16[8,2,8,48,128]{4,3,2,1,0:T(8,128)(2,1)}, bf16[8,2,8,48,128]{4,3,2,1,0:T(8,128)(2,1)}) custom-call(f32[16,8,128]{2,1,0:T(8,128)} %get-tuple-element.51.picked_ref, s32[4,2048]{1,0:T(4,128)} %bitcast.65, f32[4,2048]{1,0:T(4,128)} %bitcast.66, ...), custom_call_target="tpu_custom_call" | custom-call | flops 5000000000 | bytes 20000000 | tf_op jit(solution)/shard_map/ocean_levels/pallas_call | solution.py:944
  253.7 7.8 %add_update.1 = bf16[2,24,48,1024]{3,2,1,0:T(8,128)(2,1)} custom-call(bf16[2,24,48,1024]{3,2,1,0:T(8,128)(2,1)} %probe_ref.3, bf16[8,2,4,48,128]{4,3,2,1,0:T(8,128)(2,1)} %get-tuple-element.50.refs_0_, bf16[8,2,4,48,128]{4,3,2,1,0:T(8,128)(2,1)} %get-tuple-element.76.refs_1_, bf16[8,2,8,48,128]{4,3,2,1,0:T(8,128)(2,1)} %get-tuple-element.77.refs_2_, ...), custom_call_target="tpu_custom_call" | custom-call | flops 2359296 | bytes 14155776 | tf_op jit(solution)/shard_map/add_update/pallas_call | solution.py:585
  261.5 1.2 copy.88
  (69 shorter events, 13.0 us)
Async XLA Ops:
  7.2 0.9 copy-start
  100.1 8.9 %copy-start.17 = (bf16[384,4]{0,1:T(4,128)(2,1)S(1)}, bf16[384,4]{0,1:T(4,128)(2,1)}, u32[]{:S(2)}) copy-start(bf16[384,4]{0,1:T(4,128)(2,1)} %param.36) | copy-start | bytes 9220
  100.1 70.0 %all-to-all-start = ((bf16[128,3,48,128]{3,2,1,0:T(8,128)(2,1)}), bf16[128,3,48,128]{3,2,1,0:T(8,128)(2,1)}, u32[]{:S(2)}, u32[]{:S(2)}) async-start(bf16[128,3,48,128]{3,2,1,0:T(8,128)(2,1)} %bitcast.51), calls=%async_computation | async-start | bytes 9437184 | tf_op jit(solution)/shard_map/all_to_all | solution.py:1062
  108.8 61.3 %reduce-scatter.2.cloned.1.call-start = ((), (), s32[]{:S(2)}) async-start(), calls=%async_computation.2 | async-start | bytes 442368 | tf_op jit(solution)/shard_map/reduce_scatter | solution.py:1075
  109.8 5.6 %copy-start.4 = (bf16[768,384]{1,0:T(8,128)(2,1)S(1)}, bf16[768,384]{1,0:T(8,128)(2,1)}, u32[]{:S(2)}) copy-start(bf16[768,384]{1,0:T(8,128)(2,1)} %param.35) | copy-start | bytes 1769476
  109.8 6.7 %copy-start.14 = (f32[200,49]{0,1:T(8,128)S(1)}, f32[200,49]{0,1:T(8,128)}, u32[]{:S(2)}) copy-start(f32[200,49]{0,1:T(8,128)} %param.47) | copy-start | bytes 117604
  109.8 6.7 %copy-start.18 = (bf16[4,200]{1,0:T(4,128)(2,1)S(1)}, bf16[4,200]{1,0:T(4,128)(2,1)}, u32[]{:S(2)}) copy-start(bf16[4,200]{1,0:T(4,128)(2,1)} %param.42) | copy-start | bytes 4804
  116.5 3.6 %copy-start.5 = (bf16[768,384]{0,1:T(8,128)(2,1)S(1)}, bf16[768,384]{0,1:T(8,128)(2,1)}, u32[]{:S(2)}) copy-start(bf16[768,384]{0,1:T(8,128)(2,1)} %copy.65) | copy-start | bytes 1769476
  116.5 4.5 %copy-start.16 = (s32[8,256]{1,0:T(8,128)S(1)}, s32[8,256]{1,0:T(8,128)}, u32[]{:S(2)}) copy-start(s32[8,256]{1,0:T(8,128)} %mask_ref.1) | copy-start | bytes 24580
  119.1 6.7 %copy-start.2 = (bf16[800,8,256]{2,1,0:T(8,128)(2,1)S(1)}, bf16[800,8,256]{2,1,0:T(8,128)(2,1)}, u32[]{:S(2)}) copy-start(bf16[800,8,256]{2,1,0:T(8,128)(2,1)} %param.45) | copy-start | bytes 9830404
  129.5 2.0 copy-start.8
  129.9 2.8 %copy-start.9 = (bf16[200,8,256]{2,1,0:T(8,128)(2,1)S(1)}, bf16[200,8,256]{2,1,0:T(8,128)(2,1)}, u32[]{:S(2)}) copy-start(bf16[200,8,256]{2,1,0:T(8,128)(2,1)} %param.43) | copy-start | bytes 2457604
  131.5 2.2 copy-start.10
  131.5 3.3 %copy-start.15 = (f32[250,49]{0,1:T(8,128)S(1)}, f32[250,49]{0,1:T(8,128)}, u32[]{:S(2)}) copy-start(f32[250,49]{0,1:T(8,128)} %param.55) | copy-start | bytes 147004
  131.5 3.3 %copy-start.12 = (bf16[200,800]{1,0:T(8,128)(2,1)S(1)}, bf16[200,800]{1,0:T(8,128)(2,1)}, u32[]{:S(2)}) copy-start(bf16[200,800]{1,0:T(8,128)(2,1)} %param.48) | copy-start | bytes 960004
  132.7 3.1 %copy-start.13 = (bf16[250,4,128]{2,1,0:T(4,128)(2,1)S(1)}, bf16[250,4,128]{2,1,0:T(4,128)(2,1)}, u32[]{:S(2)}) copy-start(bf16[250,4,128]{2,1,0:T(4,128)(2,1)} %param.51) | copy-start | bytes 768004
  132.7 3.8 %copy-start.11 = (bf16[200,250]{1,0:T(8,128)(2,1)S(1)}, bf16[200,250]{1,0:T(8,128)(2,1)}, u32[]{:S(2)}) copy-start(bf16[200,250]{1,0:T(8,128)(2,1)} %param.50) | copy-start | bytes 300004
  137.9 28.6 %copy-start.3 = (f32[2,200,392]{2,1,0:T(8,128)S(1)}, f32[2,200,392]{2,1,0:T(8,128)}, u32[]{:S(2)}) copy-start(f32[2,200,392]{2,1,0:T(8,128)} %copy.71) | copy-start | bytes 1881604
  137.9 28.6 %copy-start.7 = (f32[200,392]{1,0:T(8,128)S(1)}, f32[200,392]{1,0:T(8,128)}, u32[]{:S(2)}) copy-start(f32[200,392]{1,0:T(8,128)} %copy.70) | copy-start | bytes 940804
  164.9 5.2 %copy-start.19 = (f32[250]{0:T(256)S(1)}, f32[250]{0:T(256)}, u32[]{:S(2)}) copy-start(f32[250]{0:T(256)} %param.54) | copy-start | bytes 3004
  164.9 6.0 %copy-start.20 = (f32[200]{0:T(256)S(1)}, f32[200]{0:T(256)}, u32[]{:S(2)}) copy-start(f32[200]{0:T(256)} %param.46) | copy-start | bytes 2404
  253.7 7.8 %copy-start.6 = (bf16[2,200,8,256]{3,2,1,0:T(8,128)(2,1)S(1)}, bf16[2,200,8,256]{3,2,1,0:T(8,128)(2,1)}, u32[]{:S(2)}) copy-start(bf16[2,200,8,256]{3,2,1,0:T(8,128)(2,1)} %get-tuple-element.87) | copy-start | bytes 4915204
  253.7 9.0 %copy-start.1 = (f32[384,48]{0,1:T(8,128)S(1)}, f32[384,48]{0,1:T(8,128)}, u32[]{:S(2)}) copy-start(f32[384,48]{0,1:T(8,128)} %param.33) | copy-start | bytes 221188
Sparse Core Ops, SparseCore 0:
  115.5 54.5 reduce-scatter.1

commit v6 on v5

--- a/solution.py
+++ b/solution.py
@@ -165,36 +165,6 @@
 ANYWHERE = pl.BlockSpec(memory_space=pl.ANY)
 
 
-def ocean_rows_kernel(in_ref, mask_ref, out_ref, wide):
-    _, chans, rows, cols = in_ref.shape
-    value = in_ref[0].astype(F32) * mask_ref[...].astype(F32)[None]
-    for t in range(cols // 128):
-        wide[t] = value[:, :, t * 128 : (t + 1) * 128].reshape(chans * rows, 128)
-    for y in range(rows):
-        for t in range(cols // 128):
-            out_ref[y, 0, :, t * 128 : (t + 1) * 128] = wide[
-                t, pl.ds(y, chans, stride=rows), :
-            ].astype(BF16)
-
-
-def ocean_rows(field, mask):
-    probes, chans, rows, cols = field.shape
-    return pl.pallas_call(
-        ocean_rows_kernel,
-        grid=(probes,),
-        in_specs=[
-            pl.BlockSpec((1, chans, rows, cols), lambda p: (p, 0, 0, 0)),
-            whole(mask.shape),
-        ],
-        out_specs=pl.BlockSpec((rows, 1, chans, cols), lambda p: (0, p, 0, 0)),
-        out_shape=jax.ShapeDtypeStruct((rows, probes, chans, cols), BF16),
-        scratch_shapes=[pltpu.VMEM((cols // 128, chans * rows, 128), F32)],
-        compiler_params=params(),
-        cost_estimate=cost(field.size, 4 * field.size),
-        name="ocean_rows",
-    )(field, mask)
-
-
 STEPS = (
     ((0, 1), (1, 0), (0, 3), (3, 0), (1, 1), (3, 3), (1, 3), (3, 1))
     + ((0, 2), (2, 0), (2, 2), (1, 2), (2, 1), (3, 2), (2, 3))
@@ -207,13 +177,26 @@
 
 
 def open_kernel(
-    blocks, probe_ref, ocean_ref, out_ref, around_ref, taken, wide, turned, tall, sems, own, edge
+    blocks,
+    probe_ref,
+    ocean_ref,
+    mask_ref,
+    out_ref,
+    around_ref,
+    start_ref,
+    taken,
+    wide,
+    turned,
+    tall,
+    sems,
+    own,
+    edge,
 ):
     send, recv, load = sems
     rows, chans, lons = probe_ref.shape
     bands, part = out_ref.shape[0], out_ref.shape[1]
     side = math.isqrt(bands)
-    lines, _, _, cols = ocean_ref.shape
+    probes, fine, lines, cols = ocean_ref.shape
     pieces, lanes = taken.shape[0], taken.shape[3]
     band, block = lax.axis_index("lat"), lax.axis_index("chan")
     lat_before, lat_after, chan_before, chan_after = neighbours(bands, blocks)
@@ -226,20 +209,32 @@
     for i in range(pieces):
         take(i).start()
     tall[...] = jnp.zeros_like(tall)
+    mask = mask_ref[...].astype(F32)
+    for p in range(probes):
+        for t in range(cols // 128):
+            at = slice(t * 128, (t + 1) * 128)
+            value = ocean_ref[p, :, :, at].astype(F32) * mask[:, at][None]
+            wide[t, 0 : fine * lines, :] = value.reshape(fine * lines, 128)
+            for y in range(lines):
+                tall[3 + y, p, :, 128 + t * 128 : 256 + t * 128] = wide[
+                    t, pl.ds(y, fine, stride=lines), :
+                ].astype(BF16)
     others = [(lat_partner(band, step, side), block) for step in STEPS]
     greet((chan_before, chan_after), others)
     inner = pl.ds(128, cols)
-    center = pltpu.make_async_copy(ocean_ref, tall.at[pl.ds(3, lines), :, :, inner], own.at[0])
-    center.start()
     finish_rows = start_edges(
-        ocean_ref.at[pl.ds(0, 3)],
-        ocean_ref.at[pl.ds(lines - 3, 3)],
+        tall.at[pl.ds(3, 3), :, :, inner],
+        tall.at[pl.ds(lines, 3), :, :, inner],
         edge.at[0],
         lat_before,
         lat_after,
         tall.at[pl.ds(lines + 3, 3), :, :, inner],
         tall.at[pl.ds(0, 3), :, :, inner],
     )
+    center = pltpu.make_async_copy(
+        tall.at[pl.ds(3, lines), :, :, inner], start_ref, own.at[pieces + 1]
+    )
+    center.start()
     copies = []
     for i in range(pieces):
         take(i).wait()
@@ -286,19 +281,20 @@
     store.wait()
 
 
-def open_exchange(probe, ocean, bands, blocks):
+def open_exchange(probe, ocean, mask, bands, blocks):
     rows, chans, lons = probe.shape
-    lines, probes, fine, cols = ocean.shape
+    probes, fine, lines, cols = ocean.shape
     pieces, lanes = 4, lons // 4
     any_spec = pl.BlockSpec(memory_space=pl.ANY)
     tall = (lines + 6, probes, fine, cols + 256)
     return pl.pallas_call(
         functools.partial(open_kernel, blocks),
-        in_specs=[any_spec, any_spec],
-        out_specs=[any_spec, any_spec],
+        in_specs=[any_spec, whole(ocean.shape), whole(mask.shape)],
+        out_specs=[any_spec, any_spec, any_spec],
         out_shape=[
             jax.ShapeDtypeStruct((bands, chans // bands, rows, lons), BF16),
             jax.ShapeDtypeStruct(tall, BF16),
+            jax.ShapeDtypeStruct((lines, probes, fine, cols), BF16),
         ],
         scratch_shapes=[
             pltpu.VMEM((pieces, rows, chans, lanes), BF16),
@@ -310,13 +306,13 @@
                 pltpu.SemaphoreType.DMA((pieces, bands - 1)),
                 pltpu.SemaphoreType.DMA((pieces,)),
             ],
-            pltpu.SemaphoreType.DMA((pieces + 1,)),
+            pltpu.SemaphoreType.DMA((pieces + 2,)),
             pltpu.SemaphoreType.DMA((2, 4)),
         ],
         compiler_params=params(collective_id=3, has_side_effects=True),
         cost_estimate=cost(0, 4 * probe.size),
         name="open_exchange",
-    )(probe, ocean)
+    )(probe, ocean, mask)
 
 
 def probe_flux_kernel(probe_ref, weight_ref, out_ref):
@@ -1032,7 +1028,6 @@
     tile_rows, tile_cols = ocean_mask.shape
     fine = ocean_probe.shape[1]
     mask = ocean_mask.astype(F32)
-    start = ocean_rows(ocean_probe, ocean_mask)
     base_rows = base_fine.transpose(1, 0, 2)
     slope_rows = slope_fine.transpose(1, 0, 2)
     base_lines = base_coarse.transpose(1, 0, 2)
@@ -1052,7 +1047,9 @@
     pool = jnp.where(meets, 0.25, 0.0).astype(BF16)
     spreadout = jnp.where(meets.T, 1.0, 0.0).astype(BF16)
 
-    gathered, around = open_exchange(flat_probe, start, bands, blocks)
+    gathered, around, start = open_exchange(
+        flat_probe, ocean_probe, ocean_mask, bands, blocks
+    )
 
     fwd_lat, inv_lat = cosine_tables(lats)
     diff = jnp.asarray(fourier_product(lons))

time: 273 us -> 272 us (level)
    pallas_call x1 -> x0, Pallas kernels: 3.06 us -> none  [ocean_rows(): pl.pallas_call(ocean_rows_kernel, grid=(probes,), in_specs=[pl.BlockSpec(...]
where the time goes in v6:
time: 272 us; the launch traced here: 269 us
  Pallas kernels  212 us (78%)
  local copies, waits for them, and re-layouts  26 us (10%)
  between operations  14.2 us (5%)
  starting transfers between devices  8.89 us (3%)
  other arithmetic  4.63 us (2%)
  waiting for transfers between devices  2.74 us (1%)
    pallas_call x1, Pallas kernels, open_exchange(): pl.pallas_call(functools.partial(open_kernel, blocks), in_specs=[any_spec...  76.4 us
    pallas_call x1, Pallas kernels, ocean_levels(): pl.pallas_call(functools.partial(ocean_kernel, bands, rows_sent), grid=(l...  60.3 us
    pallas_call x1, Pallas kernels, depthwise(): pl.pallas_call(depth_kernel, grid=(probes,), in_specs=[pl.BlockSpec((high...  26.9 us
    pallas_call x1, Pallas kernels, pointwise(): pl.pallas_call(functools.partial(point_kernel, sent), grid=(rows // GROUP...  21 us
    pallas_call x1, Pallas kernels, lat_filter(): pl.pallas_call(filter_kernel, grid=(chans,), in_specs=[pl.BlockSpec((band...  13.8 us
    unnamed x51, local copies, waits for them, and re-layouts  11.3 us
    all_to_all x1, starting transfers between devices, local(): lax.all_to_all(mixed.reshape(bands * blocks, part, pair, 128), ('lat', 'c...  8.67 us
    pallas_call x1, Pallas kernels, add_update(): pl.pallas_call(functools.partial(add_kernel, starts), grid=(rows // step,...  7.8 us
  transfers between devices with their start and end apart: 2, of which 1 were waited for; matrix products, arithmetic and copies ran while one was open for 10% of the time, Pallas kernels for 12%

profile of v6, /device:TPU:32, one launch (start us, length us, event | category | flops | bytes accessed | tf_op | source)
XLA Modules:
  0.0 268.6 jit_solution(7595972571699159639)
XLA Ops:
  7.2 0.9 copy-done
  8.9 76.4 %open_exchange.1 = (bf16[16,3,48,1024]{3,2,1,0:T(8,128)(2,1)}, bf16[14,2,200,512]{3,2,1,0:T(8,128)(2,1)}, bf16[8,2,200,256]{3,2,1,0:T(8,128)(2,1)}) custom-call(bf16[48,48,1024]{2,1,0:T(8,128)(2,1)} %bitcast.49, bf16[2,200,8,256]{3,2,1,0:T(8,128)(2,1)} %ocean_ref.1, s32[8,256]{1,0:T(8,128)} %mask_ref.1), custom_call_target="tpu_custom_call" | custom-call | bytes 9437184 | tf_op jit(solution)/shard_map/open_exchange/pallas_call | solution.py:290
  85.3 13.8 %lat_filter.1 = bf16[16,8,3,48,128]{4,3,2,1,0:T(8,128)(2,1)} custom-call(bf16[16,3,48,1024]{3,2,1,0:T(8,128)(2,1)} %get-tuple-element.43.in_ref, bf16[384,384]{1,0:T(8,128)(2,1)} %constant.50.clone.fwd_ref, bf16[384,384]{1,0:T(8,128)(2,1)} %constant.51.clone.inv_ref, f32[384,3]{1,0:T(8,128)} %copy.78.filt_ref, bf16[1024,1024]{1,0:T(8,128)(2,1)} %constant.49.clone.diff_ref), custom_call_target="tpu_custom_call" | custom-call | flops 8400000000 | bytes 9437184 | tf_op jit(solution)/shard_map/lat_filter/pallas_call | solution.py:386
  99.2 8.7 %all-to-all-start = ((bf16[128,3,48,128]{3,2,1,0:T(8,128)(2,1)}), bf16[128,3,48,128]{3,2,1,0:T(8,128)(2,1)}, u32[]{:S(2)}, u32[]{:S(2)}) async-start(bf16[128,3,48,128]{3,2,1,0:T(8,128)(2,1)} %bitcast.51), calls=%async_computation | async-start | bytes 9437184 | tf_op jit(solution)/shard_map/all_to_all | solution.py:1059
  108.8 5.6 %probe_flux.1 = bf16[8,192,128]{2,1,0:T(8,128)(2,1)} custom-call(bf16[2,24,48,1024]{3,2,1,0:T(8,128)(2,1)} %probe_ref.3, bf16[8,96]{1,0:T(8,128)(2,1)} %fusion.2.weight_ref), custom_call_target="tpu_custom_call" | custom-call | flops 37748736 | bytes 4718592 | tf_op jit(solution)/shard_map/probe_flux/pallas_call | solution.py:335
  114.4 1.1 copy.65
  118.2 1.0 broadcast_bitcast_fusion
  119.2 0.9 maximum_bitcast_fusion.wout_ref
  120.6 2.3 copy.71
  123.0 1.9 copy.70
  124.9 2.4 copy.83
  127.4 1.3 reshape.87
  129.6 1.1 copy.64
  130.6 1.1 copy.84
  131.7 1.1 copy.85
  132.8 1.0 copy.74
  133.8 1.0 copy.72
  137.0 26.9 %depthwise.1.spread_ref = f32[8,200,512]{2,1,0:T(8,128)} custom-call(bf16[14,2,200,512]{3,2,1,0:T(8,128)(2,1)} %get-tuple-element.45.in_ref, f32[392,256]{1,0:T(8,128)} %broadcast_bitcast_fusion.3.taps_ref), custom_call_target="tpu_custom_call" | custom-call | flops 163840000 | bytes 11468800 | tf_op jit(solution)/shard_map/depthwise/pallas_call | solution.py:640
  165.5 0.9 multiply_convert_fusion.mix_ref
  166.4 2.7 %reduce-scatter.2.cloned.1.call-done.pflux_ref = bf16[1,192,128]{2,1,0:T(8,128)(2,1)} async-done(((bf16[8,192,128]{2,1,0:T(8,128)(2,1)}), bf16[1,192,128]{2,1,0:T(8,128)(2,1)}) %reduce-scatter.2.cloned.1.call-update) | async-done | bytes 49168 | tf_op jit(solution)/shard_map/reduce_scatter | solution.py:1072
  171.5 21.0 %pointwise.1 = (bf16[8,2,24,48,128]{4,3,2,1,0:T(8,128)(2,1)}, f32[16,8,128]{2,1,0:T(8,128)}, bf16[8,2,4,48,128]{4,3,2,1,0:T(8,128)(2,1)}) custom-call(bf16[384,48,128]{2,1,0:T(8,128)(2,1)} %bitcast.2.mixed_ref, bf16[24,768,128]{2,1,0:T(8,128)(2,1)} %slope_ref.1, bf16[768,384]{1,0:T(8,128)(2,1)} %bitcast.58, bf16[392,768]{1,0:T(8,128)(2,1)} %maximum_bitcast_fusion.wout_ref, ...), custom_call_target="tpu_custom_call" | custom-call | flops 7299999744 | bytes 14155776 | tf_op jit(solution)/shard_map/pointwise/pallas_call | solution.py:518
  192.5 60.3 %ocean_levels.1 = (bf16[2,200,8,256]{3,2,1,0:T(8,128)(2,1)}, bf16[8,2,4,48,128]{4,3,2,1,0:T(8,128)(2,1)}, bf16[8,2,8,48,128]{4,3,2,1,0:T(8,128)(2,1)}, bf16[8,2,8,48,128]{4,3,2,1,0:T(8,128)(2,1)}) custom-call(f32[16,8,128]{2,1,0:T(8,128)} %get-tuple-element.53.picked_ref, s32[4,2048]{1,0:T(4,128)} %bitcast.65, f32[4,2048]{1,0:T(4,128)} %bitcast.66, ...), custom_call_target="tpu_custom_call" | custom-call | flops 5000000000 | bytes 20000000 | tf_op jit(solution)/shard_map/ocean_levels/pallas_call | solution.py:940
  252.8 7.8 %add_update.1 = bf16[2,24,48,1024]{3,2,1,0:T(8,128)(2,1)} custom-call(bf16[2,24,48,1024]{3,2,1,0:T(8,128)(2,1)} %probe_ref.3, bf16[8,2,4,48,128]{4,3,2,1,0:T(8,128)(2,1)} %get-tuple-element.52.refs_0_, bf16[8,2,4,48,128]{4,3,2,1,0:T(8,128)(2,1)} %get-tuple-element.78.refs_1_, bf16[8,2,8,48,128]{4,3,2,1,0:T(8,128)(2,1)} %get-tuple-element.79.refs_2_, ...), custom_call_target="tpu_custom_call" | custom-call | flops 2359296 | bytes 14155776 | tf_op jit(solution)/shard_map/add_update/pallas_call | solution.py:581
  260.6 1.2 copy.88
  (68 shorter events, 12.1 us)
Async XLA Ops:
  7.2 0.9 copy-start
  99.2 8.9 %copy-start.17 = (bf16[384,4]{0,1:T(4,128)(2,1)S(1)}, bf16[384,4]{0,1:T(4,128)(2,1)}, u32[]{:S(2)}) copy-start(bf16[384,4]{0,1:T(4,128)(2,1)} %param.36) | copy-start | bytes 9220
  99.2 70.0 %all-to-all-start = ((bf16[128,3,48,128]{3,2,1,0:T(8,128)(2,1)}), bf16[128,3,48,128]{3,2,1,0:T(8,128)(2,1)}, u32[]{:S(2)}, u32[]{:S(2)}) async-start(bf16[128,3,48,128]{3,2,1,0:T(8,128)(2,1)} %bitcast.51), calls=%async_computation | async-start | bytes 9437184 | tf_op jit(solution)/shard_map/all_to_all | solution.py:1059
  107.8 61.3 %reduce-scatter.2.cloned.1.call-start = ((), (), s32[]{:S(2)}) async-start(), calls=%async_computation.2 | async-start | bytes 442368 | tf_op jit(solution)/shard_map/reduce_scatter | solution.py:1072
  108.8 5.6 %copy-start.4 = (bf16[768,384]{1,0:T(8,128)(2,1)S(1)}, bf16[768,384]{1,0:T(8,128)(2,1)}, u32[]{:S(2)}) copy-start(bf16[768,384]{1,0:T(8,128)(2,1)} %param.35) | copy-start | bytes 1769476
  108.8 6.7 %copy-start.14 = (f32[200,49]{0,1:T(8,128)S(1)}, f32[200,49]{0,1:T(8,128)}, u32[]{:S(2)}) copy-start(f32[200,49]{0,1:T(8,128)} %param.47) | copy-start | bytes 117604
  108.8 6.7 %copy-start.18 = (bf16[4,200]{1,0:T(4,128)(2,1)S(1)}, bf16[4,200]{1,0:T(4,128)(2,1)}, u32[]{:S(2)}) copy-start(bf16[4,200]{1,0:T(4,128)(2,1)} %param.42) | copy-start | bytes 4804
  115.5 3.6 %copy-start.5 = (bf16[768,384]{0,1:T(8,128)(2,1)S(1)}, bf16[768,384]{0,1:T(8,128)(2,1)}, u32[]{:S(2)}) copy-start(bf16[768,384]{0,1:T(8,128)(2,1)} %copy.65) | copy-start | bytes 1769476
  115.5 4.5 %copy-start.16 = (s32[8,256]{1,0:T(8,128)S(1)}, s32[8,256]{1,0:T(8,128)}, u32[]{:S(2)}) copy-start(s32[8,256]{1,0:T(8,128)} %mask_ref.1) | copy-start | bytes 24580
  118.2 6.7 %copy-start.2 = (bf16[800,8,256]{2,1,0:T(8,128)(2,1)S(1)}, bf16[800,8,256]{2,1,0:T(8,128)(2,1)}, u32[]{:S(2)}) copy-start(bf16[800,8,256]{2,1,0:T(8,128)(2,1)} %param.45) | copy-start | bytes 9830404
  128.6 2.0 copy-start.8
  129.0 2.7 %copy-start.9 = (bf16[200,8,256]{2,1,0:T(8,128)(2,1)S(1)}, bf16[200,8,256]{2,1,0:T(8,128)(2,1)}, u32[]{:S(2)}) copy-start(bf16[200,8,256]{2,1,0:T(8,128)(2,1)} %param.43) | copy-start | bytes 2457604
  130.6 2.2 copy-start.10
  130.6 3.2 %copy-start.15 = (f32[250,49]{0,1:T(8,128)S(1)}, f32[250,49]{0,1:T(8,128)}, u32[]{:S(2)}) copy-start(f32[250,49]{0,1:T(8,128)} %param.55) | copy-start | bytes 147004
  130.6 3.2 %copy-start.12 = (bf16[200,800]{1,0:T(8,128)(2,1)S(1)}, bf16[200,800]{1,0:T(8,128)(2,1)}, u32[]{:S(2)}) copy-start(bf16[200,800]{1,0:T(8,128)(2,1)} %param.48) | copy-start | bytes 960004
  131.7 3.1 %copy-start.13 = (bf16[250,4,128]{2,1,0:T(4,128)(2,1)S(1)}, bf16[250,4,128]{2,1,0:T(4,128)(2,1)}, u32[]{:S(2)}) copy-start(bf16[250,4,128]{2,1,0:T(4,128)(2,1)} %param.51) | copy-start | bytes 768004
  131.7 3.8 %copy-start.11 = (bf16[200,250]{1,0:T(8,128)(2,1)S(1)}, bf16[200,250]{1,0:T(8,128)(2,1)}, u32[]{:S(2)}) copy-start(bf16[200,250]{1,0:T(8,128)(2,1)} %param.50) | copy-start | bytes 300004
  137.0 28.5 %copy-start.3 = (f32[2,200,392]{2,1,0:T(8,128)S(1)}, f32[2,200,392]{2,1,0:T(8,128)}, u32[]{:S(2)}) copy-start(f32[2,200,392]{2,1,0:T(8,128)} %copy.71) | copy-start | bytes 1881604
  137.0 28.5 %copy-start.7 = (f32[200,392]{1,0:T(8,128)S(1)}, f32[200,392]{1,0:T(8,128)}, u32[]{:S(2)}) copy-start(f32[200,392]{1,0:T(8,128)} %copy.70) | copy-start | bytes 940804
  163.9 5.3 %copy-start.19 = (f32[250]{0:T(256)S(1)}, f32[250]{0:T(256)}, u32[]{:S(2)}) copy-start(f32[250]{0:T(256)} %param.54) | copy-start | bytes 3004
  163.9 6.1 %copy-start.20 = (f32[200]{0:T(256)S(1)}, f32[200]{0:T(256)}, u32[]{:S(2)}) copy-start(f32[200]{0:T(256)} %param.46) | copy-start | bytes 2404
  252.8 7.8 %copy-start.6 = (bf16[2,200,8,256]{3,2,1,0:T(8,128)(2,1)S(1)}, bf16[2,200,8,256]{3,2,1,0:T(8,128)(2,1)}, u32[]{:S(2)}) copy-start(bf16[2,200,8,256]{3,2,1,0:T(8,128)(2,1)} %get-tuple-element.89) | copy-start | bytes 4915204
  252.8 9.0 %copy-start.1 = (f32[384,48]{0,1:T(8,128)S(1)}, f32[384,48]{0,1:T(8,128)}, u32[]{:S(2)}) copy-start(f32[384,48]{0,1:T(8,128)} %param.33) | copy-start | bytes 221188
Sparse Core Ops, SparseCore 0:
  114.5 54.5 reduce-scatter.1
